TPU v7x, 256 devices: a whole 4x4x8 slice. The times are simulated.
256 devices in a mesh: dp: 16 (over y_lo, x, core), seq: 8 (over z), enc: 2 (over y_hi).
Axes of the slice: x: 4, y: 4 (y_hi: 2, y_lo: 2; y = y_hi * 2 + y_lo), z: 8, core: 2. Of those that a mesh axis runs over, the one named last changes fastest.
Arguments:
- image_qkv: bfloat16 [32, 1024, 4608], P(('dp', 'enc'), 'seq'), may hold values from -7 to 7
- residual: bfloat16 [32, 1024, 2432], P(('dp', 'enc'), 'seq'), may hold values from -1.5 to 1.5
- gate: float32 [32, 2432], P(('dp', 'enc')), may hold values from 0.5 to 2
- cotangent: bfloat16 [32, 1024, 2432], P(('dp', 'enc'), 'seq'), may hold values from -6 to 6
- t5_states: bfloat16 [32, 256, 4096], P('dp', 'seq', 'enc'), may hold values from -6 to 6
- text_weight: bfloat16 [2, 4096, 1536], P(None, 'enc', 'seq'), may hold values from -0.09375 to 0.09375
- out_weight: bfloat16 [1536, 2432], P(('dp', 'seq', 'enc')), may hold values from -0.15625 to 0.15625
- caption_len: int32 [32], P(('dp', 'enc')), may hold values from 1 to 256, as said below
Outputs:
- block_out: bfloat16 [32, 1024, 2432], P(('dp', 'enc'), 'seq')
- d_gate: float32 [32, 2432], P(('dp', 'enc'))
- d_out_weight: float32 [1536, 2432], P(('dp', 'seq', 'enc'))
Inputs may be any that keep to these rules, and one draw needn't show every extreme that they name: `caption_len`: some image has all 256 caption slots valid.
All inputs are finite; a program needn't handle non-finite values.
Results may differ from a plain program's by a relative error of at most 0.024.
Values may be sent and summed in bfloat16 or wider, within the bound.
No kernel may reach another device: no remote copies, remote signals or barrier semaphores. Data moves between devices by JAX's collectives and lax.ppermute only.
A program may use at most 128 MiB of HBM per device.

v0:
```python
import jax
import jax.numpy as jnp
from jax import lax
from jax.sharding import PartitionSpec as P

HEAD = 64


def attend(query, key_img, value_img, key_txt, value_txt, length):
    rows = query.shape[0]
    block = min(512, rows)
    scale = query.shape[2] ** (-0.5)
    valid = jnp.arange(key_txt.shape[0], dtype=jnp.int32) < length

    def one_block(qblock):
        s_img = (
            jnp.einsum("qhe,khe->hqk", qblock, key_img, preferred_element_type=jnp.float32) * scale
        )
        s_txt = (
            jnp.einsum("qhe,khe->hqk", qblock, key_txt, preferred_element_type=jnp.float32) * scale
        )
        s_txt = jnp.where(valid[None, None, :], s_txt, -jnp.inf)
        top = jnp.maximum(
            jnp.max(s_img, axis=-1, keepdims=True), jnp.max(s_txt, axis=-1, keepdims=True)
        )
        p_img = jnp.exp(s_img - top)
        p_txt = jnp.exp(s_txt - top)
        total = jnp.sum(p_img, axis=-1, keepdims=True) + jnp.sum(p_txt, axis=-1, keepdims=True)
        w_img = (p_img / total).astype(jnp.bfloat16)
        w_txt = (p_txt / total).astype(jnp.bfloat16)
        out = jnp.einsum("hqk,khe->qhe", w_img, value_img, preferred_element_type=jnp.float32)
        out = out + jnp.einsum("hqk,khe->qhe", w_txt, value_txt, preferred_element_type=jnp.float32)
        return out.astype(jnp.bfloat16)

    blocks = query.reshape(rows // block, block, query.shape[1], query.shape[2])
    result = lax.map(one_block, blocks)
    return result.reshape(rows, query.shape[1], query.shape[2])


def per_device(
    image_qkv, residual, gate, cotangent, t5_states, text_weight, out_weight, caption_len
):
    seq_count = lax.axis_size("seq")
    img_count, tok_count, columns = image_qkv.shape
    group = columns // seq_count
    local_heads = group // (3 * HEAD)
    partial_kv = jnp.einsum(
        "ntf,cfa->ntca",
        lax.all_gather(t5_states, "seq", axis=1, tiled=True),
        text_weight,
        preferred_element_type=jnp.float32,
    )
    text_kv = lax.psum_scatter(
        partial_kv.astype(jnp.bfloat16), "enc", scatter_dimension=0, tiled=True
    )
    txt_len = text_kv.shape[1]
    text_kv = text_kv.reshape(img_count, txt_len, 2, local_heads, HEAD)
    spread = lax.all_to_all(
        image_qkv.reshape(img_count, tok_count, seq_count, group),
        "seq",
        split_axis=2,
        concat_axis=1,
        tiled=True,
    )
    full_len = spread.shape[1]
    spread = spread.reshape(img_count, full_len, local_heads, 3, HEAD)

    def per_image(piece, tkv, length):
        return attend(piece[:, :, 0], piece[:, :, 1], piece[:, :, 2], tkv[:, 0], tkv[:, 1], length)

    attn_heads = jax.vmap(per_image)(spread, text_kv, caption_len)
    head_cols = attn_heads.reshape(img_count * full_len, local_heads * HEAD)
    attn_heads = attn_heads.reshape(img_count, full_len, 1, local_heads * HEAD)
    gathered = lax.all_to_all(attn_heads, "seq", split_axis=1, concat_axis=2, tiled=True)
    attn_flat = gathered.reshape(img_count * tok_count, columns // 3)
    width = out_weight.shape[1]
    proj = jnp.dot(
        attn_flat,
        lax.all_gather(out_weight, ("dp", "seq", "enc"), axis=0, tiled=True),
        preferred_element_type=jnp.float32,
    )
    proj = proj.reshape(img_count, tok_count, width)
    block_out = (residual.astype(jnp.float32) + gate[:, None, :] * proj).astype(jnp.bfloat16)
    cot_float = cotangent.astype(jnp.float32)
    d_gate = lax.psum(jnp.sum(cot_float * proj, axis=1), "seq")
    scaled = (
        (gate[:, None, :] * cot_float).astype(jnp.bfloat16).reshape(img_count * tok_count, width)
    )
    own_rows = out_weight.shape[0]
    scaled_full = lax.all_gather(
        scaled.reshape(img_count, tok_count, width), "seq", axis=1, tiled=True
    )
    scaled_full = scaled_full.reshape(img_count * full_len, width)
    head_grad = lax.dot_general(
        head_cols, scaled_full, (((0,), (0,)), ((), ())), preferred_element_type=jnp.float32
    )
    dp_count = lax.axis_size("dp")
    enc_count = lax.axis_size("enc")
    head_grad = head_grad.reshape(dp_count // seq_count, seq_count, enc_count, own_rows, width)
    pairs = lax.psum_scatter(
        head_grad.astype(jnp.bfloat16), "enc", scatter_dimension=2, tiled=True
    ).astype(jnp.float32)
    moved = lax.all_to_all(
        pairs.astype(jnp.bfloat16), "seq", split_axis=1, concat_axis=0, tiled=True
    ).astype(pairs.dtype)
    moved = moved.reshape(dp_count * own_rows, width)
    d_out_weight = lax.psum_scatter(
        moved.astype(jnp.bfloat16), "dp", scatter_dimension=0, tiled=True
    ).astype(jnp.float32)
    return (block_out, d_gate, d_out_weight)


def solution(mesh):
    in_specs = (
        P(("dp", "enc"), "seq", None),
        P(("dp", "enc"), "seq", None),
        P(("dp", "enc"), None),
        P(("dp", "enc"), "seq", None),
        P("dp", "seq", "enc"),
        P(None, "enc", "seq"),
        P(("dp", "seq", "enc"), None),
        P(("dp", "enc")),
    )
    out_specs = (
        P(("dp", "enc"), "seq", None),
        P(("dp", "enc"), None),
        P(("dp", "seq", "enc"), None),
    )
    return jax.shard_map(
        per_device, mesh=mesh, in_specs=in_specs, out_specs=out_specs, check_vma=False
    )
```

profile of v0, /device:TPU:4, one launch (start us, length us, event | category | flops | bytes accessed | tf_op | source)
XLA Modules:
  0.0 1068.1 jit_solution(15236251242690601095)
XLA Ops:
  8.0 0.0 all-gather.5.cloned.1.call-start
  8.1 0.7 all-gather.5.cloned.1.call-update
  8.8 0.0 reduce-scatter.5.cloned.1.call-start
  8.8 45.9 %all-gather.5.cloned.1.call-done = bf16[2,256,2048]{2,1,0:T(8,128)(2,1)} async-done(((bf16[2,32,2048]{2,1,0:T(8,128)(2,1)}), bf16[2,256,2048]{2,1,0:T(8,128)(2,1)}) %all-gather.5.cloned.1.call-update) | async-done | bytes 2097168 | tf_op jit(solution)/shard_map/all_gather | solution.py:49
  54.7 3.3 fusion.28
  58.1 0.0 all-gather.9.cloned.1.call-start
  58.1 0.5 all-gather.9.cloned.1.call-update
  58.7 1.4 copy.34
  60.1 4.3 all-to-all-start
  64.4 27.9 %all-to-all-done = bf16[1,128,8,576]{1,3,0,2:T(8,128)(2,1)S(1)} async-done(((bf16[1,128,8,576]{1,3,0,2:T(8,128)(2,1)}), bf16[1,128,8,576]{1,3,0,2:T(8,128)(2,1)S(1)}, u32[]{:S(2)}, u32[]{:S(2)}) %all-to-all-start) | async-done | bytes 1179680 | tf_op jit(solution)/shard_map/all_to_all | solution.py:58
  92.3 1.8 copy.36
  94.1 2.3 reshape.124
  96.4 0.9 slice_bitcast_fusion
  97.2 0.3 squeeze.17
  97.6 1.0 slice_bitcast_fusion.2
  98.5 14.1 %while.11 = (s32[]{:T(128)}, bf16[2,1,512,3,64]{2,4,3,1,0:T(8,128)(2,1)}, bf16[2,1,512,3,64]{2,4,3,1,0:T(8,128)(2,1)S(1)}, bf16[1,1024,3,64]{1,3,2,0:T(8,128)(2,...) while((s32[]{:T(128)}, ...), condition=%wide.region_6.7_spmd.clone, body=%wide.region_1.6_spmd.clone.sunk | while | flops 520811776 | bytes 29201324 | solution.py:36
  98.6 0.7 compare_reduce_fusion.2
  99.2 0.4 fusion.49
  99.7 1.1 multiply_reduce_fusion.2
  100.8 0.2 fusion.51
  101.0 1.3 fusion.50
  102.4 2.1 fusion.52
  104.5 0.4 fusion.53
  104.9 0.7 copy-done.5
  105.6 0.7 compare_reduce_fusion.2
  106.3 0.4 fusion.49
  106.7 1.1 multiply_reduce_fusion.2
  107.8 0.2 fusion.51
  108.1 1.3 fusion.50
  109.4 2.1 fusion.52
  111.5 0.4 fusion.53
  111.9 0.7 copy-done.5
  112.7 1.4 copy.38
  114.1 0.3 transpose.32
  114.3 0.8 copy.39
  115.2 0.5 broadcast.39
  115.7 4.0 reduce.12
  119.8 1.3 reshape.145
  121.1 3.5 all-to-all-start.1
  124.6 0.2 all-gather.7.cloned.1.call-start
  124.8 11.5 %all-to-all-done.1 = bf16[8,2,12288]{2,1,0:T(2,128)(2,1)S(1)} async-done(((bf16[8,2,12288]{2,1,0:T(2,128)(2,1)}), bf16[8,2,12288]{2,1,0:T(2,128)(2,1)S(1)}, u32[]{:S(2)}, u32[]{:S(2)}) %all-to-all-start.1) | async-done | bytes 393248 | tf_op jit(solution)/shard_map/all_to_all | solution.py:74
  136.4 0.7 reshape.146
  137.1 0.6 copy.40
  137.7 0.1 copy.51
  137.8 0.1 copy.41
  137.9 644.8 %all-gather.9.cloned.1.call-done = bf16[256,6,2432]{2,1,0:T(8,128)(2,1)} async-done(((bf16[1,6,2432]{2,1,0:T(8,128)(2,1)}), bf16[256,6,2432]{2,1,0:T(8,128)(2,1)}) %all-gather.9.cloned.1.call-update) | async-done | bytes 7471120 | tf_op jit(solution)/shard_map/all_gather | solution.py:79
  782.7 12.9 %reshape.130 = bf16[1536,2432]{1,0:T(8,128)(2,1)} reshape(bf16[256,6,2432]{2,1,0:T(8,128)(2,1)} %all-gather.9.cloned.1.call-done) | data formatting | bytes 14942208
  795.7 5.6 fusion.33
  801.3 0.0 all-reduce.5.cloned.1.call-start
  801.5 0.1 dot_general.28
  801.6 67.8 %all-gather.7.cloned.1.call-done = bf16[1,1024,2432]{2,1,0:T(8,128)(2,1)} async-done(((bf16[1,128,2432]{2,1,0:T(8,128)(2,1)}), bf16[1,1024,2432]{2,1,0:T(8,128)(2,1)}) %all-gather.7.cloned.1.call-update) | async-done | bytes 4980752 | tf_op jit(solution)/shard_map/all_gather | solution.py:90
  869.4 4.6 fusion.22
  874.1 0.0 all-reduce.7.cloned.1.call-start
  874.1 0.6 dynamic-slice
  874.7 48.9 %all-reduce.5.cloned.1.call-done = bf16[2,8,2,6,2432]{4,1,3,2,0:T(8,128)(2,1)} async-done(((bf16[2,8,2,6,2432]{4,1,3,2,0:T(8,128)(2,1)}), bf16[2,8,2,6,2432]{4,1,3,2,0:T(8,128)(2,1)}) %all-reduce.5.cloned.1.call-update) | async-done | bytes 933904
  923.6 1.7 constant_dynamic-slice_fusion
  925.3 0.4 copy.44
  925.7 23.1 %all_to_all.48 = bf16[2,8,1,6,2432]{4,0,3,2,1:T(2,128)(2,1)S(1)} all-to-all(bf16[2,8,1,6,2432]{4,0,3,2,1:T(2,128)(2,1)S(1)} %copy.44), channel_id=1, replica_groups=mesh['dp'=16,'seq'=8,'enc'=2] {'seq'}, dimensions={1} | all-to-all | bytes 933888 | tf_op jit(solution)/shard_map/all_to_all | solution.py:103
  948.8 0.1 copy.45
  948.8 0.9 all_to_all.44
  949.8 0.6 dynamic-slice.2
  951.1 15.8 %psum.7 = f32[1,2432]{1,0:T(1,128)} all-reduce(f32[1,2432]{1,0:T(1,128)S(1)} %reduce_sum.30), channel_id=1, replica_groups=mesh['dp'=16,'seq'=8,'enc'=2] {'seq'}, use_global_device_ids=true, to_apply=%region_8.9 | all-reduce | flops 2432 | bytes 19456 | tf_op jit(solution)/shard_map/psum | solution.py:85
  966.9 92.6 %all-reduce.7.cloned.1.call-done = bf16[96,2432]{1,0:T(8,128)(2,1)} async-done(((bf16[96,2432]{1,0:T(8,128)(2,1)}), bf16[96,2432]{1,0:T(8,128)(2,1)}) %all-reduce.7.cloned.1.call-update) | async-done | bytes 466960
  1059.5 1.5 dynamic-slice_convert_fusion
  (34 shorter events, 0.3 us)
Async XLA Ops:
  8.0 46.7 %copy-start = (bf16[2,2048,192]{1,2,0:T(8,128)(2,1)S(1)}, bf16[2,2048,192]{1,2,0:T(8,128)(2,1)}, u32[]{:S(2)}) copy-start(bf16[2,2048,192]{1,2,0:T(8,128)(2,1)} %param.15) | copy-start | bytes 4718596
  8.0 46.7 %all-gather.5.cloned.1.call-start = ((), (), s32[]{:S(2)}) async-start(), calls=%async_computation.4 | async-start | bytes 2359296 | tf_op jit(solution)/shard_map/all_gather | solution.py:49
  8.7 49.9 %copy-start.1 = (bf16[1,128,4608]{2,1,0:T(8,128)(2,1)S(1)}, bf16[1,128,4608]{2,1,0:T(8,128)(2,1)}, u32[]{:S(2)}) copy-start(bf16[1,128,4608]{2,1,0:T(8,128)(2,1)} %param.10) | copy-start | bytes 3538948
  8.8 88.8 %reduce-scatter.5.cloned.1.call-start = ((), (), s32[]{:S(2)}) async-start(), calls=%async_computation.5 | async-start | bytes 589824 | tf_op jit(solution)/shard_map/reduce_scatter | solution.py:53
  58.1 724.6 %all-gather.9.cloned.1.call-start = ((), (), s32[]{:S(2)}) async-start(), calls=%async_computation.7 | async-start | bytes 10000384 | tf_op jit(solution)/shard_map/all_gather | solution.py:79
  60.1 32.2 %all-to-all-start = ((bf16[1,128,8,576]{1,3,0,2:T(8,128)(2,1)}), bf16[1,128,8,576]{1,3,0,2:T(8,128)(2,1)S(1)}, u32[]{:S(2)}, u32[]{:S(2)}) async-start(bf16[1,128,8,576]{1,3,0,2:T(8,128)(2,1)} %bitcast.140), calls=%async_computation | async-start | bytes 2359296 | tf_op jit(solution)/shard_map/all_to_all | solution.py:58
  97.2 1.3 copy-start.3
  102.3 2.1 copy-start.4
  104.9 0.8 copy-start.5
  109.4 2.1 copy-start.4
  111.9 0.8 copy-start.5
  115.7 9.1 copy-start.6
  121.1 15.3 %all-to-all-start.1 = ((bf16[8,2,12288]{2,1,0:T(2,128)(2,1)}), bf16[8,2,12288]{2,1,0:T(2,128)(2,1)S(1)}, u32[]{:S(2)}, u32[]{:S(2)}) async-start(bf16[8,2,12288]{2,1,0:T(2,128)(2,1)} %reshape.145), calls=%async_computation.2 | async-start | bytes 786432 | tf_op jit(solution)/shard_map/all_to_all | solution.py:74
  124.6 744.9 %all-gather.7.cloned.1.call-start = ((), (), s32[]{:S(2)}) async-start(), calls=%async_computation.6 | async-start | bytes 5603328 | tf_op jit(solution)/shard_map/all_gather | solution.py:90
  137.9 657.8 %copy-start.2 = (bf16[1,128,2432]{2,1,0:T(8,128)(2,1)S(1)}, bf16[1,128,2432]{2,1,0:T(8,128)(2,1)}, u32[]{:S(2)}) copy-start(bf16[1,128,2432]{2,1,0:T(8,128)(2,1)} %param.13) | copy-start | bytes 1867780
  801.3 122.3 %all-reduce.5.cloned.1.call-start = ((), (), s32[]{:S(2)}) async-start(), calls=%async_computation.8 | async-start | bytes 1867776
  801.6 72.5 %copy-start.8 = (u32[256]{0:T(256)S(1)}, u32[256]{0:T(256)}, u32[]{:S(2)}) copy-start(u32[256]{0:T(256)} %constant.31) | copy-start | bytes 3076
  874.1 185.4 %all-reduce.7.cloned.1.call-start = ((), (), s32[]{:S(2)}) async-start(), calls=%async_computation.9 | async-start | bytes 933888
  925.7 24.1 %copy-start.7 = (u32[256]{0:T(256)S(1)}, u32[256]{0:T(256)}, u32[]{:S(2)}) copy-start(u32[256]{0:T(256)} %constant.35) | copy-start | bytes 3076
Sparse Core Ops, SparseCore 0:
  10.6 44.0 all-gather.4
  58.2 18.2 reduce-scatter.4
  801.5 67.9 all-gather.6
  874.2 49.3 all-reduce.4
  949.9 109.4 all-reduce.6
Sparse Core Ops, SparseCore 1:
  60.6 722.1 all-gather.8
where the time goes:
time: 1080 us; the launch traced here: 1070 us
  waiting for transfers between devices  941 us (87%)
  blocking collectives  38.9 us (4%)
  local copies, waits for them, and re-layouts  32.4 us (3%)
  matrix products  21.7 us (2%)
  between operations  16.1 us (1%)
    all_gather x1, waiting for transfers between devices, per_device(): lax.all_gather(out_weight, ('dp', 'seq', 'enc'), axis=0, tiled=True)  645 us
    unnamed x8, waiting for transfers between devices  143 us
    all_gather x1, waiting for transfers between devices, per_device(): lax.all_gather(scaled.reshape(img_count, tok_count, width), 'seq', axis=1...  67.8 us
    all_gather x1, waiting for transfers between devices, per_device(): lax.all_gather(t5_states, 'seq', axis=1, tiled=True)  45.9 us
    all_to_all x1, waiting for transfers between devices, per_device(): lax.all_to_all(image_qkv.reshape(img_count, tok_count, seq_count, group),...  27.9 us
    all_to_all x1, blocking collectives, per_device(): lax.all_to_all(pairs.astype(jnp.bfloat16), 'seq', split_axis=1, concat_ax...  23.1 us
  transfers between devices with their start and end apart: 8, of which 7 were waited for; matrix products, arithmetic and copies ran while one was open for 3% of the time, Pallas kernels for 0%

commit v1 on v0

v1 whole, which is shorter than its diff:
```python
import jax
import jax.numpy as jnp
from jax import lax
from jax.sharding import PartitionSpec as P

HEAD = 64
PLANE = ("dp", "enc")
WHOLE = ("dp", "seq", "enc")
DOWN = 4


def attend(query, key, value, bias):
    scale = query.shape[2] ** (-0.5)
    s = jnp.einsum("qhe,khe->hqk", query, key, preferred_element_type=jnp.float32) * scale
    s = s + bias[None, None, :]
    p = jnp.exp(s - jnp.max(s, axis=-1, keepdims=True))
    w = (p / jnp.sum(p, axis=-1, keepdims=True)).astype(jnp.bfloat16)
    out = jnp.einsum("hqk,khe->qhe", w, value, preferred_element_type=jnp.float32)
    return out.astype(jnp.bfloat16)


def per_device(
    image_qkv, residual, gate, cotangent, t5_states, text_weight, out_weight, caption_len
):
    n_dp, n_seq, n_enc = lax.axis_size("dp"), lax.axis_size("seq"), lax.axis_size("enc")
    _, tok, columns = image_qkv.shape
    group = columns // n_seq
    heads = group // (3 * HEAD)
    own_rows, width = out_weight.shape
    enc = lax.axis_index("enc")

    flat = own_rows * width
    lanes = t5_states.shape[2]
    wide = flat // own_rows // lanes * lanes
    narrow = width - wide
    own_txt = t5_states.shape[0] * t5_states.shape[1]

    rest = -(-own_rows * narrow // lanes)
    tail = jnp.pad(out_weight[:, wide:].reshape(-1), (0, rest * lanes - own_rows * narrow))
    packed = jnp.concatenate(
        [t5_states.reshape(own_txt, lanes), out_weight[:, :wide], tail.reshape(rest, lanes)], axis=0
    )
    packed_full = lax.all_gather(packed, "seq", axis=0)
    spread = lax.all_to_all(
        image_qkv.reshape(tok, n_seq, group), "seq", split_axis=1, concat_axis=0, tiled=True
    )
    full = tok * n_seq
    spread = spread.reshape(full, heads, 3, HEAD)

    cot_float = cotangent[0].astype(jnp.float32)
    scaled = (gate * cot_float).astype(jnp.bfloat16)
    blocks = {0: scaled}

    def ring_step(j):
        if j <= DOWN:
            blocks[j] = lax.ppermute(
                blocks[j - 1], "seq", [(i, (i - 1) % n_seq) for i in range(n_seq)]
            )
        if j < n_seq - DOWN:
            blocks[-j] = lax.ppermute(
                blocks[1 - j], "seq", [(i, (i + 1) % n_seq) for i in range(n_seq)]
            )

    def done_with(j, *values):
        mine = [k for k in blocks if abs(k) == j]
        held = lax.optimization_barrier((tuple(blocks[k] for k in mine), values))
        blocks.update(zip(mine, held[0]))
        return held[1]

    ring_step(1)
    packed_full, spread = done_with(1, packed_full, spread)
    ring_step(2)

    t5_full = packed_full[:, :own_txt].reshape(n_seq * own_txt, lanes)
    w_main = packed_full[:, own_txt : own_txt + own_rows]
    w_rest = packed_full[:, own_txt + own_rows :].reshape(n_seq, rest * lanes)
    w_rest = w_rest[:, : own_rows * narrow].reshape(n_seq, own_rows, narrow)
    w_seq = jnp.concatenate([w_main, w_rest], axis=2)
    swap = [(0, 1), (1, 0)]
    w_got = lax.ppermute(w_seq, "enc", swap)
    w_pair = jnp.stack(
        [jnp.where(enc == 0, w_seq, w_got), jnp.where(enc == 0, w_got, w_seq)], axis=1
    )
    w_full = lax.all_gather(
        w_pair.reshape(n_seq * n_enc * own_rows, width), "dp", axis=0, tiled=True
    )
    partial = lax.dot_general(
        t5_full, text_weight, (((1,), (1,)), ((), ())), preferred_element_type=jnp.float32
    )
    partial = partial.reshape(n_seq, 2, -1, 2, heads * HEAD)
    mine = jnp.where(enc == 0, partial[:, 0], partial[:, 1])
    other = jnp.where(enc == 0, partial[:, 1], partial[:, 0]).astype(jnp.bfloat16)
    got = lax.ppermute(other, "enc", swap)
    got, spread = done_with(2, got, spread)
    ring_step(3)
    text_kv = (mine + got.astype(jnp.float32)).astype(jnp.bfloat16)
    txt = text_kv.shape[0] * text_kv.shape[1]
    text_kv = text_kv.reshape(txt, 2, heads, HEAD)

    bias = jnp.concatenate(
        [
            jnp.zeros((full,), jnp.float32),
            jnp.where(jnp.arange(txt, dtype=jnp.int32) < caption_len[0], 0.0, -jnp.inf),
        ]
    )
    key = jnp.concatenate([spread[:, :, 1], text_kv[:, 0]], axis=0)
    value = jnp.concatenate([spread[:, :, 2], text_kv[:, 1]], axis=0)
    attn = attend(spread[:, :, 0], key, value, bias).reshape(full, heads * HEAD)
    (attn,) = done_with(3, attn)
    ring_step(4)
    attn_tok = lax.all_to_all(
        attn.reshape(n_seq, tok, heads * HEAD), "seq", split_axis=0, concat_axis=0
    )
    (attn_tok,) = done_with(4, attn_tok)
    attn_tok = jnp.swapaxes(attn_tok, 0, 1).reshape(tok, n_seq * heads * HEAD)
    proj = jnp.dot(attn_tok, w_full, preferred_element_type=jnp.float32)
    block_out = (residual[0].astype(jnp.float32) + gate * proj).astype(jnp.bfloat16)
    d_gate = jnp.sum(cot_float * proj, axis=0, keepdims=True)
    for bit in (1, 2, 4):
        d_gate = d_gate + lax.ppermute(d_gate, "seq", [(i, i ^ bit) for i in range(n_seq)])

    me = lax.axis_index("seq")
    grad = 0.0
    for j, block in blocks.items():
        rows = lax.dynamic_slice_in_dim(attn, (me + j) % n_seq * tok, tok, axis=0)
        grad = grad + lax.dot_general(
            rows, block, (((0,), (0,)), ((), ())), preferred_element_type=jnp.float32
        )
    grad = grad.astype(jnp.bfloat16)
    pieces = lax.all_to_all(grad.reshape(n_dp * n_enc, own_rows, width), PLANE, 0, 0)
    block = jnp.sum(pieces.astype(jnp.float32), axis=0).astype(jnp.bfloat16)
    perm = [
        ((d * n_seq + s) * n_enc + e, s * n_dp * n_enc + d * n_enc + e)
        for d in range(n_dp)
        for s in range(n_seq)
        for e in range(n_enc)
    ]
    d_out_weight = lax.ppermute(block, WHOLE, perm).astype(jnp.float32)
    return (block_out[None], d_gate, d_out_weight)


def solution(mesh):
    in_specs = (
        P(("dp", "enc"), "seq", None),
        P(("dp", "enc"), "seq", None),
        P(("dp", "enc"), None),
        P(("dp", "enc"), "seq", None),
        P("dp", "seq", "enc"),
        P(None, "enc", "seq"),
        P(("dp", "seq", "enc"), None),
        P(("dp", "enc")),
    )
    out_specs = (
        P(("dp", "enc"), "seq", None),
        P(("dp", "enc"), None),
        P(("dp", "seq", "enc"), None),
    )
    return jax.shard_map(
        per_device, mesh=mesh, in_specs=in_specs, out_specs=out_specs, check_vma=False
    )
```

time: 1080 us -> 229 us (0.21)
  waiting for transfers between devices: 941 us -> 91.6 us
  starting transfers between devices: 8.17 us -> 55.3 us
  blocking collectives: 38.9 us -> 0 us
  matrix products: 21.7 us -> 41.6 us
  local copies, waits for them, and re-layouts: 32.4 us -> 17.7 us
    all_gather x3 -> x2, waiting for transfers between devices: 759 us -> 0.29 us  [the longest x1 0.27 us: per_device(): packed_full = lax.all_gather(packed, 'seq', axis=0)]
    unnamed x8 -> x2, waiting for transfers between devices: 143 us -> 0.03 us
    ppermute x0 -> x13, waiting for transfers between devices: none -> 43.2 us  [the longest x4 18.2 us: ring_step(): lax.ppermute(blocks[j - 1], 'seq', [(i, (i - 1) % n_seq) for i in range(n...]
    ppermute x0 -> x13, starting transfers between devices: none -> 30.4 us  [the longest x1 9.84 us: per_device(): d_out_weight = lax.ppermute(block, WHOLE, perm).astype(jnp.float32)]
    all_to_all x1 -> x0, blocking collectives: 23.1 us -> none  [per_device(): lax.all_to_all(pairs.astype(jnp.bfloat16), 'seq', split_axis=1, concat_ax...]
    all_to_all x2 -> x3, starting transfers between devices: 7.75 us -> 24.8 us  [the longest x1 10.3 us: per_device(): lax.all_to_all(grad.reshape(n_dp * n_enc, own_rows, width), PLANE, 0, 0)]
    psum x1 -> x0, blocking collectives: 15.8 us -> none  [per_device(): d_gate = lax.psum(jnp.sum(cot_float * proj, axis=1), 'seq')]
    unnamed x25 -> x29, local copies, waits for them, and re-layouts: 20 us -> 5.27 us
  transfers between devices with their start and end apart: 8 -> 18, of which waited for: 7 -> 12; matrix products, arithmetic and copies ran while one was open for 3% -> 25% of each run, Pallas kernels for 0% -> 0%
where the time goes in v1:
time: 229 us; the launch traced here: 228 us
  waiting for transfers between devices  91.6 us (40%)
  starting transfers between devices  55.3 us (24%)
  matrix products  41.6 us (18%)
  local copies, waits for them, and re-layouts  17.7 us (8%)
  between operations  15.1 us (7%)
  other arithmetic  6.64 us (3%)
    all_to_all x1, waiting for transfers between devices, per_device(): lax.all_to_all(image_qkv.reshape(tok, n_seq, group), 'seq', split_axis=1,...  39.3 us
    dot_general x8, matrix products, per_device(): lax.dot_general(rows, block, (((0,), (0,)), ((), ())), preferred_element_...  18.3 us
    ppermute x4, waiting for transfers between devices, ring_step(): lax.ppermute(blocks[j - 1], 'seq', [(i, (i - 1) % n_seq) for i in range(n...  18.2 us
    ppermute x3, waiting for transfers between devices, per_device(): lax.ppermute(d_gate, 'seq', [(i, i ^ bit) for i in range(n_seq)])  11.1 us
    all_to_all x1, starting transfers between devices, per_device(): lax.all_to_all(grad.reshape(n_dp * n_enc, own_rows, width), PLANE, 0, 0)  10.3 us
    ppermute x1, starting transfers between devices, per_device(): d_out_weight = lax.ppermute(block, WHOLE, perm).astype(jnp.float32)  9.84 us
    ppermute x4, starting transfers between devices, ring_step(): lax.ppermute(blocks[j - 1], 'seq', [(i, (i - 1) % n_seq) for i in range(n...  9.27 us
    all_to_all x1, waiting for transfers between devices, per_device(): lax.all_to_all(grad.reshape(n_dp * n_enc, own_rows, width), PLANE, 0, 0)  8.58 us
  transfers between devices with their start and end apart: 18, of which 12 were waited for; matrix products, arithmetic and copies ran while one was open for 25% of the time, Pallas kernels for 0%

profile of v1, /device:TPU:4, one launch (start us, length us, event | category | flops | bytes accessed | tf_op | source)
XLA Modules:
  0.0 227.9 jit_solution(3366900061419427365)
XLA Ops:
  7.2 0.9 slice.41
  8.1 0.7 slice.42
  8.8 1.7 pad_maximum_fusion.7
  10.6 2.4 %copy.44 = bf16[1,128,4608]{1,2,0:T(8,128)(2,1)} copy(bf16[1,128,4608]{2,1,0:T(8,128)(2,1)} %param.8) | data formatting | bytes 2359296 | tf_op args[0]
  13.0 8.5 %all-to-all-start = ((bf16[128,8,576]{0,2,1:T(8,128)(2,1)}), bf16[128,8,576]{0,2,1:T(8,128)(2,1)S(1)}, u32[]{:S(2)}, u32[]{:S(2)}) async-start(bf16[128,8,576]{0,2,1:T(8,128)(2,1)} %bitcast.108), calls=%async_computation | async-start | bytes 2359296 | tf_op jit(solution)/shard_map/all_to_all | solution.py:44
  21.6 0.9 fusion.16
  22.5 3.2 %collective-permute-start = (bf16[128,2432]{1,0:T(8,128)(2,1)}, bf16[128,2432]{1,0:T(8,128)(2,1)}, u32[]{:S(2)}, u32[]{:S(2)}) collective-permute-start(bf16[128,2432]{1,0:T(8,128)(2,1)} %fusion.16), channel_id=1, source_target_pairs={{0,14},{2,0},{4,2},{6,4},{8,6},{10,8},{12,10},{14,12},{1,15},{3,1}... | collective-permute-start | bytes 1867784 | tf_op jit(solution)/shard_map/ppermute | solution.py:56
  25.7 39.3 %all-to-all-done = bf16[128,8,576]{0,2,1:T(8,128)(2,1)S(1)} async-done(((bf16[128,8,576]{0,2,1:T(8,128)(2,1)}), bf16[128,8,576]{0,2,1:T(8,128)(2,1)S(1)}, u32[]{:S(2)}, u32[]{:S(2)}) %all-to-all-start) | async-done | bytes 1179680 | tf_op jit(solution)/shard_map/all_to_all | solution.py:44
  65.0 1.8 copy.45
  66.7 2.3 reshape.66
  69.0 15.7 %collective-permute-done = bf16[128,2432]{1,0:T(8,128)(2,1)} collective-permute-done((bf16[128,2432]{1,0:T(8,128)(2,1)}, bf16[128,2432]{1,0:T(8,128)(2,1)}, u32[]{:S(2)}, u32[]{:S(2)}) %collective-permute-start) | collective-permute-done | bytes 622624 | tf_op jit(solution)/shard_map/ppermute | solution.py:56
  84.7 1.1 collective-permute-done.1
  85.8 0.3 all-gather.6.cloned.1.call-done
  86.1 0.6 copy-done.8
  86.6 1.0 slice.51
  87.6 1.0 slice_bitcast_fusion.11
  88.7 0.8 pad_maximum_fusion.6
  89.5 3.2 %collective-permute-start.8 = (bf16[8,6,2432]{2,1,0:T(8,128)(2,1)}, bf16[8,6,2432]{2,1,0:T(8,128)(2,1)S(1)}, u32[]{:S(2)}, u32[]{:S(2)}) collective-permute-start(bf16[8,6,2432]{2,1,0:T(8,128)(2,1)} %pad_maximum_fusion.6), channel_id=1, source_target_pairs={{0,1},{1,0},{2,3},{3,2},{4,5},{5,4},{6,7},{7,6},{8,9},{9,8},{10,11... | collective-permute-start | bytes 700424 | tf_op jit(solution)/shard_map/ppermute | solution.py:80
  92.7 7.3 %collective-permute-done.8 = bf16[8,6,2432]{2,1,0:T(8,128)(2,1)S(1)} collective-permute-done((bf16[8,6,2432]{2,1,0:T(8,128)(2,1)}, bf16[8,6,2432]{2,1,0:T(8,128)(2,1)S(1)}, u32[]{:S(2)}, u32[]{:S(2)}) %collective-permute-start.8) | collective-permute-done | bytes 233504 | tf_op jit(solution)/shard_map/ppermute | solution.py:80
  99.9 0.1 select_bitcast_fusion.1
  100.1 0.2 pad_maximum_fusion
  100.2 0.9 reshape.73
  101.2 1.8 slice.43
  103.0 1.2 collective-permute-start.2
  104.2 0.9 collective-permute-start.3
  105.1 1.3 fusion.13
  106.4 1.0 copy-done.6
  107.5 3.3 %collective-permute-start.4 = (bf16[8,32,2,192]{3,1,2,0:T(8,128)(2,1)S(1)}, bf16[8,32,2,192]{3,1,2,0:T(8,128)(2,1)S(1)}, u32[]{:S(2)}, u32[]{:S(2)}) collective-permute-start(bf16[8,32,2,192]{3,1,2,0:T(8,128)(2,1)S(1)} %fusion.26), channel_id=1, source_target_pairs={{0,1},{1,0},{2,3},{3,2},{4,5},{5,4},{6,7},{7,6},{8,9},{9,8},{10,11... | collective-permute-start | bytes 589832 | tf_op jit(solution)/shard_map/ppermute | solution.py:93
  111.5 4.0 %collective-permute-done.4 = bf16[8,32,2,192]{3,1,2,0:T(8,128)(2,1)S(1)} collective-permute-done((bf16[8,32,2,192]{3,1,2,0:T(8,128)(2,1)S(1)}, bf16[8,32,2,192]{3,1,2,0:T(8,128)(2,1)S(1)}, u32[]{:S(2)}, u32[]{:S(2)}) %collective-permute-start.4) | collective-permute-done | bytes 196640 | tf_op jit(solution)/shard_map/ppermute | solution.py:93
  115.4 2.5 %collective-permute-done.2 = bf16[128,2432]{1,0:T(8,128)(2,1)} collective-permute-done((bf16[128,2432]{1,0:T(8,128)(2,1)}, bf16[128,2432]{1,0:T(8,128)(2,1)}, u32[]{:S(2)}, u32[]{:S(2)}) %collective-permute-start.2) | collective-permute-done | bytes 622624 | tf_op jit(solution)/shard_map/ppermute | solution.py:56
  117.9 1.5 collective-permute-done.3
  119.5 1.3 fusion.21
  120.8 0.4 copy.61
  121.2 0.5 reshape.80
  121.8 1.8 collective-permute-start.5
  123.6 0.3 collective-permute-start.6
  123.9 8.0 %fusion.55 = (f32[3,1024]{1,0:T(4,128)S(1)}, f32[3,1024,1280]{2,1,0:T(8,128)}) fusion(f32[1280]{0:T(1024)S(1)} %concatenate.18, bf16[256,3,64]{0,2,1:T(8,128)(2,1)S(1)} %get-tuple-element.36, bf16[1024,3,64]{0,2,1:T(8,128)(2,1)S(1)} %get-tuple-element.32, bf16[1024,3,3,64]{0,3,2,1:T(8,128)(2,1)S(1)} %reshape.66), kind=kOutput, calls=%fused_computation.76 | convolution fusion | flops 520029440 | bytes 16633856 | tf_op jit(solution)/shard_map/sub | solution.py:16
  131.9 8.3 %fusion.15 = bf16[3,64,1024]{2,1,0:T(8,128)(2,1)S(1)} fusion(f32[3,1024,1280]{2,1,0:T(8,128)} %get-tuple-element.38, f32[3,1024]{1,0:T(4,128)S(1)} %get-tuple-element.37, bf16[256,3,64]{0,2,1:T(8,128)(2,1)S(1)} %get-tuple-element.35, bf16[1024,3,64]{0,2,1:T(8,128)(2,1)S(1)} %get-tuple-element.31), kind=kOutput, calls=%fused_computation.21 | convolution fusion | flops 512360448 | bytes 16625664 | tf_op jit(solution)/shard_map/hqk,khe->qhe/dot_general | solution.py:18
  140.3 3.0 %collective-permute-start.7 = (bf16[128,2432]{1,0:T(8,128)(2,1)}, bf16[128,2432]{1,0:T(8,128)(2,1)}, u32[]{:S(2)}, u32[]{:S(2)}) collective-permute-start(bf16[128,2432]{1,0:T(8,128)(2,1)} %collective-permute-done.5), channel_id=1, source_target_pairs={{0,14},{2,0},{4,2},{6,4},{8,6},{10,8},{12,10},{14,12},{1,15},{3,1}... | collective-permute-start | bytes 1867784 | tf_op jit(solution)/shard_map/ppermute | solution.py:56
  143.3 0.8 copy_bitcast_fusion
  144.2 6.1 %all-to-all-start.1 = ((bf16[8,128,192]{1,2,0:T(8,128)(2,1)}), bf16[8,128,192]{1,2,0:T(8,128)(2,1)S(1)}, u32[]{:S(2)}, u32[]{:S(2)}) async-start(bf16[8,128,192]{1,2,0:T(8,128)(2,1)} %copy_bitcast_fusion), calls=%async_computation.1 | async-start | bytes 786432 | tf_op jit(solution)/shard_map/all_to_all | solution.py:111
  150.3 1.5 fusion.38
  151.7 1.5 fusion.35
  153.2 2.8 %fusion.33 = f32[192,2432]{1,0:T(8,128)} fusion(bf16[128,2432]{1,0:T(8,128)(2,1)} %collective-permute-done.3, bf16[1024,192]{0,1:T(8,128)(2,1)S(1)} %bitcast.117, s32[]{:T(128)S(6)} %select_n.108), kind=kOutput, calls=%fused_computation.55 | convolution fusion | flops 119537664 | bytes 2539524 | tf_op jit(solution)/shard_map/dot_general | solution.py:126
  156.0 2.8 %fusion.31 = f32[192,2432]{1,0:T(8,128)} fusion(bf16[128,2432]{1,0:T(8,128)(2,1)} %collective-permute-done.5, bf16[1024,192]{0,1:T(8,128)(2,1)S(1)} %bitcast.118, s32[]{:T(128)S(6)} %select_n.110), kind=kOutput, calls=%fused_computation.53 | convolution fusion | flops 119537664 | bytes 2539524 | tf_op jit(solution)/shard_map/dot_general | solution.py:126
  158.8 1.6 fusion.29
  160.5 2.7 %convolution_add_fusion.1 = f32[192,2432]{1,0:T(8,128)} fusion(f32[192,2432]{1,0:T(8,128)S(1)} %fusion.38, bf16[128,2432]{1,0:T(8,128)(2,1)} %fusion.16, bf16[1024,192]{0,1:T(8,128)(2,1)S(1)} %bitcast.120, s32[]{:T(128)S(6)} %select_n.100), kind=kOutput, calls=%fused_computation.14 | convolution fusion | flops 120004608 | bytes 4407300 | tf_op jit(solution)/shard_map/dot_general | solution.py:126
  163.2 0.2 all-to-all-done.1
  163.4 1.7 fusion.27
  165.1 0.2 copy-done.2
  165.3 3.8 %fusion.10 = bf16[192,2432]{1,0:T(8,128)(2,1)S(1)} fusion(f32[192,2432]{1,0:T(8,128)S(1)} %fusion.27, f32[192,2432]{1,0:T(8,128)} %fusion.29, f32[192,2432]{1,0:T(8,128)} %fusion.31, f32[192,2432]{1,0:T(8,128)S(1)} %copy-done.2, f32[192,2432]{1,0:T(8,128)S(1)} %fusion.35, f32[192,2432]{1,0:T(8,128)} %convolution_add_fusion.1, ...), kind=kOutput, calls=%fused_computation.15 | convolution fusion | flops 122806272 | bytes 12812292 | tf_op jit(solution)/shard_map/dot_general | solution.py:126
  169.0 1.2 reshape.74
  170.3 10.3 %all-to-all-start.2 = ((bf16[32,6,2432]{2,1,0:T(8,128)(2,1)}), bf16[32,6,2432]{2,1,0:T(8,128)(2,1)S(1)}, u32[]{:S(2)}, u32[]{:S(2)}) async-start(bf16[32,6,2432]{2,1,0:T(8,128)(2,1)} %reshape.74), calls=%async_computation.2 | async-start | bytes 2490368 | tf_op jit(solution)/shard_map/all_to_all | solution.py:130
  180.6 5.7 %fusion.17 = (f32[2432]{0:T(1024)S(1)}, bf16[1,128,2432]{2,1,0:T(8,128)(2,1)}) fusion(bf16[1,128,2432]{2,1,0:T(8,128)(2,1)} %param.11, f32[2432]{0:T(1024)S(1)} %reduce.1, bf16[1,128,2432]{2,1,0:T(8,128)(2,1)} %param.9, bf16[128,1536]{0,1:T(8,128)(2,1)S(1)} %bitcast.109, bf16[1536,2432]{1,0:T(8,128)(2,1)} %all-gather.4.cloned.1.call-done), kind=kOutput, calls=%fused_computation.23 | convolution fusion | flops 958477952 | bytes 9751552 | tf_op jit(solution)/shard_map/dot_general | solution.py:116
  186.3 3.1 %collective-permute-start.9 = (f32[1,2432]{1,0:T(1,128)S(1)}, f32[1,2432]{1,0:T(1,128)S(1)}, u32[]{:S(2)}, u32[]{:S(2)}) collective-permute-start(f32[1,2432]{1,0:T(1,128)S(1)} %broadcast_in_dim.21), channel_id=1, source_target_pairs={{0,2},{2,0},{4,6},{6,4},{8,10},{10,8},{12,14},{14,12},{1,3},{3,1},... | collective-permute-start | bytes 29192 | tf_op jit(solution)/shard_map/ppermute | solution.py:120
  189.4 8.6 %all-to-all-done.2 = bf16[32,6,2432]{2,1,0:T(8,128)(2,1)S(1)} async-done(((bf16[32,6,2432]{2,1,0:T(8,128)(2,1)}), bf16[32,6,2432]{2,1,0:T(8,128)(2,1)S(1)}, u32[]{:S(2)}, u32[]{:S(2)}) %all-to-all-start.2) | async-done | bytes 933920 | tf_op jit(solution)/shard_map/all_to_all | solution.py:130
  198.0 0.3 reduce_sum.32
  198.2 9.8 %collective-permute-start.12 = (bf16[6,2432]{1,0:T(8,128)(2,1)S(1)}, bf16[6,2432]{1,0:T(8,128)(2,1)S(1)}, u32[]{:S(2)}, u32[]{:S(2)}) collective-permute-start(bf16[6,2432]{1,0:T(8,128)(2,1)S(1)} %reduce_sum.32), channel_id=1, source_target_pairs={{0,0},{1,1},{2,32},{3,33},{4,64},{5,65},{6,96},{7,97},{8,128},{9,1... | collective-permute-start | bytes 87560 | tf_op jit(solution)/shard_map/ppermute | solution.py:138
  208.1 0.1 collective-permute-start.10
  208.2 4.6 %collective-permute-done.10 = f32[1,2432]{1,0:T(1,128)S(1)} collective-permute-done((f32[1,2432]{1,0:T(1,128)S(1)}, f32[1,2432]{1,0:T(1,128)S(1)}, u32[]{:S(2)}, u32[]{:S(2)}) %collective-permute-start.10) | collective-permute-done | bytes 9760 | tf_op jit(solution)/shard_map/ppermute | solution.py:120
  212.8 0.4 collective-permute-start.11
  213.2 0.6 convert_element_type.63
  213.9 6.6 %collective-permute-done.11 = f32[1,2432]{1,0:T(1,128)S(1)} collective-permute-done((f32[1,2432]{1,0:T(1,128)S(1)}, f32[1,2432]{1,0:T(1,128)S(1)}, u32[]{:S(2)}, u32[]{:S(2)}) %collective-permute-start.11) | collective-permute-done | bytes 9760 | tf_op jit(solution)/shard_map/ppermute | solution.py:120
  220.4 0.6 add.124
  (49 shorter events, 0.5 us)
Async XLA Ops:
  7.2 97.9 %copy-start = (bf16[2,2048,192]{1,2,0:T(8,128)(2,1)S(1)}, bf16[2,2048,192]{1,2,0:T(8,128)(2,1)}, u32[]{:S(2)}) copy-start(bf16[2,2048,192]{1,2,0:T(8,128)(2,1)} %param.13) | copy-start | bytes 4718596
  7.2 78.9 %all-gather.6.cloned.1.call-start = ((), (), s32[]{:S(2)}) async-start(), calls=%async_computation.4 | async-start | bytes 2654208 | tf_op jit(solution)/shard_map/all_gather | solution.py:43
  10.5 11.0 %copy-start.12 = (f32[1,2432]{1,0:T(1,128)S(1)}, f32[1,2432]{1,0:T(1,128)}, u32[]{:S(2)}) copy-start(f32[1,2432]{1,0:T(1,128)} %param.10) | copy-start | bytes 29188
  10.6 11.0 %copy-start.5 = (bf16[1,128,2432]{2,1,0:T(8,128)(2,1)S(1)}, bf16[1,128,2432]{2,1,0:T(8,128)(2,1)}, u32[]{:S(2)}) copy-start(bf16[1,128,2432]{2,1,0:T(8,128)(2,1)} %param.11) | copy-start | bytes 1867780
  13.0 52.0 %all-to-all-start = ((bf16[128,8,576]{0,2,1:T(8,128)(2,1)}), bf16[128,8,576]{0,2,1:T(8,128)(2,1)S(1)}, u32[]{:S(2)}, u32[]{:S(2)}) async-start(bf16[128,8,576]{0,2,1:T(8,128)(2,1)} %bitcast.108), calls=%async_computation | async-start | bytes 2359296 | tf_op jit(solution)/shard_map/all_to_all | solution.py:44
  21.5 159.1 %all-gather.4.cloned.1.call-start = ((), (), s32[]{:S(2)}) async-start(), calls=%async_computation.3 | async-start | bytes 7938048 | tf_op jit(solution)/shard_map/all_gather | solution.py:84
  22.5 62.2 %collective-permute-start = (bf16[128,2432]{1,0:T(8,128)(2,1)}, bf16[128,2432]{1,0:T(8,128)(2,1)}, u32[]{:S(2)}, u32[]{:S(2)}) collective-permute-start(bf16[128,2432]{1,0:T(8,128)(2,1)} %fusion.16), channel_id=1, source_target_pairs={{0,14},{2,0},{4,2},{6,4},{8,6},{10,8},{12,10},{14,12},{1,15},{3,1}... | collective-permute-start | bytes 1867784 | tf_op jit(solution)/shard_map/ppermute | solution.py:56
  25.7 60.1 %collective-permute-start.1 = (bf16[128,2432]{1,0:T(8,128)(2,1)}, bf16[128,2432]{1,0:T(8,128)(2,1)S(1)}, u32[]{:S(2)}, u32[]{:S(2)}) collective-permute-start(bf16[128,2432]{1,0:T(8,128)(2,1)} %fusion.16), channel_id=1, source_target_pairs={{0,2},{2,4},{4,6},{6,8},{8,10},{10,12},{12,14},{14,0},{1,3},{3,5},... | collective-permute-start | bytes 1867784 | tf_op jit(solution)/shard_map/ppermute | solution.py:60
  85.8 0.8 copy-start.8
  89.5 10.5 %collective-permute-start.8 = (bf16[8,6,2432]{2,1,0:T(8,128)(2,1)}, bf16[8,6,2432]{2,1,0:T(8,128)(2,1)S(1)}, u32[]{:S(2)}, u32[]{:S(2)}) collective-permute-start(bf16[8,6,2432]{2,1,0:T(8,128)(2,1)} %pad_maximum_fusion.6), channel_id=1, source_target_pairs={{0,1},{1,0},{2,3},{3,2},{4,5},{5,4},{6,7},{7,6},{8,9},{9,8},{10,11... | collective-permute-start | bytes 700424 | tf_op jit(solution)/shard_map/ppermute | solution.py:80
  101.2 3.1 %copy-start.9 = (bf16[128,2432]{1,0:T(8,128)(2,1)S(1)}, bf16[128,2432]{1,0:T(8,128)(2,1)}, u32[]{:S(2)}) copy-start(bf16[128,2432]{1,0:T(8,128)(2,1)} %copy-done.8) | copy-start | bytes 1867780
  103.0 14.9 %collective-permute-start.2 = (bf16[128,2432]{1,0:T(8,128)(2,1)}, bf16[128,2432]{1,0:T(8,128)(2,1)}, u32[]{:S(2)}, u32[]{:S(2)}) collective-permute-start(bf16[128,2432]{1,0:T(8,128)(2,1)} %collective-permute-done), channel_id=1, source_target_pairs={{0,14},{2,0},{4,2},{6,4},{8,6},{10,8},{12,10},{14,12},{1,15},{3,1}... | collective-permute-start | bytes 1867784 | tf_op jit(solution)/shard_map/ppermute | solution.py:56
  104.2 15.2 %collective-permute-start.3 = (bf16[128,2432]{1,0:T(8,128)(2,1)S(1)}, bf16[128,2432]{1,0:T(8,128)(2,1)}, u32[]{:S(2)}, u32[]{:S(2)}) collective-permute-start(bf16[128,2432]{1,0:T(8,128)(2,1)S(1)} %copy-done.9), channel_id=1, source_target_pairs={{0,2},{2,4},{4,6},{6,8},{8,10},{10,12},{12,14},{14,0},{1,3},{3,5},... | collective-permute-start | bytes 1867784 | tf_op jit(solution)/shard_map/ppermute | solution.py:60
  106.4 1.0 copy-start.6
  107.5 8.0 %collective-permute-start.4 = (bf16[8,32,2,192]{3,1,2,0:T(8,128)(2,1)S(1)}, bf16[8,32,2,192]{3,1,2,0:T(8,128)(2,1)S(1)}, u32[]{:S(2)}, u32[]{:S(2)}) collective-permute-start(bf16[8,32,2,192]{3,1,2,0:T(8,128)(2,1)S(1)} %fusion.26), channel_id=1, source_target_pairs={{0,1},{1,0},{2,3},{3,2},{4,5},{5,4},{6,7},{7,6},{8,9},{9,8},{10,11... | collective-permute-start | bytes 589832 | tf_op jit(solution)/shard_map/ppermute | solution.py:93
  121.8 18.5 %collective-permute-start.5 = (bf16[128,2432]{1,0:T(8,128)(2,1)}, bf16[128,2432]{1,0:T(8,128)(2,1)}, u32[]{:S(2)}, u32[]{:S(2)}) collective-permute-start(bf16[128,2432]{1,0:T(8,128)(2,1)} %collective-permute-done.2), channel_id=1, source_target_pairs={{0,14},{2,0},{4,2},{6,4},{8,6},{10,8},{12,10},{14,12},{1,15},{3,1}... | collective-permute-start | bytes 1867784 | tf_op jit(solution)/shard_map/ppermute | solution.py:56
  123.6 16.7 %collective-permute-start.6 = (bf16[128,2432]{1,0:T(8,128)(2,1)}, bf16[128,2432]{1,0:T(8,128)(2,1)S(1)}, u32[]{:S(2)}, u32[]{:S(2)}) collective-permute-start(bf16[128,2432]{1,0:T(8,128)(2,1)} %collective-permute-done.3), channel_id=1, source_target_pairs={{0,2},{2,4},{4,6},{6,8},{8,10},{10,12},{12,14},{14,0},{1,3},{3,5},... | collective-permute-start | bytes 1867784 | tf_op jit(solution)/shard_map/ppermute | solution.py:60
  140.2 23.2 %copy-start.7 = (bf16[3,64,1024]{2,1,0:T(8,128)(2,1)}, bf16[3,64,1024]{2,1,0:T(8,128)(2,1)S(1)}, u32[]{:S(2)}) copy-start(bf16[3,64,1024]{2,1,0:T(8,128)(2,1)S(1)} %fusion.15) | copy-start | bytes 1179652
  140.3 10.0 %copy-start.10 = (bf16[128,2432]{1,0:T(8,128)(2,1)}, bf16[128,2432]{1,0:T(8,128)(2,1)S(1)}, u32[]{:S(2)}) copy-start(bf16[128,2432]{1,0:T(8,128)(2,1)S(1)} %collective-permute-done.6) | copy-start | bytes 1867780
  140.3 22.9 %collective-permute-start.7 = (bf16[128,2432]{1,0:T(8,128)(2,1)}, bf16[128,2432]{1,0:T(8,128)(2,1)}, u32[]{:S(2)}, u32[]{:S(2)}) collective-permute-start(bf16[128,2432]{1,0:T(8,128)(2,1)} %collective-permute-done.5), channel_id=1, source_target_pairs={{0,14},{2,0},{4,2},{6,4},{8,6},{10,8},{12,10},{14,12},{1,15},{3,1}... | collective-permute-start | bytes 1867784 | tf_op jit(solution)/shard_map/ppermute | solution.py:56
  144.2 19.2 %all-to-all-start.1 = ((bf16[8,128,192]{1,2,0:T(8,128)(2,1)}), bf16[8,128,192]{1,2,0:T(8,128)(2,1)S(1)}, u32[]{:S(2)}, u32[]{:S(2)}) async-start(bf16[8,128,192]{1,2,0:T(8,128)(2,1)} %copy_bitcast_fusion), calls=%async_computation.1 | async-start | bytes 786432 | tf_op jit(solution)/shard_map/all_to_all | solution.py:111
  156.0 2.8 %copy-start.11 = (bf16[128,2432]{1,0:T(8,128)(2,1)S(1)}, bf16[128,2432]{1,0:T(8,128)(2,1)}, u32[]{:S(2)}) copy-start(bf16[128,2432]{1,0:T(8,128)(2,1)} %copy-done.10) | copy-start | bytes 1867780
  163.4 5.6 %copy-start.3 = (bf16[8,128,192]{1,2,0:T(8,128)(2,1)}, bf16[8,128,192]{1,2,0:T(8,128)(2,1)S(1)}, u32[]{:S(2)}) copy-start(bf16[8,128,192]{1,2,0:T(8,128)(2,1)S(1)} %all-to-all-done.1) | copy-start | bytes 1179652
  163.4 1.8 copy-start.2
  170.3 10.3 %copy-start.4 = (bf16[8,128,192]{1,2,0:T(8,128)(2,1)S(1)}, bf16[8,128,192]{1,2,0:T(8,128)(2,1)}, u32[]{:S(2)}) copy-start(bf16[8,128,192]{1,2,0:T(8,128)(2,1)} %copy-done.3) | copy-start | bytes 1179652
  170.3 27.7 %all-to-all-start.2 = ((bf16[32,6,2432]{2,1,0:T(8,128)(2,1)}), bf16[32,6,2432]{2,1,0:T(8,128)(2,1)S(1)}, u32[]{:S(2)}, u32[]{:S(2)}) async-start(bf16[32,6,2432]{2,1,0:T(8,128)(2,1)} %reshape.74), calls=%async_computation.2 | async-start | bytes 2490368 | tf_op jit(solution)/shard_map/all_to_all | solution.py:130
  180.6 40.4 %copy-start.1 = (bf16[2,2048,192]{1,2,0:T(8,128)(2,1)S(1)}, bf16[2,2048,192]{1,2,0:T(8,128)(2,1)}, u32[]{:S(2)}) copy-start(bf16[2,2048,192]{1,2,0:T(8,128)(2,1)} %param.13) | copy-start | bytes 4718596
  186.3 21.8 %collective-permute-start.9 = (f32[1,2432]{1,0:T(1,128)S(1)}, f32[1,2432]{1,0:T(1,128)S(1)}, u32[]{:S(2)}, u32[]{:S(2)}) collective-permute-start(f32[1,2432]{1,0:T(1,128)S(1)} %broadcast_in_dim.21), channel_id=1, source_target_pairs={{0,2},{2,0},{4,6},{6,4},{8,10},{10,8},{12,14},{14,12},{1,3},{3,1},... | collective-permute-start | bytes 29192 | tf_op jit(solution)/shard_map/ppermute | solution.py:120
  198.2 15.0 %collective-permute-start.12 = (bf16[6,2432]{1,0:T(8,128)(2,1)S(1)}, bf16[6,2432]{1,0:T(8,128)(2,1)S(1)}, u32[]{:S(2)}, u32[]{:S(2)}) collective-permute-start(bf16[6,2432]{1,0:T(8,128)(2,1)S(1)} %reduce_sum.32), channel_id=1, source_target_pairs={{0,0},{1,1},{2,32},{3,33},{4,64},{5,65},{6,96},{7,97},{8,128},{9,1... | collective-permute-start | bytes 87560 | tf_op jit(solution)/shard_map/ppermute | solution.py:138
  208.1 4.7 %collective-permute-start.10 = (f32[1,2432]{1,0:T(1,128)S(1)}, f32[1,2432]{1,0:T(1,128)S(1)}, u32[]{:S(2)}, u32[]{:S(2)}) collective-permute-start(f32[1,2432]{1,0:T(1,128)S(1)} %reshape_add_fusion), channel_id=1, source_target_pairs={{0,4},{2,6},{4,0},{6,2},{8,12},{10,14},{12,8},{14,10},{1,5},{3,7},... | collective-permute-start | bytes 29192 | tf_op jit(solution)/shard_map/ppermute | solution.py:120
  212.8 7.7 %collective-permute-start.11 = (f32[1,2432]{1,0:T(1,128)S(1)}, f32[1,2432]{1,0:T(1,128)S(1)}, u32[]{:S(2)}, u32[]{:S(2)}) collective-permute-start(f32[1,2432]{1,0:T(1,128)S(1)} %add.123), channel_id=1, source_target_pairs={{0,8},{2,10},{4,12},{6,14},{8,0},{10,2},{12,4},{14,6},{1,9},{3,11}... | collective-permute-start | bytes 29192 | tf_op jit(solution)/shard_map/ppermute | solution.py:120
Sparse Core Ops, SparseCore 0:
  10.7 75.3 all-gather.5
  101.3 49.8 all-gather.3

commit v2 on v1

v2 whole, which is shorter than its diff:
```python
import functools

import jax
import jax.numpy as jnp
from jax import lax
from jax.experimental import pallas as pl
from jax.experimental.pallas import tpu as pltpu
from jax.sharding import PartitionSpec as P

HEAD = 64
QUERY_ROWS = 256
COLUMNS = 640
PLANE = ("dp", "enc")
WHOLE = ("dp", "seq", "enc")
LOG2E = 1.4426950408889634
DOT_NT = (((1,), (1,)), ((), ()))
DOT_TN = (((0,), (0,)), ((), ()))


def attend_kernel(length_ref, qkv_ref, mine_ref, got_ref, out_ref):
    full, txt = qkv_ref.shape[0], mine_ref.shape[1]
    factor = HEAD ** (-0.5) * LOG2E
    rows = min(QUERY_ROWS, full)
    text_kv = (mine_ref[...] + got_ref[...].astype(jnp.float32)).astype(jnp.bfloat16)
    valid = lax.broadcasted_iota(jnp.int32, (1, txt), 1) < length_ref[0]
    for h in range(out_ref.shape[1] // HEAD):
        base = 3 * h * HEAD
        cols = slice(h * HEAD, (h + 1) * HEAD)
        k_img = qkv_ref[:, base + HEAD : base + 2 * HEAD]
        v_img = qkv_ref[:, base + 2 * HEAD : base + 3 * HEAD]
        k_txt, v_txt = text_kv[0, :, cols], text_kv[1, :, cols]
        for r in range(full // rows):
            q = qkv_ref[r * rows : (r + 1) * rows, base : base + HEAD]
            s_img = lax.dot_general(q, k_img, DOT_NT, preferred_element_type=jnp.float32)
            s_txt = lax.dot_general(q, k_txt, DOT_NT, preferred_element_type=jnp.float32)
            s_txt = jnp.where(valid, s_txt, -jnp.inf)
            top = jnp.maximum(
                jnp.max(s_img, axis=1, keepdims=True), jnp.max(s_txt, axis=1, keepdims=True)
            )
            p_img = jnp.exp2((s_img - top) * factor)
            p_txt = jnp.exp2((s_txt - top) * factor)
            total = jnp.sum(p_img, axis=1, keepdims=True) + jnp.sum(p_txt, axis=1, keepdims=True)
            out = jnp.dot(p_img.astype(jnp.bfloat16), v_img, preferred_element_type=jnp.float32)
            out += jnp.dot(p_txt.astype(jnp.bfloat16), v_txt, preferred_element_type=jnp.float32)
            out_ref[r * rows : (r + 1) * rows, cols] = (out / total).astype(out_ref.dtype)


def attend(length, qkv, mine, got):
    full, group = qkv.shape
    keys = full + mine.shape[1]
    return pl.pallas_call(
        attend_kernel,
        out_shape=jax.ShapeDtypeStruct((full, group // 3), jnp.bfloat16),
        in_specs=[pl.BlockSpec(memory_space=pltpu.SMEM)]
        + [pl.BlockSpec(memory_space=pltpu.VMEM)] * 3,
        out_specs=pl.BlockSpec(memory_space=pltpu.VMEM),
        compiler_params=pltpu.CompilerParams(vmem_limit_bytes=40 * 2**20),
        cost_estimate=pl.CostEstimate(
            flops=4 * full * keys * group // 3,
            bytes_accessed=2 * full * group * 2,
            transcendentals=full * keys * group // (3 * HEAD),
        ),
    )(length, qkv, mine, got)


def grad_kernel(order, start_ref, attn_ref, *refs):
    *block_refs, out_ref = refs
    tok, width = block_refs[0].shape
    count = len(block_refs)
    lhs = []
    for j in order:
        row = lax.rem(start_ref[0] + j + count, count) * tok
        lhs.append(attn_ref[pl.ds(pl.multiple_of(row, tok), tok), :])
    for c in range(0, width, COLUMNS):
        cols = slice(c, min(c + COLUMNS, width))
        total = lax.dot_general(
            lhs[0], block_refs[0][:, cols], DOT_TN, preferred_element_type=jnp.float32
        )
        for rows, ref in zip(lhs[1:], block_refs[1:]):
            total += lax.dot_general(
                rows, ref[:, cols], DOT_TN, preferred_element_type=jnp.float32
            )
        out_ref[:, cols] = total.astype(out_ref.dtype)


def gradient(me, attn, blocks):
    order = sorted(blocks)
    tok, width = blocks[0].shape
    return pl.pallas_call(
        functools.partial(grad_kernel, order),
        out_shape=jax.ShapeDtypeStruct((attn.shape[1], width), jnp.bfloat16),
        in_specs=[pl.BlockSpec(memory_space=pltpu.SMEM)]
        + [pl.BlockSpec(memory_space=pltpu.VMEM)] * (1 + len(order)),
        out_specs=pl.BlockSpec(memory_space=pltpu.VMEM),
        compiler_params=pltpu.CompilerParams(vmem_limit_bytes=40 * 2**20),
        cost_estimate=pl.CostEstimate(
            flops=2 * attn.shape[0] * attn.shape[1] * width,
            bytes_accessed=2 * attn.shape[0] * width,
            transcendentals=0,
        ),
    )(me.reshape(1), attn, *[blocks[j] for j in order])


def per_device(
    image_qkv, residual, gate, cotangent, t5_states, text_weight, out_weight, caption_len
):
    n_dp, n_seq, n_enc = lax.axis_size("dp"), lax.axis_size("seq"), lax.axis_size("enc")
    _, tok, columns = image_qkv.shape
    group = columns // n_seq
    own_rows, width = out_weight.shape
    enc, me = lax.axis_index("enc"), lax.axis_index("seq")
    swap = [(0, 1), (1, 0)]

    w_seq = lax.all_to_all(
        jnp.broadcast_to(out_weight[None], (n_seq, own_rows, width)), "seq", 0, 0
    )
    w_got = lax.ppermute(w_seq, "enc", swap)
    w_pair = jnp.stack(
        [jnp.where(enc == 0, w_seq, w_got), jnp.where(enc == 0, w_got, w_seq)], axis=1
    ).reshape(n_seq * n_enc * own_rows, width)

    t5_full = lax.all_gather(t5_states, "seq", axis=1, tiled=True)
    spread = lax.all_to_all(
        jnp.swapaxes(image_qkv.reshape(tok, n_seq, group), 0, 1), "seq", 0, 0
    )
    spread = spread.reshape(tok * n_seq, group)

    cot_float = cotangent[0].astype(jnp.float32)
    scaled = (gate * cot_float).astype(jnp.bfloat16)
    blocks = {0: scaled}

    def ring_step(j):
        towards = -1 if j > 0 else 1
        blocks[j] = lax.ppermute(
            blocks[j + towards], "seq", [(i, (i + towards) % n_seq) for i in range(n_seq)]
        )

    def done_with(steps, *values):
        held = lax.optimization_barrier((tuple(blocks[j] for j in steps), values))
        blocks.update(zip(steps, held[0]))
        return held[1]

    ring_step(-1)
    ring_step(1)
    t5_full, spread, w_pair = done_with([-1, 1], t5_full, spread, w_pair)
    w_full = lax.all_gather(w_pair, "dp", axis=0, tiled=True)
    ring_step(-2)
    ring_step(2)

    partial = jnp.einsum(
        "ntf,cfa->ncta", t5_full, text_weight, preferred_element_type=jnp.float32
    )
    mine = jnp.where(enc == 0, partial[0], partial[1])
    other = jnp.where(enc == 0, partial[1], partial[0]).astype(jnp.bfloat16)
    got = lax.ppermute(other, "enc", swap)
    (got,) = done_with([-2], got)
    ring_step(-3)

    attn = attend(caption_len, spread, mine, got)
    (attn,) = done_with([-3, 2], attn)
    ring_step(-4)
    ring_step(3)

    attn_tok = lax.all_to_all(
        attn.reshape(n_seq, tok, group // 3), "seq", split_axis=0, concat_axis=0
    )
    attn_tok = jnp.swapaxes(attn_tok, 0, 1).reshape(tok, columns // 3)

    grad = gradient(me, attn, blocks)
    pieces = lax.all_to_all(grad.reshape(n_dp * n_enc, own_rows, width), PLANE, 0, 0)
    proj = jnp.dot(attn_tok, w_full, preferred_element_type=jnp.float32)
    block_out = (residual[0].astype(jnp.float32) + gate * proj).astype(jnp.bfloat16)
    d_gate = jnp.sum(cot_float * proj, axis=0, keepdims=True)
    bit = 1
    while bit < n_seq:
        d_gate = d_gate + lax.ppermute(d_gate, "seq", [(i, i ^ bit) for i in range(n_seq)])
        bit *= 2
    pieces, d_gate = lax.optimization_barrier((pieces, d_gate))
    block = jnp.sum(pieces.astype(jnp.float32), axis=0).astype(jnp.bfloat16)
    perm = [
        ((d * n_seq + s) * n_enc + e, s * n_dp * n_enc + d * n_enc + e)
        for d in range(n_dp)
        for s in range(n_seq)
        for e in range(n_enc)
    ]
    d_out_weight = lax.ppermute(block, WHOLE, perm).astype(jnp.float32)
    return (block_out[None], d_gate, d_out_weight)


def solution(mesh):
    in_specs = (
        P(("dp", "enc"), "seq", None),
        P(("dp", "enc"), "seq", None),
        P(("dp", "enc"), None),
        P(("dp", "enc"), "seq", None),
        P("dp", "seq", "enc"),
        P(None, "enc", "seq"),
        P(("dp", "seq", "enc"), None),
        P(("dp", "enc")),
    )
    out_specs = (
        P(("dp", "enc"), "seq", None),
        P(("dp", "enc"), None),
        P(("dp", "seq", "enc"), None),
    )
    return jax.shard_map(
        per_device, mesh=mesh, in_specs=in_specs, out_specs=out_specs, check_vma=False
    )
```

time: 229 us -> 201 us (0.88)
  matrix products: 41.6 us -> 8.41 us
  waiting for transfers between devices: 91.6 us -> 103 us
  Pallas kernels: 0 us -> 10.7 us
  starting transfers between devices: 55.3 us -> 47.1 us
  local copies, waits for them, and re-layouts: 17.7 us -> 11.8 us
  other arithmetic: 6.64 us -> 2 us
    dot_general x10 -> x1, matrix products: 27.9 us -> 2.85 us  [per_device(): jnp.einsum('ntf,cfa->ncta', t5_full, text_weight, preferred_element_type=...]
    ppermute x7, waiting for transfers between devices: 20.8 us -> 34.3 us  [ring_step(): lax.ppermute(blocks[j + towards], 'seq', [(i, (i + towards) % n_seq) for...]
    pallas_call x0 -> x2, Pallas kernels: none -> 10.7 us  [the longest x1 6.75 us: attend(): pl.pallas_call(attend_kernel, out_shape=jax.ShapeDtypeStruct((full, group...]
    all_to_all x1, waiting for transfers between devices: 8.58 us -> 0.01 us  [per_device(): lax.all_to_all(grad.reshape(n_dp * n_enc, own_rows, width), PLANE, 0, 0)]
    sub x1 -> x0, matrix products: 8 us -> none  [attend(): p = jnp.exp(s - jnp.max(s, axis=-1, keepdims=True))]
    ppermute x1, starting transfers between devices: 9.84 us -> 3.77 us  [per_device(): d_out_weight = lax.ppermute(block, WHOLE, perm).astype(jnp.float32)]
    ppermute x1, waiting for transfers between devices: 7.29 us -> 1.85 us  [per_device(): w_got = lax.ppermute(w_seq, 'enc', swap)]
    ppermute x1, waiting for transfers between devices: 0.01 us -> 5.39 us  [per_device(): d_out_weight = lax.ppermute(block, WHOLE, perm).astype(jnp.float32)]
  transfers between devices with their start and end apart: 18 -> 19, of which waited for: 12 -> 13; matrix products, arithmetic and copies ran while one was open for 25% -> 9% of each run, Pallas kernels for 0% -> 5%
where the time goes in v2:
time: 201 us; the launch traced here: 198 us
  waiting for transfers between devices  103 us (51%)
  starting transfers between devices  47.1 us (23%)
  between operations  14.9 us (7%)
  local copies, waits for them, and re-layouts  11.8 us (6%)
  Pallas kernels  10.7 us (5%)
  matrix products  8.41 us (4%)
    ppermute x7, waiting for transfers between devices, ring_step(): lax.ppermute(blocks[j + towards], 'seq', [(i, (i + towards) % n_seq) for...  34.3 us
    all_to_all x1, waiting for transfers between devices, per_device(): lax.all_to_all(jnp.swapaxes(image_qkv.reshape(tok, n_seq, group), 0, 1),...  32.5 us
    ppermute x3, waiting for transfers between devices, per_device(): lax.ppermute(d_gate, 'seq', [(i, i ^ bit) for i in range(n_seq)])  13.1 us
    all_to_all x1, waiting for transfers between devices, per_device(): lax.all_to_all(jnp.broadcast_to(out_weight[None], (n_seq, own_rows, width...  11.9 us
    ppermute x7, starting transfers between devices, ring_step(): lax.ppermute(blocks[j + towards], 'seq', [(i, (i + towards) % n_seq) for...  9.63 us
    all_to_all x1, starting transfers between devices, per_device(): lax.all_to_all(jnp.broadcast_to(out_weight[None], (n_seq, own_rows, width...  8.47 us
    all_to_all x1, starting transfers between devices, per_device(): lax.all_to_all(grad.reshape(n_dp * n_enc, own_rows, width), PLANE, 0, 0)  7.5 us
    pallas_call x1, Pallas kernels, attend(): pl.pallas_call(attend_kernel, out_shape=jax.ShapeDtypeStruct((full, group...  6.75 us
  transfers between devices with their start and end apart: 19, of which 13 were waited for; matrix products, arithmetic and copies ran while one was open for 9% of the time, Pallas kernels for 5%

profile of v2, /device:TPU:4, one launch (start us, length us, event | category | flops | bytes accessed | tf_op | source)
XLA Modules:
  0.0 197.7 jit_solution(5128991081916859799)
XLA Ops:
  7.2 0.0 copy-start
  7.2 0.0 copy-start.9
  7.2 0.0 all-gather.3.cloned.1.call-start
  7.2 0.7 all-gather.3.cloned.1.call-update
  7.9 1.5 broadcast_in_dim.12
  9.5 8.5 %all-to-all-start.1 = ((bf16[8,6,2432]{2,1,0:T(8,128)(2,1)}), bf16[8,6,2432]{2,1,0:T(8,128)(2,1)S(1)}, u32[]{:S(2)}, u32[]{:S(2)}) async-start(bf16[8,6,2432]{2,1,0:T(8,128)(2,1)} %broadcast_in_dim.12), calls=%async_computation.1 | async-start | bytes 622592 | tf_op jit(solution)/shard_map/all_to_all | solution.py:114
  17.9 0.0 copy-done.9
  17.9 1.4 copy.13
  19.4 11.9 %all-to-all-done.1 = bf16[8,6,2432]{2,1,0:T(8,128)(2,1)S(1)} async-done(((bf16[8,6,2432]{2,1,0:T(8,128)(2,1)}), bf16[8,6,2432]{2,1,0:T(8,128)(2,1)S(1)}, u32[]{:S(2)}, u32[]{:S(2)}) %all-to-all-start.1) | async-done | bytes 233504 | tf_op jit(solution)/shard_map/all_to_all | solution.py:114
  31.3 4.3 %all-to-all-start = ((bf16[8,128,576]{1,2,0:T(8,128)(2,1)}), bf16[8,128,576]{1,2,0:T(8,128)(2,1)}, u32[]{:S(2)}, u32[]{:S(2)}) async-start(bf16[8,128,576]{1,2,0:T(8,128)(2,1)} %bitcast.3), calls=%async_computation | async-start | bytes 2359296 | tf_op jit(solution)/shard_map/all_to_all | solution.py:123
  35.6 0.0 all-gather.5.cloned.1.call-start
  35.7 3.4 %collective-permute-start.2 = (bf16[8,6,2432]{2,1,0:T(8,128)(2,1)S(1)}, bf16[8,6,2432]{2,1,0:T(8,128)(2,1)S(1)}, u32[]{:S(2)}, u32[]{:S(2)}) collective-permute-start(bf16[8,6,2432]{2,1,0:T(8,128)(2,1)S(1)} %all-to-all-done.1), channel_id=1, source_target_pairs={{0,1},{1,0},{2,3},{3,2},{4,5},{5,4},{6,7},{7,6},{8,9},{9,8},{10,11... | collective-permute-start | bytes 700424 | tf_op jit(solution)/shard_map/ppermute | solution.py:117
  39.1 0.1 fusion.8.refs_4_
  39.2 3.2 %collective-permute-start.1 = (bf16[128,2432]{1,0:T(8,128)(2,1)S(1)}, bf16[128,2432]{1,0:T(8,128)(2,1)}, u32[]{:S(2)}, u32[]{:S(2)}) collective-permute-start(bf16[128,2432]{1,0:T(8,128)(2,1)S(1)} %fusion.8.refs_4_), channel_id=1, source_target_pairs={{0,14},{2,0},{4,2},{6,4},{8,6},{10,8},{12,10},{14,12},{1,15},{3,1}... | collective-permute-start | bytes 1867784 | tf_op jit(solution)/shard_map/ppermute | solution.py:134
  42.4 0.0 collective-permute-start
  42.4 1.8 collective-permute-done.2
  44.2 0.1 select_bitcast_fusion.2
  44.3 0.2 pad_maximum_fusion
  44.5 1.0 reshape.39
  45.4 32.5 %all-to-all-done = bf16[8,128,576]{1,2,0:T(8,128)(2,1)} async-done(((bf16[8,128,576]{1,2,0:T(8,128)(2,1)}), bf16[8,128,576]{1,2,0:T(8,128)(2,1)}, u32[]{:S(2)}, u32[]{:S(2)}) %all-to-all-start) | async-done | bytes 1179680 | tf_op jit(solution)/shard_map/all_to_all | solution.py:123
  77.9 2.4 %copy.14 = bf16[8,128,576]{2,1,0:T(8,128)(2,1)} copy(bf16[8,128,576]{1,2,0:T(8,128)(2,1)} %all-to-all-done) | data formatting | bytes 2359296 | tf_op jit(solution)/shard_map/all_to_all | solution.py:123
  80.3 7.4 %collective-permute-done.1.refs_5_ = bf16[128,2432]{1,0:T(8,128)(2,1)} collective-permute-done((bf16[128,2432]{1,0:T(8,128)(2,1)S(1)}, bf16[128,2432]{1,0:T(8,128)(2,1)}, u32[]{:S(2)}, u32[]{:S(2)}) %collective-permute-start.1) | collective-permute-done | bytes 622624 | tf_op jit(solution)/shard_map/ppermute | solution.py:134
  87.7 0.9 collective-permute-done.refs_3_
  88.6 0.0 all-gather.5.cloned.1.call-update
  88.6 1.1 collective-permute-start.3
  89.7 2.9 %fusion.3 = f32[2,2,256,192]{3,2,1,0:T(8,128)S(1)} fusion(bf16[2,2048,192]{1,2,0:T(8,128)(2,1)S(1)} %copy-done, bf16[2,256,2048]{2,1,0:T(8,128)(2,1)} %all-gather.3.cloned.1.call-done), kind=kOutput, calls=%fused_computation.5 | convolution fusion | flops 805306368 | bytes 4456448 | tf_op jit(solution)/shard_map/ntf,cfa->ncta/dot_general | solution.py:150
  92.6 0.1 fusion.12
  92.7 3.3 %collective-permute-start.4 = (bf16[2,256,192]{2,1,0:T(8,128)(2,1)S(1)}, bf16[2,256,192]{2,1,0:T(8,128)(2,1)S(1)}, u32[]{:S(2)}, u32[]{:S(2)}) collective-permute-start(bf16[2,256,192]{2,1,0:T(8,128)(2,1)S(1)} %fusion.12), channel_id=1, source_target_pairs={{0,1},{1,0},{2,3},{3,2},{4,5},{5,4},{6,7},{7,6},{8,9},{9,8},{10,11... | collective-permute-start | bytes 589832 | tf_op jit(solution)/shard_map/ppermute | solution.py:155
  95.9 2.1 %collective-permute-start.6 = (bf16[128,2432]{1,0:T(8,128)(2,1)}, bf16[128,2432]{1,0:T(8,128)(2,1)}, u32[]{:S(2)}, u32[]{:S(2)}) collective-permute-start(bf16[128,2432]{1,0:T(8,128)(2,1)} %collective-permute-done.1.refs_5_), channel_id=1, source_target_pairs={{0,14},{2,0},{4,2},{6,4},{8,6},{10,8},{12,10},{14,12},{1,15},{3,1}... | collective-permute-start | bytes 1867784 | tf_op jit(solution)/shard_map/ppermute | solution.py:134
  98.1 3.0 %collective-permute-done.4.got_ref = bf16[2,256,192]{2,1,0:T(8,128)(2,1)S(1)} collective-permute-done((bf16[2,256,192]{2,1,0:T(8,128)(2,1)S(1)}, bf16[2,256,192]{2,1,0:T(8,128)(2,1)S(1)}, u32[]{:S(2)}, u32[]{:S(2)}) %collective-permute-start.4) | collective-permute-done | bytes 196640 | tf_op jit(solution)/shard_map/ppermute | solution.py:155
  101.1 4.0 %collective-permute-done.3.refs_2_ = bf16[128,2432]{1,0:T(8,128)(2,1)S(1)} collective-permute-done((bf16[128,2432]{1,0:T(8,128)(2,1)S(1)}, bf16[128,2432]{1,0:T(8,128)(2,1)S(1)}, u32[]{:S(2)}, u32[]{:S(2)}) %collective-permute-start.3) | collective-permute-done | bytes 622624 | tf_op jit(solution)/shard_map/ppermute | solution.py:134
  105.2 0.0 collective-permute-start.5
  105.8 0.1 select_bitcast_fusion.mine_ref
  105.9 6.7 %shard_map.103.attn_ref = bf16[1024,192]{1,0:T(8,128)(2,1)S(1)} custom-call(s32[1]{0:T(128)S(6)} %copy.20.length_ref, bf16[1024,576]{1,0:T(8,128)(2,1)S(1)} %bitcast.45, f32[2,256,192]{2,1,0:T(8,128)S(1)} %select_bitcast_fusion.mine_ref, bf16[2,256,192]{2,1,0:T(8,128)(2,1)S(1)} %collective-permute-done.4.got_ref), custom_call_target="tpu_custom_call" | custom-call | flops 1006632960 | bytes 2359296 | tf_op jit(solution)/shard_map/pallas_call | solution.py:51
  112.7 0.0 collective-permute-done.6.refs_6_
  112.7 8.1 %collective-permute-done.5.refs_1_ = bf16[128,2432]{1,0:T(8,128)(2,1)} collective-permute-done((bf16[128,2432]{1,0:T(8,128)(2,1)S(1)}, bf16[128,2432]{1,0:T(8,128)(2,1)}, u32[]{:S(2)}, u32[]{:S(2)}) %collective-permute-start.5) | collective-permute-done | bytes 622624 | tf_op jit(solution)/shard_map/ppermute | solution.py:134
  120.8 0.0 collective-permute-start.7
  120.8 3.2 %collective-permute-start.8 = (bf16[128,2432]{1,0:T(8,128)(2,1)}, bf16[128,2432]{1,0:T(8,128)(2,1)}, u32[]{:S(2)}, u32[]{:S(2)}) collective-permute-start(bf16[128,2432]{1,0:T(8,128)(2,1)} %collective-permute-done.6.refs_6_), channel_id=1, source_target_pairs={{0,14},{2,0},{4,2},{6,4},{8,6},{10,8},{12,10},{14,12},{1,15},{3,1}... | collective-permute-start | bytes 1867784 | tf_op jit(solution)/shard_map/ppermute | solution.py:134
  124.0 1.0 copy.17
  125.0 3.7 %all-to-all-start.2 = ((bf16[8,128,192]{1,2,0:T(8,128)(2,1)}), bf16[8,128,192]{1,2,0:T(8,128)(2,1)S(1)}, u32[]{:S(2)}, u32[]{:S(2)}) async-start(bf16[8,128,192]{1,2,0:T(8,128)(2,1)} %copy.17), calls=%async_computation.2 | async-start | bytes 786432 | tf_op jit(solution)/shard_map/all_to_all | solution.py:164
  128.7 13.9 %collective-permute-done.7.refs_0_ = bf16[128,2432]{1,0:T(8,128)(2,1)} collective-permute-done((bf16[128,2432]{1,0:T(8,128)(2,1)}, bf16[128,2432]{1,0:T(8,128)(2,1)}, u32[]{:S(2)}, u32[]{:S(2)}) %collective-permute-start.7) | collective-permute-done | bytes 622624 | tf_op jit(solution)/shard_map/ppermute | solution.py:134
  142.6 0.0 collective-permute-done.8.refs_7_
  142.6 0.0 copy-done.1
  142.6 1.0 copy-done.2
  143.6 1.1 copy-done.5
  144.7 1.1 copy-done.7
  145.8 3.9 %shard_map.104 = bf16[192,2432]{1,0:T(8,128)(2,1)S(1)} custom-call(s32[1]{0:T(128)} %bitcast.18.start_ref, bf16[1024,192]{1,0:T(8,128)(2,1)S(1)} %copy-done.2, bf16[128,2432]{1,0:T(8,128)(2,1)} %collective-permute-done.7.refs_0_, bf16[128,2432]{1,0:T(8,128)(2,1)} %collective-permute-done.5.refs_1_, bf16[128,2432]{1,0:T(8,128)(2,1)S(1)} %copy-done.7, ...), custom_call_target="tpu_custom_call" | custom-call | flops 956301312 | bytes 4980736 | tf_op jit(solution)/shard_map/pallas_call | solution.py:89
  149.7 1.3 reshape.43
  151.0 0.0 all-to-all-done.2
  151.0 7.5 %all-to-all-start.3 = ((bf16[32,6,2432]{2,1,0:T(8,128)(2,1)}), bf16[32,6,2432]{2,1,0:T(8,128)(2,1)S(1)}, u32[]{:S(2)}, u32[]{:S(2)}) async-start(bf16[32,6,2432]{2,1,0:T(8,128)(2,1)} %reshape.43), calls=%async_computation.3 | async-start | bytes 2490368 | tf_op jit(solution)/shard_map/all_to_all | solution.py:170
  158.5 0.0 all-gather.5.cloned.1.call-done
  158.5 5.6 %fusion.9 = (f32[2432]{0:T(1024)S(1)}, bf16[1,128,2432]{2,1,0:T(8,128)(2,1)}) fusion(bf16[1,128,2432]{2,1,0:T(8,128)(2,1)} %param.11, f32[2432]{0:T(1024)S(1)} %reduce.1, bf16[1,128,2432]{2,1,0:T(8,128)(2,1)} %param.9, bf16[128,1536]{0,1:T(8,128)(2,1)S(1)} %bitcast.46, bf16[1536,2432]{1,0:T(8,128)(2,1)} %all-gather.5.cloned.1.call-done), kind=kOutput, calls=%fused_computation.7 | convolution fusion | flops 958477952 | bytes 9751552 | tf_op jit(solution)/shard_map/dot_general | solution.py:171
  164.1 0.1 collective-permute-start.9
  164.2 3.7 %collective-permute-done.9 = f32[1,2432]{1,0:T(1,128)S(1)} collective-permute-done((f32[1,2432]{1,0:T(1,128)S(1)}, f32[1,2432]{1,0:T(1,128)S(1)}, u32[]{:S(2)}, u32[]{:S(2)}) %collective-permute-start.9) | collective-permute-done | bytes 9760 | tf_op jit(solution)/shard_map/ppermute | solution.py:176
  167.9 0.8 collective-permute-start.10
  168.7 3.9 %collective-permute-done.10 = f32[1,2432]{1,0:T(1,128)S(1)} collective-permute-done((f32[1,2432]{1,0:T(1,128)S(1)}, f32[1,2432]{1,0:T(1,128)S(1)}, u32[]{:S(2)}, u32[]{:S(2)}) %collective-permute-start.10) | collective-permute-done | bytes 9760 | tf_op jit(solution)/shard_map/ppermute | solution.py:176
  172.6 2.1 %collective-permute-start.11 = (f32[1,2432]{1,0:T(1,128)S(1)}, f32[1,2432]{1,0:T(1,128)S(1)}, u32[]{:S(2)}, u32[]{:S(2)}) collective-permute-start(f32[1,2432]{1,0:T(1,128)S(1)} %add.14), channel_id=1, source_target_pairs={{0,8},{2,10},{4,12},{6,14},{8,0},{10,2},{12,4},{14,6},{1,9},{3,11}... | collective-permute-start | bytes 29192 | tf_op jit(solution)/shard_map/ppermute | solution.py:176
  174.6 5.6 %collective-permute-done.11 = f32[1,2432]{1,0:T(1,128)S(1)} collective-permute-done((f32[1,2432]{1,0:T(1,128)S(1)}, f32[1,2432]{1,0:T(1,128)S(1)}, u32[]{:S(2)}, u32[]{:S(2)}) %collective-permute-start.11) | collective-permute-done | bytes 9760 | tf_op jit(solution)/shard_map/ppermute | solution.py:176
  180.2 0.6 add.15
  180.8 0.0 all-to-all-done.3
  180.8 0.3 reduce_sum.22
  181.1 3.8 %collective-permute-start.12 = (bf16[6,2432]{1,0:T(8,128)(2,1)S(1)}, bf16[6,2432]{1,0:T(8,128)(2,1)S(1)}, u32[]{:S(2)}, u32[]{:S(2)}) collective-permute-start(bf16[6,2432]{1,0:T(8,128)(2,1)S(1)} %reduce_sum.22), channel_id=1, source_target_pairs={{0,0},{1,1},{2,32},{3,33},{4,64},{5,65},{6,96},{7,97},{8,128},{9,1... | collective-permute-start | bytes 87560 | tf_op jit(solution)/shard_map/ppermute | solution.py:186
  184.9 5.4 %collective-permute-done.12 = bf16[6,2432]{1,0:T(8,128)(2,1)S(1)} collective-permute-done((bf16[6,2432]{1,0:T(8,128)(2,1)S(1)}, bf16[6,2432]{1,0:T(8,128)(2,1)S(1)}, u32[]{:S(2)}, u32[]{:S(2)}) %collective-permute-start.12) | collective-permute-done | bytes 29216 | tf_op jit(solution)/shard_map/ppermute | solution.py:186
  190.3 0.6 convert_element_type.37
  (20 shorter events, 0.1 us)
Async XLA Ops:
  7.2 82.6 %copy-start = (bf16[2,2048,192]{1,2,0:T(8,128)(2,1)S(1)}, bf16[2,2048,192]{1,2,0:T(8,128)(2,1)}, u32[]{:S(2)}) copy-start(bf16[2,2048,192]{1,2,0:T(8,128)(2,1)} %param.13) | copy-start | bytes 4718596
  7.2 10.7 %copy-start.9 = (bf16[1,128,4608]{2,1,0:T(8,128)(2,1)S(1)}, bf16[1,128,4608]{2,1,0:T(8,128)(2,1)}, u32[]{:S(2)}) copy-start(bf16[1,128,4608]{2,1,0:T(8,128)(2,1)} %param.8) | copy-start | bytes 3538948
  7.2 81.4 %all-gather.3.cloned.1.call-start = ((), (), s32[]{:S(2)}) async-start(), calls=%async_computation.4 | async-start | bytes 2359296 | tf_op jit(solution)/shard_map/all_gather | solution.py:122
  9.5 21.8 %all-to-all-start.1 = ((bf16[8,6,2432]{2,1,0:T(8,128)(2,1)}), bf16[8,6,2432]{2,1,0:T(8,128)(2,1)S(1)}, u32[]{:S(2)}, u32[]{:S(2)}) async-start(bf16[8,6,2432]{2,1,0:T(8,128)(2,1)} %broadcast_in_dim.12), calls=%async_computation.1 | async-start | bytes 622592 | tf_op jit(solution)/shard_map/all_to_all | solution.py:114
  19.4 16.3 %copy-start.10 = (f32[1,2432]{1,0:T(1,128)S(1)}, f32[1,2432]{1,0:T(1,128)}, u32[]{:S(2)}) copy-start(f32[1,2432]{1,0:T(1,128)} %param.10) | copy-start | bytes 29188
  19.4 19.7 %copy-start.8 = (bf16[1,128,2432]{2,1,0:T(8,128)(2,1)S(1)}, bf16[1,128,2432]{2,1,0:T(8,128)(2,1)}, u32[]{:S(2)}) copy-start(bf16[1,128,2432]{2,1,0:T(8,128)(2,1)} %param.11) | copy-start | bytes 1867780
  31.3 46.6 %all-to-all-start = ((bf16[8,128,576]{1,2,0:T(8,128)(2,1)}), bf16[8,128,576]{1,2,0:T(8,128)(2,1)}, u32[]{:S(2)}, u32[]{:S(2)}) async-start(bf16[8,128,576]{1,2,0:T(8,128)(2,1)} %bitcast.3), calls=%async_computation | async-start | bytes 2359296 | tf_op jit(solution)/shard_map/all_to_all | solution.py:123
  35.6 123.0 %all-gather.5.cloned.1.call-start = ((), (), s32[]{:S(2)}) async-start(), calls=%async_computation.5 | async-start | bytes 7938048 | tf_op jit(solution)/shard_map/all_gather | solution.py:146
  35.7 8.5 %collective-permute-start.2 = (bf16[8,6,2432]{2,1,0:T(8,128)(2,1)S(1)}, bf16[8,6,2432]{2,1,0:T(8,128)(2,1)S(1)}, u32[]{:S(2)}, u32[]{:S(2)}) collective-permute-start(bf16[8,6,2432]{2,1,0:T(8,128)(2,1)S(1)} %all-to-all-done.1), channel_id=1, source_target_pairs={{0,1},{1,0},{2,3},{3,2},{4,5},{5,4},{6,7},{7,6},{8,9},{9,8},{10,11... | collective-permute-start | bytes 700424 | tf_op jit(solution)/shard_map/ppermute | solution.py:117
  39.2 48.5 %collective-permute-start.1 = (bf16[128,2432]{1,0:T(8,128)(2,1)S(1)}, bf16[128,2432]{1,0:T(8,128)(2,1)}, u32[]{:S(2)}, u32[]{:S(2)}) collective-permute-start(bf16[128,2432]{1,0:T(8,128)(2,1)S(1)} %fusion.8.refs_4_), channel_id=1, source_target_pairs={{0,14},{2,0},{4,2},{6,4},{8,6},{10,8},{12,10},{14,12},{1,15},{3,1}... | collective-permute-start | bytes 1867784 | tf_op jit(solution)/shard_map/ppermute | solution.py:134
  42.4 46.2 %collective-permute-start = (bf16[128,2432]{1,0:T(8,128)(2,1)S(1)}, bf16[128,2432]{1,0:T(8,128)(2,1)S(1)}, u32[]{:S(2)}, u32[]{:S(2)}) collective-permute-start(bf16[128,2432]{1,0:T(8,128)(2,1)S(1)} %fusion.8.refs_4_), channel_id=1, source_target_pairs={{0,2},{2,4},{4,6},{6,8},{8,10},{10,12},{12,14},{14,0},{1,3},{3,5},... | collective-permute-start | bytes 1867784 | tf_op jit(solution)/shard_map/ppermute | solution.py:134
  88.6 4.0 %copy-start.4 = (bf16[128,2432]{1,0:T(8,128)(2,1)}, bf16[128,2432]{1,0:T(8,128)(2,1)S(1)}, u32[]{:S(2)}) copy-start(bf16[128,2432]{1,0:T(8,128)(2,1)S(1)} %collective-permute-done.refs_3_) | copy-start | bytes 1867780
  88.6 16.5 %collective-permute-start.3 = (bf16[128,2432]{1,0:T(8,128)(2,1)S(1)}, bf16[128,2432]{1,0:T(8,128)(2,1)S(1)}, u32[]{:S(2)}, u32[]{:S(2)}) collective-permute-start(bf16[128,2432]{1,0:T(8,128)(2,1)S(1)} %collective-permute-done.refs_3_), channel_id=1, source_target_pairs={{0,2},{2,4},{4,6},{6,8},{8,10},{10,12},{12,14},{14,0},{1,3},{3,5},... | collective-permute-start | bytes 1867784 | tf_op jit(solution)/shard_map/ppermute | solution.py:134
  92.6 13.3 %copy-start.3 = (bf16[8,128,576]{2,1,0:T(8,128)(2,1)S(1)}, bf16[8,128,576]{2,1,0:T(8,128)(2,1)}, u32[]{:S(2)}) copy-start(bf16[8,128,576]{2,1,0:T(8,128)(2,1)} %copy.14) | copy-start | bytes 3538948
  92.7 8.5 %collective-permute-start.4 = (bf16[2,256,192]{2,1,0:T(8,128)(2,1)S(1)}, bf16[2,256,192]{2,1,0:T(8,128)(2,1)S(1)}, u32[]{:S(2)}, u32[]{:S(2)}) collective-permute-start(bf16[2,256,192]{2,1,0:T(8,128)(2,1)S(1)} %fusion.12), channel_id=1, source_target_pairs={{0,1},{1,0},{2,3},{3,2},{4,5},{5,4},{6,7},{7,6},{8,9},{9,8},{10,11... | collective-permute-start | bytes 589832 | tf_op jit(solution)/shard_map/ppermute | solution.py:155
  95.9 16.8 %collective-permute-start.6 = (bf16[128,2432]{1,0:T(8,128)(2,1)}, bf16[128,2432]{1,0:T(8,128)(2,1)}, u32[]{:S(2)}, u32[]{:S(2)}) collective-permute-start(bf16[128,2432]{1,0:T(8,128)(2,1)} %collective-permute-done.1.refs_5_), channel_id=1, source_target_pairs={{0,14},{2,0},{4,2},{6,4},{8,6},{10,8},{12,10},{14,12},{1,15},{3,1}... | collective-permute-start | bytes 1867784 | tf_op jit(solution)/shard_map/ppermute | solution.py:134
  105.2 7.5 %copy-start.6 = (bf16[128,2432]{1,0:T(8,128)(2,1)}, bf16[128,2432]{1,0:T(8,128)(2,1)S(1)}, u32[]{:S(2)}) copy-start(bf16[128,2432]{1,0:T(8,128)(2,1)S(1)} %collective-permute-done.3.refs_2_) | copy-start | bytes 1867780
  105.2 15.6 %collective-permute-start.5 = (bf16[128,2432]{1,0:T(8,128)(2,1)S(1)}, bf16[128,2432]{1,0:T(8,128)(2,1)}, u32[]{:S(2)}, u32[]{:S(2)}) collective-permute-start(bf16[128,2432]{1,0:T(8,128)(2,1)S(1)} %collective-permute-done.3.refs_2_), channel_id=1, source_target_pairs={{0,2},{2,4},{4,6},{6,8},{8,10},{10,12},{12,14},{14,0},{1,3},{3,5},... | collective-permute-start | bytes 1867784 | tf_op jit(solution)/shard_map/ppermute | solution.py:134
  112.7 29.9 %copy-start.1 = (bf16[1024,192]{1,0:T(8,128)(2,1)}, bf16[1024,192]{1,0:T(8,128)(2,1)S(1)}, u32[]{:S(2)}) copy-start(bf16[1024,192]{1,0:T(8,128)(2,1)S(1)} %shard_map.103.attn_ref) | copy-start | bytes 1179652
  120.8 21.8 %collective-permute-start.7 = (bf16[128,2432]{1,0:T(8,128)(2,1)}, bf16[128,2432]{1,0:T(8,128)(2,1)}, u32[]{:S(2)}, u32[]{:S(2)}) collective-permute-start(bf16[128,2432]{1,0:T(8,128)(2,1)} %collective-permute-done.5.refs_1_), channel_id=1, source_target_pairs={{0,2},{2,4},{4,6},{6,8},{8,10},{10,12},{12,14},{14,0},{1,3},{3,5},... | collective-permute-start | bytes 1867784 | tf_op jit(solution)/shard_map/ppermute | solution.py:134
  120.8 21.8 %collective-permute-start.8 = (bf16[128,2432]{1,0:T(8,128)(2,1)}, bf16[128,2432]{1,0:T(8,128)(2,1)}, u32[]{:S(2)}, u32[]{:S(2)}) collective-permute-start(bf16[128,2432]{1,0:T(8,128)(2,1)} %collective-permute-done.6.refs_6_), channel_id=1, source_target_pairs={{0,14},{2,0},{4,2},{6,4},{8,6},{10,8},{12,10},{14,12},{1,15},{3,1}... | collective-permute-start | bytes 1867784 | tf_op jit(solution)/shard_map/ppermute | solution.py:134
  125.0 26.0 %all-to-all-start.2 = ((bf16[8,128,192]{1,2,0:T(8,128)(2,1)}), bf16[8,128,192]{1,2,0:T(8,128)(2,1)S(1)}, u32[]{:S(2)}, u32[]{:S(2)}) async-start(bf16[8,128,192]{1,2,0:T(8,128)(2,1)} %copy.17), calls=%async_computation.2 | async-start | bytes 786432 | tf_op jit(solution)/shard_map/all_to_all | solution.py:164
  142.6 1.0 copy-start.2
  143.6 1.1 copy-start.5
  144.7 1.1 copy-start.7
  151.0 29.8 %all-to-all-start.3 = ((bf16[32,6,2432]{2,1,0:T(8,128)(2,1)}), bf16[32,6,2432]{2,1,0:T(8,128)(2,1)S(1)}, u32[]{:S(2)}, u32[]{:S(2)}) async-start(bf16[32,6,2432]{2,1,0:T(8,128)(2,1)} %reshape.43), calls=%async_computation.3 | async-start | bytes 2490368 | tf_op jit(solution)/shard_map/all_to_all | solution.py:170
  164.1 3.8 %collective-permute-start.9 = (f32[1,2432]{1,0:T(1,128)S(1)}, f32[1,2432]{1,0:T(1,128)S(1)}, u32[]{:S(2)}, u32[]{:S(2)}) collective-permute-start(f32[1,2432]{1,0:T(1,128)S(1)} %broadcast_in_dim.14), channel_id=1, source_target_pairs={{0,2},{2,0},{4,6},{6,4},{8,10},{10,8},{12,14},{14,12},{1,3},{3,1},... | collective-permute-start | bytes 29192 | tf_op jit(solution)/shard_map/ppermute | solution.py:176
  167.9 4.7 %collective-permute-start.10 = (f32[1,2432]{1,0:T(1,128)S(1)}, f32[1,2432]{1,0:T(1,128)S(1)}, u32[]{:S(2)}, u32[]{:S(2)}) collective-permute-start(f32[1,2432]{1,0:T(1,128)S(1)} %reshape_add_fusion), channel_id=1, source_target_pairs={{0,4},{2,6},{4,0},{6,2},{8,12},{10,14},{12,8},{14,10},{1,5},{3,7},... | collective-permute-start | bytes 29192 | tf_op jit(solution)/shard_map/ppermute | solution.py:176
  172.6 7.7 %collective-permute-start.11 = (f32[1,2432]{1,0:T(1,128)S(1)}, f32[1,2432]{1,0:T(1,128)S(1)}, u32[]{:S(2)}, u32[]{:S(2)}) collective-permute-start(f32[1,2432]{1,0:T(1,128)S(1)} %add.14), channel_id=1, source_target_pairs={{0,8},{2,10},{4,12},{6,14},{8,0},{10,2},{12,4},{14,6},{1,9},{3,11}... | collective-permute-start | bytes 29192 | tf_op jit(solution)/shard_map/ppermute | solution.py:176
  181.1 9.2 %collective-permute-start.12 = (bf16[6,2432]{1,0:T(8,128)(2,1)S(1)}, bf16[6,2432]{1,0:T(8,128)(2,1)S(1)}, u32[]{:S(2)}, u32[]{:S(2)}) collective-permute-start(bf16[6,2432]{1,0:T(8,128)(2,1)S(1)} %reduce_sum.22), channel_id=1, source_target_pairs={{0,0},{1,1},{2,32},{3,33},{4,64},{5,65},{6,96},{7,97},{8,128},{9,1... | collective-permute-start | bytes 87560 | tf_op jit(solution)/shard_map/ppermute | solution.py:186
Sparse Core Ops, SparseCore 0:
  9.8 69.2 all-gather.2
  88.8 48.3 all-gather.4

commit v3 on v2

--- a/solution.py
+++ b/solution.py
@@ -63,42 +63,42 @@
     )(length, qkv, mine, got)
 
 
-def grad_kernel(order, start_ref, attn_ref, *refs):
-    *block_refs, out_ref = refs
-    tok, width = block_refs[0].shape
-    count = len(block_refs)
+def grad_kernel(places, count, start_ref, attn_ref, *refs):
+    block_refs, before_refs, out_ref = refs[: len(places)], refs[len(places) : -1], refs[-1]
+    tok, width = attn_ref.shape[0] // count, out_ref.shape[1]
     lhs = []
-    for j in order:
-        row = lax.rem(start_ref[0] + j + count, count) * tok
-        lhs.append(attn_ref[pl.ds(pl.multiple_of(row, tok), tok), :])
+    for (j, first), ref in zip(places, block_refs):
+        rows = ref.shape[0]
+        row = lax.rem(start_ref[0] + j + count, count) * tok + first
+        lhs.append(attn_ref[pl.ds(pl.multiple_of(row, rows), rows), :])
     for c in range(0, width, COLUMNS):
         cols = slice(c, min(c + COLUMNS, width))
-        total = lax.dot_general(
-            lhs[0], block_refs[0][:, cols], DOT_TN, preferred_element_type=jnp.float32
+        parts = [
+            lax.dot_general(rows, ref[:, cols], DOT_TN, preferred_element_type=jnp.float32)
+            for rows, ref in zip(lhs, block_refs)
+        ]
+        out_ref[:, cols] = sum(parts[1:] + [r[:, cols] for r in before_refs], parts[0]).astype(
+            out_ref.dtype
         )
-        for rows, ref in zip(lhs[1:], block_refs[1:]):
-            total += lax.dot_general(
-                rows, ref[:, cols], DOT_TN, preferred_element_type=jnp.float32
-            )
-        out_ref[:, cols] = total.astype(out_ref.dtype)
-
-
-def gradient(me, attn, blocks):
-    order = sorted(blocks)
-    tok, width = blocks[0].shape
+
+
+def gradient(me, count, attn, blocks, dtype, *before):
+    places, arrays = list(blocks), list(blocks.values())
+    width = arrays[0].shape[1]
+    rows = sum(a.shape[0] for a in arrays)
     return pl.pallas_call(
-        functools.partial(grad_kernel, order),
-        out_shape=jax.ShapeDtypeStruct((attn.shape[1], width), jnp.bfloat16),
+        functools.partial(grad_kernel, places, count),
+        out_shape=jax.ShapeDtypeStruct((attn.shape[1], width), dtype),
         in_specs=[pl.BlockSpec(memory_space=pltpu.SMEM)]
-        + [pl.BlockSpec(memory_space=pltpu.VMEM)] * (1 + len(order)),
+        + [pl.BlockSpec(memory_space=pltpu.VMEM)] * (1 + len(arrays) + len(before)),
         out_specs=pl.BlockSpec(memory_space=pltpu.VMEM),
         compiler_params=pltpu.CompilerParams(vmem_limit_bytes=40 * 2**20),
         cost_estimate=pl.CostEstimate(
-            flops=2 * attn.shape[0] * attn.shape[1] * width,
-            bytes_accessed=2 * attn.shape[0] * width,
+            flops=2 * rows * attn.shape[1] * width,
+            bytes_accessed=2 * rows * width,
             transcendentals=0,
         ),
-    )(me.reshape(1), attn, *[blocks[j] for j in order])
+    )(me.reshape(1), attn, *arrays, *before)
 
 
 def per_device(
@@ -119,21 +119,16 @@
         [jnp.where(enc == 0, w_seq, w_got), jnp.where(enc == 0, w_got, w_seq)], axis=1
     ).reshape(n_seq * n_enc * own_rows, width)
 
-    t5_full = lax.all_gather(t5_states, "seq", axis=1, tiled=True)
-    spread = lax.all_to_all(
-        jnp.swapaxes(image_qkv.reshape(tok, n_seq, group), 0, 1), "seq", 0, 0
-    )
-    spread = spread.reshape(tok * n_seq, group)
-
     cot_float = cotangent[0].astype(jnp.float32)
     scaled = (gate * cot_float).astype(jnp.bfloat16)
     blocks = {0: scaled}
 
+    def send(block, towards):
+        return lax.ppermute(block, "seq", [(i, (i + towards) % n_seq) for i in range(n_seq)])
+
     def ring_step(j):
         towards = -1 if j > 0 else 1
-        blocks[j] = lax.ppermute(
-            blocks[j + towards], "seq", [(i, (i + towards) % n_seq) for i in range(n_seq)]
-        )
+        blocks[j] = send(blocks[j + towards], towards)
 
     def done_with(steps, *values):
         held = lax.optimization_barrier((tuple(blocks[j] for j in steps), values))
@@ -142,10 +137,18 @@
 
     ring_step(-1)
     ring_step(1)
-    t5_full, spread, w_pair = done_with([-1, 1], t5_full, spread, w_pair)
-    w_full = lax.all_gather(w_pair, "dp", axis=0, tiled=True)
+
+    t5_full = lax.all_gather(t5_states, "seq", axis=1, tiled=True)
+    (image_qkv,) = done_with([-1, 1], image_qkv)
+    spread = lax.all_to_all(
+        jnp.swapaxes(image_qkv.reshape(tok, n_seq, group), 0, 1), "seq", 0, 0
+    )
+    spread = spread.reshape(tok * n_seq, group)
+
     ring_step(-2)
     ring_step(2)
+    t5_full, spread, w_pair = lax.optimization_barrier((t5_full, spread, w_pair))
+    w_full = lax.all_gather(w_pair, "dp", axis=0, tiled=True)
 
     partial = jnp.einsum(
         "ntf,cfa->ncta", t5_full, text_weight, preferred_element_type=jnp.float32
@@ -153,20 +156,25 @@
     mine = jnp.where(enc == 0, partial[0], partial[1])
     other = jnp.where(enc == 0, partial[1], partial[0]).astype(jnp.bfloat16)
     got = lax.ppermute(other, "enc", swap)
-    (got,) = done_with([-2], got)
+    (got,) = done_with([-2, 2], got)
     ring_step(-3)
+    ring_step(3)
 
     attn = attend(caption_len, spread, mine, got)
-    (attn,) = done_with([-3, 2], attn)
-    ring_step(-4)
-    ring_step(3)
+    (attn,) = done_with([-3, 3], attn)
+    last = n_seq // 2
+    opposite = {
+        (last, 0): send(blocks[1 - last][: tok // 2], 1),
+        (last, tok // 2): send(blocks[last - 1][tok // 2 :], -1),
+    }
 
     attn_tok = lax.all_to_all(
         attn.reshape(n_seq, tok, group // 3), "seq", split_axis=0, concat_axis=0
     )
     attn_tok = jnp.swapaxes(attn_tok, 0, 1).reshape(tok, columns // 3)
 
-    grad = gradient(me, attn, blocks)
+    grad = gradient(me, n_seq, attn, {(j, 0): b for j, b in blocks.items()}, jnp.float32)
+    grad = gradient(me, n_seq, attn, opposite, jnp.bfloat16, grad)
     pieces = lax.all_to_all(grad.reshape(n_dp * n_enc, own_rows, width), PLANE, 0, 0)
     proj = jnp.dot(attn_tok, w_full, preferred_element_type=jnp.float32)
     block_out = (residual[0].astype(jnp.float32) + gate * proj).astype(jnp.bfloat16)

time: 201 us -> 192 us (0.955)
  waiting for transfers between devices: 103 us -> 67.9 us
  starting transfers between devices: 47.1 us -> 66 us
  local copies, waits for them, and re-layouts: 11.8 us -> 15.6 us
  other arithmetic: 2 us -> 5.57 us
    all_to_all x1, waiting for transfers between devices: 32.5 us -> 21.7 us  [per_device(): lax.all_to_all(jnp.swapaxes(image_qkv.reshape(tok, n_seq, group), 0, 1),...]
    all_to_all x1, waiting for transfers between devices: 11.9 us -> 2.49 us  [per_device(): lax.all_to_all(jnp.broadcast_to(out_weight[None], (n_seq, own_rows, width...]
    ppermute x3, starting transfers between devices: 2.96 us -> 10.1 us  [per_device(): lax.ppermute(d_gate, 'seq', [(i, i ^ bit) for i in range(n_seq)])]
    ppermute x7 -> x8, waiting for transfers between devices: 34.3 us -> 27.4 us  [send(): lax.ppermute(block, 'seq', [(i, (i + towards) % n_seq) for i in range(n_s...]
    ppermute x3, waiting for transfers between devices: 13.1 us -> 6.31 us  [per_device(): lax.ppermute(d_gate, 'seq', [(i, i ^ bit) for i in range(n_seq)])]
    ppermute x7 -> x8, starting transfers between devices: 9.63 us -> 16 us  [send(): lax.ppermute(block, 'seq', [(i, (i + towards) % n_seq) for i in range(n_s...]
    ppermute x1, waiting for transfers between devices: 1.85 us -> 5.16 us  [per_device(): w_got = lax.ppermute(w_seq, 'enc', swap)]
    ppermute x1, starting transfers between devices: 3.77 us -> 6.82 us  [per_device(): d_out_weight = lax.ppermute(block, WHOLE, perm).astype(jnp.float32)]
  transfers between devices with their start and end apart: 19 -> 20, of which waited for: 13 -> 12; matrix products, arithmetic and copies ran while one was open for 9% -> 13% of each run, Pallas kernels for 5% -> 6%
where the time goes in v3:
time: 192 us; the launch traced here: 190 us
  waiting for transfers between devices  67.9 us (35%)
  starting transfers between devices  66 us (34%)
  local copies, waits for them, and re-layouts  15.6 us (8%)
  between operations  14.9 us (8%)
  Pallas kernels  11.7 us (6%)
  matrix products  8.33 us (4%)
  other arithmetic  5.57 us (3%)
    ppermute x8, waiting for transfers between devices, send(): lax.ppermute(block, 'seq', [(i, (i + towards) % n_seq) for i in range(n_s...  27.4 us
    all_to_all x1, waiting for transfers between devices, per_device(): lax.all_to_all(jnp.swapaxes(image_qkv.reshape(tok, n_seq, group), 0, 1),...  21.7 us
    ppermute x8, starting transfers between devices, send(): lax.ppermute(block, 'seq', [(i, (i + towards) % n_seq) for i in range(n_s...  16 us
    ppermute x3, starting transfers between devices, per_device(): lax.ppermute(d_gate, 'seq', [(i, i ^ bit) for i in range(n_seq)])  10.1 us
    all_to_all x1, starting transfers between devices, per_device(): lax.all_to_all(grad.reshape(n_dp * n_enc, own_rows, width), PLANE, 0, 0)  9.28 us
    ppermute x1, starting transfers between devices, per_device(): d_out_weight = lax.ppermute(block, WHOLE, perm).astype(jnp.float32)  6.82 us
    pallas_call x1, Pallas kernels, attend(): pl.pallas_call(attend_kernel, out_shape=jax.ShapeDtypeStruct((full, group...  6.78 us
    all_to_all x1, starting transfers between devices, per_device(): lax.all_to_all(jnp.swapaxes(image_qkv.reshape(tok, n_seq, group), 0, 1),...  6.67 us
  transfers between devices with their start and end apart: 20, of which 12 were waited for; matrix products, arithmetic and copies ran while one was open for 13% of the time, Pallas kernels for 6%

profile of v3, /device:TPU:4, one launch (start us, length us, event | category | flops | bytes accessed | tf_op | source)
XLA Modules:
  0.0 190.0 jit_solution(15359808545625859212)
XLA Ops:
  7.2 0.0 copy-start
  7.2 0.0 all-gather.3.cloned.1.call-start
  7.2 0.7 all-gather.3.cloned.1.call-update
  7.9 0.7 reduce.1
  8.7 1.2 fusion.8.refs_0_
  9.8 2.0 %collective-permute-start = (bf16[128,2432]{1,0:T(8,128)(2,1)S(1)}, bf16[128,2432]{1,0:T(8,128)(2,1)S(1)}, u32[]{:S(2)}, u32[]{:S(2)}) collective-permute-start(bf16[128,2432]{1,0:T(8,128)(2,1)S(1)} %fusion.8.refs_0_), channel_id=1, source_target_pairs={{0,2},{2,4},{4,6},{6,8},{8,10},{10,12},{12,14},{14,0},{1,3},{3,5},... | collective-permute-start | bytes 1867784 | tf_op jit(solution)/shard_map/ppermute | solution.py:127
  11.8 4.0 %collective-permute-start.1 = (bf16[128,2432]{1,0:T(8,128)(2,1)S(1)}, bf16[128,2432]{1,0:T(8,128)(2,1)}, u32[]{:S(2)}, u32[]{:S(2)}) collective-permute-start(bf16[128,2432]{1,0:T(8,128)(2,1)S(1)} %fusion.8.refs_0_), channel_id=1, source_target_pairs={{0,14},{2,0},{4,2},{6,4},{8,6},{10,8},{12,10},{14,12},{1,15},{3,1}... | collective-permute-start | bytes 1867784 | tf_op jit(solution)/shard_map/ppermute | solution.py:127
  15.9 0.7 broadcast_in_dim.12
  16.6 5.8 %all-to-all-start.1 = ((bf16[8,6,2432]{2,1,0:T(8,128)(2,1)}), bf16[8,6,2432]{2,1,0:T(8,128)(2,1)S(1)}, u32[]{:S(2)}, u32[]{:S(2)}) async-start(bf16[8,6,2432]{2,1,0:T(8,128)(2,1)} %broadcast_in_dim.12), calls=%async_computation.1 | async-start | bytes 622592 | tf_op jit(solution)/shard_map/all_to_all | solution.py:114
  22.4 12.1 %collective-permute-done.refs_1_ = bf16[128,2432]{1,0:T(8,128)(2,1)S(1)} collective-permute-done((bf16[128,2432]{1,0:T(8,128)(2,1)S(1)}, bf16[128,2432]{1,0:T(8,128)(2,1)S(1)}, u32[]{:S(2)}, u32[]{:S(2)}) %collective-permute-start) | collective-permute-done | bytes 622624 | tf_op jit(solution)/shard_map/ppermute | solution.py:127
  34.5 5.3 %collective-permute-done.1.refs_2_ = bf16[128,2432]{1,0:T(8,128)(2,1)} collective-permute-done((bf16[128,2432]{1,0:T(8,128)(2,1)S(1)}, bf16[128,2432]{1,0:T(8,128)(2,1)}, u32[]{:S(2)}, u32[]{:S(2)}) %collective-permute-start.1) | collective-permute-done | bytes 622624 | tf_op jit(solution)/shard_map/ppermute | solution.py:127
  39.8 2.4 %copy.13 = bf16[1,128,4608]{1,2,0:T(8,128)(2,1)} copy(bf16[1,128,4608]{2,1,0:T(8,128)(2,1)} %param.8) | data formatting | bytes 2359296 | tf_op jit(solution)/shard_map/optimization_barrier | solution.py:134
  42.2 2.5 %all-to-all-done.1 = bf16[8,6,2432]{2,1,0:T(8,128)(2,1)S(1)} async-done(((bf16[8,6,2432]{2,1,0:T(8,128)(2,1)}), bf16[8,6,2432]{2,1,0:T(8,128)(2,1)S(1)}, u32[]{:S(2)}, u32[]{:S(2)}) %all-to-all-start.1) | async-done | bytes 233504 | tf_op jit(solution)/shard_map/all_to_all | solution.py:114
  44.7 6.7 %all-to-all-start = ((bf16[8,128,576]{1,2,0:T(8,128)(2,1)}), bf16[8,128,576]{1,2,0:T(8,128)(2,1)}, u32[]{:S(2)}, u32[]{:S(2)}) async-start(bf16[8,128,576]{1,2,0:T(8,128)(2,1)} %bitcast.46), calls=%async_computation | async-start | bytes 2359296 | tf_op jit(solution)/shard_map/all_to_all | solution.py:143
  51.3 0.0 all-gather.5.cloned.1.call-start
  51.4 3.4 %collective-permute-start.4 = (bf16[8,6,2432]{2,1,0:T(8,128)(2,1)S(1)}, bf16[8,6,2432]{2,1,0:T(8,128)(2,1)}, u32[]{:S(2)}, u32[]{:S(2)}) collective-permute-start(bf16[8,6,2432]{2,1,0:T(8,128)(2,1)S(1)} %all-to-all-done.1), channel_id=1, source_target_pairs={{0,1},{1,0},{2,3},{3,2},{4,5},{5,4},{6,7},{7,6},{8,9},{9,8},{10,11... | collective-permute-start | bytes 700424 | tf_op jit(solution)/shard_map/ppermute | solution.py:117
  54.8 5.2 %collective-permute-done.4 = bf16[8,6,2432]{2,1,0:T(8,128)(2,1)} collective-permute-done((bf16[8,6,2432]{2,1,0:T(8,128)(2,1)S(1)}, bf16[8,6,2432]{2,1,0:T(8,128)(2,1)}, u32[]{:S(2)}, u32[]{:S(2)}) %collective-permute-start.4) | collective-permute-done | bytes 233504 | tf_op jit(solution)/shard_map/ppermute | solution.py:117
  60.0 1.0 select_bitcast_fusion.2
  61.0 1.0 pad_maximum_fusion
  62.0 2.0 %reshape.40 = bf16[96,2432]{1,0:T(8,128)(2,1)} reshape(bf16[8,2,6,2432]{3,2,1,0:T(8,128)(2,1)} %pad_maximum_fusion) | data formatting | bytes 933888 | tf_op jit(solution)/shard_map/reshape | solution.py:120
  64.0 21.7 %all-to-all-done = bf16[8,128,576]{1,2,0:T(8,128)(2,1)} async-done(((bf16[8,128,576]{1,2,0:T(8,128)(2,1)}), bf16[8,128,576]{1,2,0:T(8,128)(2,1)}, u32[]{:S(2)}, u32[]{:S(2)}) %all-to-all-start) | async-done | bytes 1179680 | tf_op jit(solution)/shard_map/all_to_all | solution.py:143
  85.8 2.4 %copy.14 = bf16[8,128,576]{2,1,0:T(8,128)(2,1)} copy(bf16[8,128,576]{1,2,0:T(8,128)(2,1)} %all-to-all-done) | data formatting | bytes 2359296 | tf_op jit(solution)/shard_map/all_to_all | solution.py:143
  88.2 0.0 all-gather.5.cloned.1.call-update
  88.2 0.1 collective-permute-start.2
  88.3 3.2 %collective-permute-start.3 = (bf16[128,2432]{1,0:T(8,128)(2,1)}, bf16[128,2432]{1,0:T(8,128)(2,1)S(1)}, u32[]{:S(2)}, u32[]{:S(2)}) collective-permute-start(bf16[128,2432]{1,0:T(8,128)(2,1)} %collective-permute-done.1.refs_2_), channel_id=1, source_target_pairs={{0,14},{2,0},{4,2},{6,4},{8,6},{10,8},{12,10},{14,12},{1,15},{3,1}... | collective-permute-start | bytes 1867784 | tf_op jit(solution)/shard_map/ppermute | solution.py:127
  91.5 2.9 %fusion.3 = f32[2,2,256,192]{3,2,1,0:T(8,128)S(1)} fusion(bf16[2,2048,192]{1,2,0:T(8,128)(2,1)S(1)} %copy-done, bf16[2,256,2048]{2,1,0:T(8,128)(2,1)} %all-gather.3.cloned.1.call-done), kind=kOutput, calls=%fused_computation.5 | convolution fusion | flops 805306368 | bytes 4456448 | tf_op jit(solution)/shard_map/ntf,cfa->ncta/dot_general | solution.py:153
  94.4 0.1 fusion.12
  94.4 3.4 %collective-permute-start.5 = (bf16[2,256,192]{2,1,0:T(8,128)(2,1)S(1)}, bf16[2,256,192]{2,1,0:T(8,128)(2,1)S(1)}, u32[]{:S(2)}, u32[]{:S(2)}) collective-permute-start(bf16[2,256,192]{2,1,0:T(8,128)(2,1)S(1)} %fusion.12), channel_id=1, source_target_pairs={{0,1},{1,0},{2,3},{3,2},{4,5},{5,4},{6,7},{7,6},{8,9},{9,8},{10,11... | collective-permute-start | bytes 589832 | tf_op jit(solution)/shard_map/ppermute | solution.py:158
  97.9 4.9 %collective-permute-done.2.refs_3_ = bf16[128,2432]{1,0:T(8,128)(2,1)S(1)} collective-permute-done((bf16[128,2432]{1,0:T(8,128)(2,1)S(1)}, bf16[128,2432]{1,0:T(8,128)(2,1)S(1)}, u32[]{:S(2)}, u32[]{:S(2)}) %collective-permute-start.2) | collective-permute-done | bytes 622624 | tf_op jit(solution)/shard_map/ppermute | solution.py:127
  102.8 0.0 collective-permute-done.5.got_ref
  102.8 0.1 collective-permute-start.6
  102.9 3.3 %collective-permute-start.7 = (bf16[128,2432]{1,0:T(8,128)(2,1)S(1)}, bf16[128,2432]{1,0:T(8,128)(2,1)}, u32[]{:S(2)}, u32[]{:S(2)}) collective-permute-start(bf16[128,2432]{1,0:T(8,128)(2,1)S(1)} %collective-permute-done.3.refs_4_), channel_id=1, source_target_pairs={{0,14},{2,0},{4,2},{6,4},{8,6},{10,8},{12,10},{14,12},{1,15},{3,1}... | collective-permute-start | bytes 1867784 | tf_op jit(solution)/shard_map/ppermute | solution.py:127
  106.9 0.1 select_bitcast_fusion.mine_ref
  107.0 6.8 %shard_map.103.attn_ref = bf16[1024,192]{1,0:T(8,128)(2,1)S(1)} custom-call(s32[1]{0:T(128)S(6)} %copy.20.length_ref, bf16[1024,576]{1,0:T(8,128)(2,1)S(1)} %bitcast.45, f32[2,256,192]{2,1,0:T(8,128)S(1)} %select_bitcast_fusion.mine_ref, bf16[2,256,192]{2,1,0:T(8,128)(2,1)S(1)} %collective-permute-done.5.got_ref), custom_call_target="tpu_custom_call" | custom-call | flops 1006632960 | bytes 2359296 | tf_op jit(solution)/shard_map/pallas_call | solution.py:51
  113.8 2.7 %collective-permute-done.6.refs_5_ = bf16[128,2432]{1,0:T(8,128)(2,1)S(1)} collective-permute-done((bf16[128,2432]{1,0:T(8,128)(2,1)S(1)}, bf16[128,2432]{1,0:T(8,128)(2,1)S(1)}, u32[]{:S(2)}, u32[]{:S(2)}) %collective-permute-start.6) | collective-permute-done | bytes 622624 | tf_op jit(solution)/shard_map/ppermute | solution.py:127
  116.6 0.9 copy.17
  117.5 4.4 %all-to-all-start.2 = ((bf16[8,128,192]{1,2,0:T(8,128)(2,1)}), bf16[8,128,192]{1,2,0:T(8,128)(2,1)}, u32[]{:S(2)}, u32[]{:S(2)}) async-start(bf16[8,128,192]{1,2,0:T(8,128)(2,1)} %copy.17), calls=%async_computation.2 | async-start | bytes 786432 | tf_op jit(solution)/shard_map/all_to_all | solution.py:171
  121.9 0.7 slice.16
  122.7 2.0 %collective-permute-start.8 = (bf16[64,2432]{1,0:T(8,128)(2,1)}, bf16[64,2432]{1,0:T(8,128)(2,1)}, u32[]{:S(2)}, u32[]{:S(2)}) collective-permute-start(bf16[64,2432]{1,0:T(8,128)(2,1)} %slice.16), channel_id=1, source_target_pairs={{0,2},{2,4},{4,6},{6,8},{8,10},{10,12},{12,14},{14,0},{1,3},{3,5},... | collective-permute-start | bytes 933896 | tf_op jit(solution)/shard_map/ppermute | solution.py:127
  124.7 1.7 slice.17
  126.5 1.2 collective-permute-start.9
  127.7 1.1 copy-done.3
  128.7 1.1 copy-done.5
  129.8 1.1 copy-done.7
  130.9 3.2 %shard_map.104.refs_2_ = f32[192,2432]{1,0:T(8,128)S(1)} custom-call(s32[1]{0:T(128)} %bitcast.18.start_ref, bf16[1024,192]{1,0:T(8,128)(2,1)S(1)} %shard_map.103.attn_ref, bf16[128,2432]{1,0:T(8,128)(2,1)S(1)} %fusion.8.refs_0_, bf16[128,2432]{1,0:T(8,128)(2,1)S(1)} %copy-done.3, bf16[128,2432]{1,0:T(8,128)(2,1)} %collective-permute-done.1.refs_2_, ...), custom_call_target="tpu_custom_call" | custom-call | flops 836763648 | bytes 4358144 | tf_op jit(solution)/shard_map/pallas_call | solution.py:89
  134.1 2.3 %collective-permute-done.8.refs_0_ = bf16[64,2432]{1,0:T(8,128)(2,1)} collective-permute-done((bf16[64,2432]{1,0:T(8,128)(2,1)}, bf16[64,2432]{1,0:T(8,128)(2,1)}, u32[]{:S(2)}, u32[]{:S(2)}) %collective-permute-start.8) | collective-permute-done | bytes 311328 | tf_op jit(solution)/shard_map/ppermute | solution.py:127
  136.4 0.0 collective-permute-done.9.refs_1_
  136.4 1.7 shard_map.105
  138.2 1.3 reshape.44
  139.5 0.0 all-to-all-done.2
  139.5 9.3 %all-to-all-start.3 = ((bf16[32,6,2432]{2,1,0:T(8,128)(2,1)}), bf16[32,6,2432]{2,1,0:T(8,128)(2,1)S(1)}, u32[]{:S(2)}, u32[]{:S(2)}) async-start(bf16[32,6,2432]{2,1,0:T(8,128)(2,1)} %reshape.44), calls=%async_computation.3 | async-start | bytes 2490368 | tf_op jit(solution)/shard_map/all_to_all | solution.py:178
  148.8 0.0 all-gather.5.cloned.1.call-done
  148.8 5.5 %fusion.9 = (f32[2432]{0:T(1024)S(1)}, bf16[1,128,2432]{2,1,0:T(8,128)(2,1)}) fusion(bf16[1,128,2432]{2,1,0:T(8,128)(2,1)S(1)} %copy-done.8, f32[2432]{0:T(1024)S(1)} %reduce.1, bf16[1,128,2432]{2,1,0:T(8,128)(2,1)} %param.9, bf16[128,1536]{0,1:T(8,128)(2,1)} %bitcast.16, bf16[1536,2432]{1,0:T(8,128)(2,1)} %all-gather.5.cloned.1.call-done), kind=kOutput, calls=%fused_computation.7 | convolution fusion | flops 958477952 | bytes 9751552 | tf_op jit(solution)/shard_map/dot_general | solution.py:179
  154.3 1.6 collective-permute-start.10
  155.9 2.1 %collective-permute-done.10 = f32[1,2432]{1,0:T(1,128)S(1)} collective-permute-done((f32[1,2432]{1,0:T(1,128)S(1)}, f32[1,2432]{1,0:T(1,128)S(1)}, u32[]{:S(2)}, u32[]{:S(2)}) %collective-permute-start.10) | collective-permute-done | bytes 9760 | tf_op jit(solution)/shard_map/ppermute | solution.py:184
  158.1 3.4 %collective-permute-start.11 = (f32[1,2432]{1,0:T(1,128)S(1)}, f32[1,2432]{1,0:T(1,128)S(1)}, u32[]{:S(2)}, u32[]{:S(2)}) collective-permute-start(f32[1,2432]{1,0:T(1,128)S(1)} %reshape_add_fusion), channel_id=1, source_target_pairs={{0,4},{2,6},{4,0},{6,2},{8,12},{10,14},{12,8},{14,10},{1,5},{3,7},... | collective-permute-start | bytes 29192 | tf_op jit(solution)/shard_map/ppermute | solution.py:184
  161.4 1.7 collective-permute-done.11
  163.1 5.1 %collective-permute-start.12 = (f32[1,2432]{1,0:T(1,128)S(1)}, f32[1,2432]{1,0:T(1,128)S(1)}, u32[]{:S(2)}, u32[]{:S(2)}) collective-permute-start(f32[1,2432]{1,0:T(1,128)S(1)} %add.14), channel_id=1, source_target_pairs={{0,8},{2,10},{4,12},{6,14},{8,0},{10,2},{12,4},{14,6},{1,9},{3,11}... | collective-permute-start | bytes 29192 | tf_op jit(solution)/shard_map/ppermute | solution.py:184
  168.2 2.5 %collective-permute-done.12 = f32[1,2432]{1,0:T(1,128)S(1)} collective-permute-done((f32[1,2432]{1,0:T(1,128)S(1)}, f32[1,2432]{1,0:T(1,128)S(1)}, u32[]{:S(2)}, u32[]{:S(2)}) %collective-permute-start.12) | collective-permute-done | bytes 9760 | tf_op jit(solution)/shard_map/ppermute | solution.py:184
  170.8 0.6 add.15
  171.4 0.3 reduce_sum.22
  171.6 6.8 %collective-permute-start.13 = (bf16[6,2432]{1,0:T(8,128)(2,1)S(1)}, bf16[6,2432]{1,0:T(8,128)(2,1)S(1)}, u32[]{:S(2)}, u32[]{:S(2)}) collective-permute-start(bf16[6,2432]{1,0:T(8,128)(2,1)S(1)} %reduce_sum.22), channel_id=1, source_target_pairs={{0,0},{1,1},{2,32},{3,33},{4,64},{5,65},{6,96},{7,97},{8,128},{9,1... | collective-permute-start | bytes 87560 | tf_op jit(solution)/shard_map/ppermute | solution.py:194
  178.4 4.0 %collective-permute-done.13 = bf16[6,2432]{1,0:T(8,128)(2,1)S(1)} collective-permute-done((bf16[6,2432]{1,0:T(8,128)(2,1)S(1)}, bf16[6,2432]{1,0:T(8,128)(2,1)S(1)}, u32[]{:S(2)}, u32[]{:S(2)}) %collective-permute-start.13) | collective-permute-done | bytes 29216 | tf_op jit(solution)/shard_map/ppermute | solution.py:194
  182.5 0.6 convert_element_type.37
  (23 shorter events, 0.1 us)
Async XLA Ops:
  7.2 84.4 %copy-start = (bf16[2,2048,192]{1,2,0:T(8,128)(2,1)S(1)}, bf16[2,2048,192]{1,2,0:T(8,128)(2,1)}, u32[]{:S(2)}) copy-start(bf16[2,2048,192]{1,2,0:T(8,128)(2,1)} %param.13) | copy-start | bytes 4718596
  7.2 8.7 %copy-start.9 = (bf16[6,2432]{1,0:T(8,128)(2,1)S(1)}, bf16[6,2432]{1,0:T(8,128)(2,1)}, u32[]{:S(2)}) copy-start(bf16[6,2432]{1,0:T(8,128)(2,1)} %param.14) | copy-start | bytes 87556
  7.2 81.0 %all-gather.3.cloned.1.call-start = ((), (), s32[]{:S(2)}) async-start(), calls=%async_computation.4 | async-start | bytes 2359296 | tf_op jit(solution)/shard_map/all_gather | solution.py:141
  9.8 24.7 %collective-permute-start = (bf16[128,2432]{1,0:T(8,128)(2,1)S(1)}, bf16[128,2432]{1,0:T(8,128)(2,1)S(1)}, u32[]{:S(2)}, u32[]{:S(2)}) collective-permute-start(bf16[128,2432]{1,0:T(8,128)(2,1)S(1)} %fusion.8.refs_0_), channel_id=1, source_target_pairs={{0,2},{2,4},{4,6},{6,8},{8,10},{10,12},{12,14},{14,0},{1,3},{3,5},... | collective-permute-start | bytes 1867784 | tf_op jit(solution)/shard_map/ppermute | solution.py:127
  11.8 28.0 %collective-permute-start.1 = (bf16[128,2432]{1,0:T(8,128)(2,1)S(1)}, bf16[128,2432]{1,0:T(8,128)(2,1)}, u32[]{:S(2)}, u32[]{:S(2)}) collective-permute-start(bf16[128,2432]{1,0:T(8,128)(2,1)S(1)} %fusion.8.refs_0_), channel_id=1, source_target_pairs={{0,14},{2,0},{4,2},{6,4},{8,6},{10,8},{12,10},{14,12},{1,15},{3,1}... | collective-permute-start | bytes 1867784 | tf_op jit(solution)/shard_map/ppermute | solution.py:127
  16.6 28.1 %all-to-all-start.1 = ((bf16[8,6,2432]{2,1,0:T(8,128)(2,1)}), bf16[8,6,2432]{2,1,0:T(8,128)(2,1)S(1)}, u32[]{:S(2)}, u32[]{:S(2)}) async-start(bf16[8,6,2432]{2,1,0:T(8,128)(2,1)} %broadcast_in_dim.12), calls=%async_computation.1 | async-start | bytes 622592 | tf_op jit(solution)/shard_map/all_to_all | solution.py:114
  34.5 53.7 %copy-start.2 = (bf16[128,2432]{1,0:T(8,128)(2,1)}, bf16[128,2432]{1,0:T(8,128)(2,1)S(1)}, u32[]{:S(2)}) copy-start(bf16[128,2432]{1,0:T(8,128)(2,1)S(1)} %collective-permute-done.refs_1_) | copy-start | bytes 1867780
  44.7 41.1 %all-to-all-start = ((bf16[8,128,576]{1,2,0:T(8,128)(2,1)}), bf16[8,128,576]{1,2,0:T(8,128)(2,1)}, u32[]{:S(2)}, u32[]{:S(2)}) async-start(bf16[8,128,576]{1,2,0:T(8,128)(2,1)} %bitcast.46), calls=%async_computation | async-start | bytes 2359296 | tf_op jit(solution)/shard_map/all_to_all | solution.py:143
  51.3 97.4 %all-gather.5.cloned.1.call-start = ((), (), s32[]{:S(2)}) async-start(), calls=%async_computation.5 | async-start | bytes 7938048 | tf_op jit(solution)/shard_map/all_gather | solution.py:151
  51.4 8.6 %collective-permute-start.4 = (bf16[8,6,2432]{2,1,0:T(8,128)(2,1)S(1)}, bf16[8,6,2432]{2,1,0:T(8,128)(2,1)}, u32[]{:S(2)}, u32[]{:S(2)}) collective-permute-start(bf16[8,6,2432]{2,1,0:T(8,128)(2,1)S(1)} %all-to-all-done.1), channel_id=1, source_target_pairs={{0,1},{1,0},{2,3},{3,2},{4,5},{5,4},{6,7},{7,6},{8,9},{9,8},{10,11... | collective-permute-start | bytes 700424 | tf_op jit(solution)/shard_map/ppermute | solution.py:117
  88.2 14.6 %collective-permute-start.2 = (bf16[128,2432]{1,0:T(8,128)(2,1)S(1)}, bf16[128,2432]{1,0:T(8,128)(2,1)S(1)}, u32[]{:S(2)}, u32[]{:S(2)}) collective-permute-start(bf16[128,2432]{1,0:T(8,128)(2,1)S(1)} %collective-permute-done.refs_1_), channel_id=1, source_target_pairs={{0,2},{2,4},{4,6},{6,8},{8,10},{10,12},{12,14},{14,0},{1,3},{3,5},... | collective-permute-start | bytes 1867784 | tf_op jit(solution)/shard_map/ppermute | solution.py:127
  88.3 14.5 %collective-permute-start.3 = (bf16[128,2432]{1,0:T(8,128)(2,1)}, bf16[128,2432]{1,0:T(8,128)(2,1)S(1)}, u32[]{:S(2)}, u32[]{:S(2)}) collective-permute-start(bf16[128,2432]{1,0:T(8,128)(2,1)} %collective-permute-done.1.refs_2_), channel_id=1, source_target_pairs={{0,14},{2,0},{4,2},{6,4},{8,6},{10,8},{12,10},{14,12},{1,15},{3,1}... | collective-permute-start | bytes 1867784 | tf_op jit(solution)/shard_map/ppermute | solution.py:127
  94.4 12.6 %copy-start.1 = (bf16[8,128,576]{2,1,0:T(8,128)(2,1)S(1)}, bf16[8,128,576]{2,1,0:T(8,128)(2,1)}, u32[]{:S(2)}) copy-start(bf16[8,128,576]{2,1,0:T(8,128)(2,1)} %copy.14) | copy-start | bytes 3538948
  94.4 8.4 %collective-permute-start.5 = (bf16[2,256,192]{2,1,0:T(8,128)(2,1)S(1)}, bf16[2,256,192]{2,1,0:T(8,128)(2,1)S(1)}, u32[]{:S(2)}, u32[]{:S(2)}) collective-permute-start(bf16[2,256,192]{2,1,0:T(8,128)(2,1)S(1)} %fusion.12), channel_id=1, source_target_pairs={{0,1},{1,0},{2,3},{3,2},{4,5},{5,4},{6,7},{7,6},{8,9},{9,8},{10,11... | collective-permute-start | bytes 589832 | tf_op jit(solution)/shard_map/ppermute | solution.py:158
  102.8 11.0 %copy-start.4 = (bf16[128,2432]{1,0:T(8,128)(2,1)}, bf16[128,2432]{1,0:T(8,128)(2,1)S(1)}, u32[]{:S(2)}) copy-start(bf16[128,2432]{1,0:T(8,128)(2,1)S(1)} %collective-permute-done.2.refs_3_) | copy-start | bytes 1867780
  102.8 11.0 %copy-start.6 = (bf16[128,2432]{1,0:T(8,128)(2,1)}, bf16[128,2432]{1,0:T(8,128)(2,1)S(1)}, u32[]{:S(2)}) copy-start(bf16[128,2432]{1,0:T(8,128)(2,1)S(1)} %collective-permute-done.3.refs_4_) | copy-start | bytes 1867780
  102.8 13.7 %collective-permute-start.6 = (bf16[128,2432]{1,0:T(8,128)(2,1)S(1)}, bf16[128,2432]{1,0:T(8,128)(2,1)S(1)}, u32[]{:S(2)}, u32[]{:S(2)}) collective-permute-start(bf16[128,2432]{1,0:T(8,128)(2,1)S(1)} %collective-permute-done.2.refs_3_), channel_id=1, source_target_pairs={{0,2},{2,4},{4,6},{6,8},{8,10},{10,12},{12,14},{14,0},{1,3},{3,5},... | collective-permute-start | bytes 1867784 | tf_op jit(solution)/shard_map/ppermute | solution.py:127
  102.9 13.6 %collective-permute-start.7 = (bf16[128,2432]{1,0:T(8,128)(2,1)S(1)}, bf16[128,2432]{1,0:T(8,128)(2,1)}, u32[]{:S(2)}, u32[]{:S(2)}) collective-permute-start(bf16[128,2432]{1,0:T(8,128)(2,1)S(1)} %collective-permute-done.3.refs_4_), channel_id=1, source_target_pairs={{0,14},{2,0},{4,2},{6,4},{8,6},{10,8},{12,10},{14,12},{1,15},{3,1}... | collective-permute-start | bytes 1867784 | tf_op jit(solution)/shard_map/ppermute | solution.py:127
  117.5 22.0 %all-to-all-start.2 = ((bf16[8,128,192]{1,2,0:T(8,128)(2,1)}), bf16[8,128,192]{1,2,0:T(8,128)(2,1)}, u32[]{:S(2)}, u32[]{:S(2)}) async-start(bf16[8,128,192]{1,2,0:T(8,128)(2,1)} %copy.17), calls=%async_computation.2 | async-start | bytes 786432 | tf_op jit(solution)/shard_map/all_to_all | solution.py:171
  122.7 13.7 %collective-permute-start.8 = (bf16[64,2432]{1,0:T(8,128)(2,1)}, bf16[64,2432]{1,0:T(8,128)(2,1)}, u32[]{:S(2)}, u32[]{:S(2)}) collective-permute-start(bf16[64,2432]{1,0:T(8,128)(2,1)} %slice.16), channel_id=1, source_target_pairs={{0,2},{2,4},{4,6},{6,8},{8,10},{10,12},{12,14},{14,0},{1,3},{3,5},... | collective-permute-start | bytes 933896 | tf_op jit(solution)/shard_map/ppermute | solution.py:127
  126.5 10.0 %collective-permute-start.9 = (bf16[64,2432]{1,0:T(8,128)(2,1)}, bf16[64,2432]{1,0:T(8,128)(2,1)}, u32[]{:S(2)}, u32[]{:S(2)}) collective-permute-start(bf16[64,2432]{1,0:T(8,128)(2,1)} %slice.17), channel_id=1, source_target_pairs={{0,14},{2,0},{4,2},{6,4},{8,6},{10,8},{12,10},{14,12},{1,15},{3,1}... | collective-permute-start | bytes 933896 | tf_op jit(solution)/shard_map/ppermute | solution.py:127
  127.7 1.1 copy-start.3
  128.7 1.1 copy-start.5
  129.8 1.1 copy-start.7
  139.5 9.3 %copy-start.8 = (bf16[1,128,2432]{2,1,0:T(8,128)(2,1)S(1)}, bf16[1,128,2432]{2,1,0:T(8,128)(2,1)}, u32[]{:S(2)}) copy-start(bf16[1,128,2432]{2,1,0:T(8,128)(2,1)} %param.11) | copy-start | bytes 1867780
  139.5 31.9 %all-to-all-start.3 = ((bf16[32,6,2432]{2,1,0:T(8,128)(2,1)}), bf16[32,6,2432]{2,1,0:T(8,128)(2,1)S(1)}, u32[]{:S(2)}, u32[]{:S(2)}) async-start(bf16[32,6,2432]{2,1,0:T(8,128)(2,1)} %reshape.44), calls=%async_computation.3 | async-start | bytes 2490368 | tf_op jit(solution)/shard_map/all_to_all | solution.py:178
  154.3 3.8 %collective-permute-start.10 = (f32[1,2432]{1,0:T(1,128)S(1)}, f32[1,2432]{1,0:T(1,128)S(1)}, u32[]{:S(2)}, u32[]{:S(2)}) collective-permute-start(f32[1,2432]{1,0:T(1,128)S(1)} %broadcast_in_dim.14), channel_id=1, source_target_pairs={{0,2},{2,0},{4,6},{6,4},{8,10},{10,8},{12,14},{14,12},{1,3},{3,1},... | collective-permute-start | bytes 29192 | tf_op jit(solution)/shard_map/ppermute | solution.py:184
  158.1 5.0 %collective-permute-start.11 = (f32[1,2432]{1,0:T(1,128)S(1)}, f32[1,2432]{1,0:T(1,128)S(1)}, u32[]{:S(2)}, u32[]{:S(2)}) collective-permute-start(f32[1,2432]{1,0:T(1,128)S(1)} %reshape_add_fusion), channel_id=1, source_target_pairs={{0,4},{2,6},{4,0},{6,2},{8,12},{10,14},{12,8},{14,10},{1,5},{3,7},... | collective-permute-start | bytes 29192 | tf_op jit(solution)/shard_map/ppermute | solution.py:184
  163.1 7.7 %collective-permute-start.12 = (f32[1,2432]{1,0:T(1,128)S(1)}, f32[1,2432]{1,0:T(1,128)S(1)}, u32[]{:S(2)}, u32[]{:S(2)}) collective-permute-start(f32[1,2432]{1,0:T(1,128)S(1)} %add.14), channel_id=1, source_target_pairs={{0,8},{2,10},{4,12},{6,14},{8,0},{10,2},{12,4},{14,6},{1,9},{3,11}... | collective-permute-start | bytes 29192 | tf_op jit(solution)/shard_map/ppermute | solution.py:184
  171.6 10.9 %collective-permute-start.13 = (bf16[6,2432]{1,0:T(8,128)(2,1)S(1)}, bf16[6,2432]{1,0:T(8,128)(2,1)S(1)}, u32[]{:S(2)}, u32[]{:S(2)}) collective-permute-start(bf16[6,2432]{1,0:T(8,128)(2,1)S(1)} %reduce_sum.22), channel_id=1, source_target_pairs={{0,0},{1,1},{2,32},{3,33},{4,64},{5,65},{6,96},{7,97},{8,128},{9,1... | collective-permute-start | bytes 87560 | tf_op jit(solution)/shard_map/ppermute | solution.py:194
Sparse Core Ops, SparseCore 0:
  9.8 64.3 all-gather.2
  88.3 49.9 all-gather.4

commit v4 on v3

--- a/solution.py
+++ b/solution.py
@@ -181,9 +181,10 @@
     d_gate = jnp.sum(cot_float * proj, axis=0, keepdims=True)
     bit = 1
     while bit < n_seq:
+        if 2 * bit == n_seq:
+            pieces, d_gate = lax.optimization_barrier((pieces, d_gate))
         d_gate = d_gate + lax.ppermute(d_gate, "seq", [(i, i ^ bit) for i in range(n_seq)])
         bit *= 2
-    pieces, d_gate = lax.optimization_barrier((pieces, d_gate))
     block = jnp.sum(pieces.astype(jnp.float32), axis=0).astype(jnp.bfloat16)
     perm = [
         ((d * n_seq + s) * n_enc + e, s * n_dp * n_enc + d * n_enc + e)

time: 192 us -> 192 us (level)
  waiting for transfers between devices: 67.9 us -> 71.6 us
  starting transfers between devices: 66 us -> 63.7 us
    ppermute x3, starting transfers between devices: 10.1 us -> 5.37 us  [per_device(): lax.ppermute(d_gate, 'seq', [(i, i ^ bit) for i in range(n_seq)])]
    ppermute x3, waiting for transfers between devices: 6.31 us -> 11.1 us  [per_device(): lax.ppermute(d_gate, 'seq', [(i, i ^ bit) for i in range(n_seq)])]
    ppermute x1, waiting for transfers between devices: 4.03 us -> 0.01 us  [per_device(): d_out_weight = lax.ppermute(block, WHOLE, perm).astype(jnp.float32)]
    all_to_all x1, waiting for transfers between devices: 0.01 us -> 3.06 us  [per_device(): lax.all_to_all(grad.reshape(n_dp * n_enc, own_rows, width), PLANE, 0, 0)]
    ppermute x1, starting transfers between devices: 6.82 us -> 9.31 us  [per_device(): d_out_weight = lax.ppermute(block, WHOLE, perm).astype(jnp.float32)]
where the time goes in v4:
time: 192 us; the launch traced here: 191 us
  waiting for transfers between devices  71.6 us (37%)
  starting transfers between devices  63.7 us (33%)
  local copies, waits for them, and re-layouts  15.6 us (8%)
  between operations  14.9 us (8%)
  Pallas kernels  11.7 us (6%)
  matrix products  8.33 us (4%)
  other arithmetic  5.57 us (3%)
    ppermute x8, waiting for transfers between devices, send(): lax.ppermute(block, 'seq', [(i, (i + towards) % n_seq) for i in range(n_s...  27.4 us
    all_to_all x1, waiting for transfers between devices, per_device(): lax.all_to_all(jnp.swapaxes(image_qkv.reshape(tok, n_seq, group), 0, 1),...  21.7 us
    ppermute x8, starting transfers between devices, send(): lax.ppermute(block, 'seq', [(i, (i + towards) % n_seq) for i in range(n_s...  16 us
    ppermute x3, waiting for transfers between devices, per_device(): lax.ppermute(d_gate, 'seq', [(i, i ^ bit) for i in range(n_seq)])  11.1 us
    ppermute x1, starting transfers between devices, per_device(): d_out_weight = lax.ppermute(block, WHOLE, perm).astype(jnp.float32)  9.31 us
    all_to_all x1, starting transfers between devices, per_device(): lax.all_to_all(grad.reshape(n_dp * n_enc, own_rows, width), PLANE, 0, 0)  9.28 us
    pallas_call x1, Pallas kernels, attend(): pl.pallas_call(attend_kernel, out_shape=jax.ShapeDtypeStruct((full, group...  6.78 us
    all_to_all x1, starting transfers between devices, per_device(): lax.all_to_all(jnp.swapaxes(image_qkv.reshape(tok, n_seq, group), 0, 1),...  6.67 us
  transfers between devices with their start and end apart: 20, of which 12 were waited for; matrix products, arithmetic and copies ran while one was open for 13% of the time, Pallas kernels for 6%

profile of v4, /device:TPU:4, one launch (start us, length us, event | category | flops | bytes accessed | tf_op | source)
XLA Modules:
  0.0 191.5 jit_solution(9045890119920689791)
XLA Ops:
  7.2 0.0 copy-start
  7.2 0.0 all-gather.3.cloned.1.call-start
  7.2 0.7 all-gather.3.cloned.1.call-update
  7.9 0.7 reduce.1
  8.7 1.2 fusion.8.refs_0_
  9.8 2.0 %collective-permute-start = (bf16[128,2432]{1,0:T(8,128)(2,1)S(1)}, bf16[128,2432]{1,0:T(8,128)(2,1)S(1)}, u32[]{:S(2)}, u32[]{:S(2)}) collective-permute-start(bf16[128,2432]{1,0:T(8,128)(2,1)S(1)} %fusion.8.refs_0_), channel_id=1, source_target_pairs={{0,2},{2,4},{4,6},{6,8},{8,10},{10,12},{12,14},{14,0},{1,3},{3,5},... | collective-permute-start | bytes 1867784 | tf_op jit(solution)/shard_map/ppermute | solution.py:127
  11.8 4.0 %collective-permute-start.1 = (bf16[128,2432]{1,0:T(8,128)(2,1)S(1)}, bf16[128,2432]{1,0:T(8,128)(2,1)}, u32[]{:S(2)}, u32[]{:S(2)}) collective-permute-start(bf16[128,2432]{1,0:T(8,128)(2,1)S(1)} %fusion.8.refs_0_), channel_id=1, source_target_pairs={{0,14},{2,0},{4,2},{6,4},{8,6},{10,8},{12,10},{14,12},{1,15},{3,1}... | collective-permute-start | bytes 1867784 | tf_op jit(solution)/shard_map/ppermute | solution.py:127
  15.9 0.7 broadcast_in_dim.12
  16.6 5.8 %all-to-all-start.1 = ((bf16[8,6,2432]{2,1,0:T(8,128)(2,1)}), bf16[8,6,2432]{2,1,0:T(8,128)(2,1)S(1)}, u32[]{:S(2)}, u32[]{:S(2)}) async-start(bf16[8,6,2432]{2,1,0:T(8,128)(2,1)} %broadcast_in_dim.12), calls=%async_computation.1 | async-start | bytes 622592 | tf_op jit(solution)/shard_map/all_to_all | solution.py:114
  22.4 12.1 %collective-permute-done.refs_1_ = bf16[128,2432]{1,0:T(8,128)(2,1)S(1)} collective-permute-done((bf16[128,2432]{1,0:T(8,128)(2,1)S(1)}, bf16[128,2432]{1,0:T(8,128)(2,1)S(1)}, u32[]{:S(2)}, u32[]{:S(2)}) %collective-permute-start) | collective-permute-done | bytes 622624 | tf_op jit(solution)/shard_map/ppermute | solution.py:127
  34.5 5.3 %collective-permute-done.1.refs_2_ = bf16[128,2432]{1,0:T(8,128)(2,1)} collective-permute-done((bf16[128,2432]{1,0:T(8,128)(2,1)S(1)}, bf16[128,2432]{1,0:T(8,128)(2,1)}, u32[]{:S(2)}, u32[]{:S(2)}) %collective-permute-start.1) | collective-permute-done | bytes 622624 | tf_op jit(solution)/shard_map/ppermute | solution.py:127
  39.8 2.4 %copy.13 = bf16[1,128,4608]{1,2,0:T(8,128)(2,1)} copy(bf16[1,128,4608]{2,1,0:T(8,128)(2,1)} %param.8) | data formatting | bytes 2359296 | tf_op jit(solution)/shard_map/optimization_barrier | solution.py:134
  42.2 2.5 %all-to-all-done.1 = bf16[8,6,2432]{2,1,0:T(8,128)(2,1)S(1)} async-done(((bf16[8,6,2432]{2,1,0:T(8,128)(2,1)}), bf16[8,6,2432]{2,1,0:T(8,128)(2,1)S(1)}, u32[]{:S(2)}, u32[]{:S(2)}) %all-to-all-start.1) | async-done | bytes 233504 | tf_op jit(solution)/shard_map/all_to_all | solution.py:114
  44.7 6.7 %all-to-all-start = ((bf16[8,128,576]{1,2,0:T(8,128)(2,1)}), bf16[8,128,576]{1,2,0:T(8,128)(2,1)}, u32[]{:S(2)}, u32[]{:S(2)}) async-start(bf16[8,128,576]{1,2,0:T(8,128)(2,1)} %bitcast.46), calls=%async_computation | async-start | bytes 2359296 | tf_op jit(solution)/shard_map/all_to_all | solution.py:143
  51.3 0.0 all-gather.5.cloned.1.call-start
  51.4 3.4 %collective-permute-start.4 = (bf16[8,6,2432]{2,1,0:T(8,128)(2,1)S(1)}, bf16[8,6,2432]{2,1,0:T(8,128)(2,1)}, u32[]{:S(2)}, u32[]{:S(2)}) collective-permute-start(bf16[8,6,2432]{2,1,0:T(8,128)(2,1)S(1)} %all-to-all-done.1), channel_id=1, source_target_pairs={{0,1},{1,0},{2,3},{3,2},{4,5},{5,4},{6,7},{7,6},{8,9},{9,8},{10,11... | collective-permute-start | bytes 700424 | tf_op jit(solution)/shard_map/ppermute | solution.py:117
  54.8 5.2 %collective-permute-done.4 = bf16[8,6,2432]{2,1,0:T(8,128)(2,1)} collective-permute-done((bf16[8,6,2432]{2,1,0:T(8,128)(2,1)S(1)}, bf16[8,6,2432]{2,1,0:T(8,128)(2,1)}, u32[]{:S(2)}, u32[]{:S(2)}) %collective-permute-start.4) | collective-permute-done | bytes 233504 | tf_op jit(solution)/shard_map/ppermute | solution.py:117
  60.0 1.0 select_bitcast_fusion.2
  61.0 1.0 pad_maximum_fusion
  62.0 2.0 %reshape.40 = bf16[96,2432]{1,0:T(8,128)(2,1)} reshape(bf16[8,2,6,2432]{3,2,1,0:T(8,128)(2,1)} %pad_maximum_fusion) | data formatting | bytes 933888 | tf_op jit(solution)/shard_map/reshape | solution.py:120
  64.0 21.7 %all-to-all-done = bf16[8,128,576]{1,2,0:T(8,128)(2,1)} async-done(((bf16[8,128,576]{1,2,0:T(8,128)(2,1)}), bf16[8,128,576]{1,2,0:T(8,128)(2,1)}, u32[]{:S(2)}, u32[]{:S(2)}) %all-to-all-start) | async-done | bytes 1179680 | tf_op jit(solution)/shard_map/all_to_all | solution.py:143
  85.8 2.4 %copy.14 = bf16[8,128,576]{2,1,0:T(8,128)(2,1)} copy(bf16[8,128,576]{1,2,0:T(8,128)(2,1)} %all-to-all-done) | data formatting | bytes 2359296 | tf_op jit(solution)/shard_map/all_to_all | solution.py:143
  88.2 0.0 all-gather.5.cloned.1.call-update
  88.2 0.1 collective-permute-start.2
  88.3 3.2 %collective-permute-start.3 = (bf16[128,2432]{1,0:T(8,128)(2,1)}, bf16[128,2432]{1,0:T(8,128)(2,1)S(1)}, u32[]{:S(2)}, u32[]{:S(2)}) collective-permute-start(bf16[128,2432]{1,0:T(8,128)(2,1)} %collective-permute-done.1.refs_2_), channel_id=1, source_target_pairs={{0,14},{2,0},{4,2},{6,4},{8,6},{10,8},{12,10},{14,12},{1,15},{3,1}... | collective-permute-start | bytes 1867784 | tf_op jit(solution)/shard_map/ppermute | solution.py:127
  91.5 2.9 %fusion.3 = f32[2,2,256,192]{3,2,1,0:T(8,128)S(1)} fusion(bf16[2,2048,192]{1,2,0:T(8,128)(2,1)S(1)} %copy-done, bf16[2,256,2048]{2,1,0:T(8,128)(2,1)} %all-gather.3.cloned.1.call-done), kind=kOutput, calls=%fused_computation.5 | convolution fusion | flops 805306368 | bytes 4456448 | tf_op jit(solution)/shard_map/ntf,cfa->ncta/dot_general | solution.py:153
  94.4 0.1 fusion.12
  94.4 3.4 %collective-permute-start.5 = (bf16[2,256,192]{2,1,0:T(8,128)(2,1)S(1)}, bf16[2,256,192]{2,1,0:T(8,128)(2,1)S(1)}, u32[]{:S(2)}, u32[]{:S(2)}) collective-permute-start(bf16[2,256,192]{2,1,0:T(8,128)(2,1)S(1)} %fusion.12), channel_id=1, source_target_pairs={{0,1},{1,0},{2,3},{3,2},{4,5},{5,4},{6,7},{7,6},{8,9},{9,8},{10,11... | collective-permute-start | bytes 589832 | tf_op jit(solution)/shard_map/ppermute | solution.py:158
  97.9 4.9 %collective-permute-done.2.refs_3_ = bf16[128,2432]{1,0:T(8,128)(2,1)S(1)} collective-permute-done((bf16[128,2432]{1,0:T(8,128)(2,1)S(1)}, bf16[128,2432]{1,0:T(8,128)(2,1)S(1)}, u32[]{:S(2)}, u32[]{:S(2)}) %collective-permute-start.2) | collective-permute-done | bytes 622624 | tf_op jit(solution)/shard_map/ppermute | solution.py:127
  102.8 0.1 collective-permute-start.6
  102.9 3.3 %collective-permute-start.7 = (bf16[128,2432]{1,0:T(8,128)(2,1)S(1)}, bf16[128,2432]{1,0:T(8,128)(2,1)}, u32[]{:S(2)}, u32[]{:S(2)}) collective-permute-start(bf16[128,2432]{1,0:T(8,128)(2,1)S(1)} %collective-permute-done.3.refs_4_), channel_id=1, source_target_pairs={{0,14},{2,0},{4,2},{6,4},{8,6},{10,8},{12,10},{14,12},{1,15},{3,1}... | collective-permute-start | bytes 1867784 | tf_op jit(solution)/shard_map/ppermute | solution.py:127
  106.9 0.1 select_bitcast_fusion.mine_ref
  107.0 6.8 %shard_map.103.attn_ref = bf16[1024,192]{1,0:T(8,128)(2,1)S(1)} custom-call(s32[1]{0:T(128)S(6)} %copy.20.length_ref, bf16[1024,576]{1,0:T(8,128)(2,1)S(1)} %bitcast.45, f32[2,256,192]{2,1,0:T(8,128)S(1)} %select_bitcast_fusion.mine_ref, bf16[2,256,192]{2,1,0:T(8,128)(2,1)S(1)} %collective-permute-done.5.got_ref), custom_call_target="tpu_custom_call" | custom-call | flops 1006632960 | bytes 2359296 | tf_op jit(solution)/shard_map/pallas_call | solution.py:51
  113.8 2.7 %collective-permute-done.6.refs_5_ = bf16[128,2432]{1,0:T(8,128)(2,1)S(1)} collective-permute-done((bf16[128,2432]{1,0:T(8,128)(2,1)S(1)}, bf16[128,2432]{1,0:T(8,128)(2,1)S(1)}, u32[]{:S(2)}, u32[]{:S(2)}) %collective-permute-start.6) | collective-permute-done | bytes 622624 | tf_op jit(solution)/shard_map/ppermute | solution.py:127
  116.6 0.0 collective-permute-done.7.refs_6_
  116.6 0.9 copy.17
  117.5 4.4 %all-to-all-start.2 = ((bf16[8,128,192]{1,2,0:T(8,128)(2,1)}), bf16[8,128,192]{1,2,0:T(8,128)(2,1)}, u32[]{:S(2)}, u32[]{:S(2)}) async-start(bf16[8,128,192]{1,2,0:T(8,128)(2,1)} %copy.17), calls=%async_computation.2 | async-start | bytes 786432 | tf_op jit(solution)/shard_map/all_to_all | solution.py:171
  121.9 0.7 slice.16
  122.7 2.0 %collective-permute-start.8 = (bf16[64,2432]{1,0:T(8,128)(2,1)}, bf16[64,2432]{1,0:T(8,128)(2,1)}, u32[]{:S(2)}, u32[]{:S(2)}) collective-permute-start(bf16[64,2432]{1,0:T(8,128)(2,1)} %slice.16), channel_id=1, source_target_pairs={{0,2},{2,4},{4,6},{6,8},{8,10},{10,12},{12,14},{14,0},{1,3},{3,5},... | collective-permute-start | bytes 933896 | tf_op jit(solution)/shard_map/ppermute | solution.py:127
  124.7 1.7 slice.17
  126.5 1.2 collective-permute-start.9
  127.7 1.1 copy-done.3
  128.7 1.1 copy-done.5
  129.8 1.1 copy-done.7
  130.9 3.2 %shard_map.104.refs_2_ = f32[192,2432]{1,0:T(8,128)S(1)} custom-call(s32[1]{0:T(128)} %bitcast.18.start_ref, bf16[1024,192]{1,0:T(8,128)(2,1)S(1)} %shard_map.103.attn_ref, bf16[128,2432]{1,0:T(8,128)(2,1)S(1)} %fusion.8.refs_0_, bf16[128,2432]{1,0:T(8,128)(2,1)S(1)} %copy-done.3, bf16[128,2432]{1,0:T(8,128)(2,1)} %collective-permute-done.1.refs_2_, ...), custom_call_target="tpu_custom_call" | custom-call | flops 836763648 | bytes 4358144 | tf_op jit(solution)/shard_map/pallas_call | solution.py:89
  134.1 2.3 %collective-permute-done.8.refs_0_ = bf16[64,2432]{1,0:T(8,128)(2,1)} collective-permute-done((bf16[64,2432]{1,0:T(8,128)(2,1)}, bf16[64,2432]{1,0:T(8,128)(2,1)}, u32[]{:S(2)}, u32[]{:S(2)}) %collective-permute-start.8) | collective-permute-done | bytes 311328 | tf_op jit(solution)/shard_map/ppermute | solution.py:127
  136.4 0.0 collective-permute-done.9.refs_1_
  136.4 1.7 shard_map.105
  138.2 1.3 reshape.44
  139.5 9.3 %all-to-all-start.3 = ((bf16[32,6,2432]{2,1,0:T(8,128)(2,1)}), bf16[32,6,2432]{2,1,0:T(8,128)(2,1)S(1)}, u32[]{:S(2)}, u32[]{:S(2)}) async-start(bf16[32,6,2432]{2,1,0:T(8,128)(2,1)} %reshape.44), calls=%async_computation.3 | async-start | bytes 2490368 | tf_op jit(solution)/shard_map/all_to_all | solution.py:178
  148.8 0.0 all-gather.5.cloned.1.call-done
  148.8 5.5 %fusion.9 = (f32[2432]{0:T(1024)S(1)}, bf16[1,128,2432]{2,1,0:T(8,128)(2,1)}) fusion(bf16[1,128,2432]{2,1,0:T(8,128)(2,1)S(1)} %copy-done.8, f32[2432]{0:T(1024)S(1)} %reduce.1, bf16[1,128,2432]{2,1,0:T(8,128)(2,1)} %param.9, bf16[128,1536]{0,1:T(8,128)(2,1)} %bitcast.16, bf16[1536,2432]{1,0:T(8,128)(2,1)} %all-gather.5.cloned.1.call-done), kind=kOutput, calls=%fused_computation.7 | convolution fusion | flops 958477952 | bytes 9751552 | tf_op jit(solution)/shard_map/dot_general | solution.py:179
  154.3 1.6 collective-permute-start.10
  155.9 2.1 %collective-permute-done.10 = f32[1,2432]{1,0:T(1,128)S(1)} collective-permute-done((f32[1,2432]{1,0:T(1,128)S(1)}, f32[1,2432]{1,0:T(1,128)S(1)}, u32[]{:S(2)}, u32[]{:S(2)}) %collective-permute-start.10) | collective-permute-done | bytes 9760 | tf_op jit(solution)/shard_map/ppermute | solution.py:186
  158.1 3.4 %collective-permute-start.11 = (f32[1,2432]{1,0:T(1,128)S(1)}, f32[1,2432]{1,0:T(1,128)S(1)}, u32[]{:S(2)}, u32[]{:S(2)}) collective-permute-start(f32[1,2432]{1,0:T(1,128)S(1)} %reshape_add_fusion), channel_id=1, source_target_pairs={{0,4},{2,6},{4,0},{6,2},{8,12},{10,14},{12,8},{14,10},{1,5},{3,7},... | collective-permute-start | bytes 29192 | tf_op jit(solution)/shard_map/ppermute | solution.py:186
  161.4 1.7 collective-permute-done.11
  163.1 3.1 %all-to-all-done.3 = bf16[32,6,2432]{2,1,0:T(8,128)(2,1)S(1)} async-done(((bf16[32,6,2432]{2,1,0:T(8,128)(2,1)}), bf16[32,6,2432]{2,1,0:T(8,128)(2,1)S(1)}, u32[]{:S(2)}, u32[]{:S(2)}) %all-to-all-start.3) | async-done | bytes 933920 | tf_op jit(solution)/shard_map/all_to_all | solution.py:178
  166.2 0.3 reduce_sum.22
  166.4 9.3 %collective-permute-start.13 = (bf16[6,2432]{1,0:T(8,128)(2,1)S(1)}, bf16[6,2432]{1,0:T(8,128)(2,1)S(1)}, u32[]{:S(2)}, u32[]{:S(2)}) collective-permute-start(bf16[6,2432]{1,0:T(8,128)(2,1)S(1)} %reduce_sum.22), channel_id=1, source_target_pairs={{0,0},{1,1},{2,32},{3,33},{4,64},{5,65},{6,96},{7,97},{8,128},{9,1... | collective-permute-start | bytes 87560 | tf_op jit(solution)/shard_map/ppermute | solution.py:195
  175.7 0.4 collective-permute-start.12
  176.1 7.3 %collective-permute-done.12 = f32[1,2432]{1,0:T(1,128)S(1)} collective-permute-done((f32[1,2432]{1,0:T(1,128)S(1)}, f32[1,2432]{1,0:T(1,128)S(1)}, u32[]{:S(2)}, u32[]{:S(2)}) %collective-permute-start.12) | collective-permute-done | bytes 9760 | tf_op jit(solution)/shard_map/ppermute | solution.py:186
  183.4 0.6 add.15
  184.0 0.0 collective-permute-done.13
  184.0 0.6 convert_element_type.37
  (23 shorter events, 0.1 us)
Async XLA Ops:
  7.2 84.4 %copy-start = (bf16[2,2048,192]{1,2,0:T(8,128)(2,1)S(1)}, bf16[2,2048,192]{1,2,0:T(8,128)(2,1)}, u32[]{:S(2)}) copy-start(bf16[2,2048,192]{1,2,0:T(8,128)(2,1)} %param.13) | copy-start | bytes 4718596
  7.2 8.7 %copy-start.9 = (bf16[6,2432]{1,0:T(8,128)(2,1)S(1)}, bf16[6,2432]{1,0:T(8,128)(2,1)}, u32[]{:S(2)}) copy-start(bf16[6,2432]{1,0:T(8,128)(2,1)} %param.14) | copy-start | bytes 87556
  7.2 81.0 %all-gather.3.cloned.1.call-start = ((), (), s32[]{:S(2)}) async-start(), calls=%async_computation.4 | async-start | bytes 2359296 | tf_op jit(solution)/shard_map/all_gather | solution.py:141
  9.8 24.7 %collective-permute-start = (bf16[128,2432]{1,0:T(8,128)(2,1)S(1)}, bf16[128,2432]{1,0:T(8,128)(2,1)S(1)}, u32[]{:S(2)}, u32[]{:S(2)}) collective-permute-start(bf16[128,2432]{1,0:T(8,128)(2,1)S(1)} %fusion.8.refs_0_), channel_id=1, source_target_pairs={{0,2},{2,4},{4,6},{6,8},{8,10},{10,12},{12,14},{14,0},{1,3},{3,5},... | collective-permute-start | bytes 1867784 | tf_op jit(solution)/shard_map/ppermute | solution.py:127
  11.8 28.0 %collective-permute-start.1 = (bf16[128,2432]{1,0:T(8,128)(2,1)S(1)}, bf16[128,2432]{1,0:T(8,128)(2,1)}, u32[]{:S(2)}, u32[]{:S(2)}) collective-permute-start(bf16[128,2432]{1,0:T(8,128)(2,1)S(1)} %fusion.8.refs_0_), channel_id=1, source_target_pairs={{0,14},{2,0},{4,2},{6,4},{8,6},{10,8},{12,10},{14,12},{1,15},{3,1}... | collective-permute-start | bytes 1867784 | tf_op jit(solution)/shard_map/ppermute | solution.py:127
  16.6 28.1 %all-to-all-start.1 = ((bf16[8,6,2432]{2,1,0:T(8,128)(2,1)}), bf16[8,6,2432]{2,1,0:T(8,128)(2,1)S(1)}, u32[]{:S(2)}, u32[]{:S(2)}) async-start(bf16[8,6,2432]{2,1,0:T(8,128)(2,1)} %broadcast_in_dim.12), calls=%async_computation.1 | async-start | bytes 622592 | tf_op jit(solution)/shard_map/all_to_all | solution.py:114
  34.5 53.7 %copy-start.2 = (bf16[128,2432]{1,0:T(8,128)(2,1)}, bf16[128,2432]{1,0:T(8,128)(2,1)S(1)}, u32[]{:S(2)}) copy-start(bf16[128,2432]{1,0:T(8,128)(2,1)S(1)} %collective-permute-done.refs_1_) | copy-start | bytes 1867780
  44.7 41.1 %all-to-all-start = ((bf16[8,128,576]{1,2,0:T(8,128)(2,1)}), bf16[8,128,576]{1,2,0:T(8,128)(2,1)}, u32[]{:S(2)}, u32[]{:S(2)}) async-start(bf16[8,128,576]{1,2,0:T(8,128)(2,1)} %bitcast.46), calls=%async_computation | async-start | bytes 2359296 | tf_op jit(solution)/shard_map/all_to_all | solution.py:143
  51.3 97.4 %all-gather.5.cloned.1.call-start = ((), (), s32[]{:S(2)}) async-start(), calls=%async_computation.5 | async-start | bytes 7938048 | tf_op jit(solution)/shard_map/all_gather | solution.py:151
  51.4 8.6 %collective-permute-start.4 = (bf16[8,6,2432]{2,1,0:T(8,128)(2,1)S(1)}, bf16[8,6,2432]{2,1,0:T(8,128)(2,1)}, u32[]{:S(2)}, u32[]{:S(2)}) collective-permute-start(bf16[8,6,2432]{2,1,0:T(8,128)(2,1)S(1)} %all-to-all-done.1), channel_id=1, source_target_pairs={{0,1},{1,0},{2,3},{3,2},{4,5},{5,4},{6,7},{7,6},{8,9},{9,8},{10,11... | collective-permute-start | bytes 700424 | tf_op jit(solution)/shard_map/ppermute | solution.py:117
  88.2 14.6 %collective-permute-start.2 = (bf16[128,2432]{1,0:T(8,128)(2,1)S(1)}, bf16[128,2432]{1,0:T(8,128)(2,1)S(1)}, u32[]{:S(2)}, u32[]{:S(2)}) collective-permute-start(bf16[128,2432]{1,0:T(8,128)(2,1)S(1)} %collective-permute-done.refs_1_), channel_id=1, source_target_pairs={{0,2},{2,4},{4,6},{6,8},{8,10},{10,12},{12,14},{14,0},{1,3},{3,5},... | collective-permute-start | bytes 1867784 | tf_op jit(solution)/shard_map/ppermute | solution.py:127
  88.3 14.5 %collective-permute-start.3 = (bf16[128,2432]{1,0:T(8,128)(2,1)}, bf16[128,2432]{1,0:T(8,128)(2,1)S(1)}, u32[]{:S(2)}, u32[]{:S(2)}) collective-permute-start(bf16[128,2432]{1,0:T(8,128)(2,1)} %collective-permute-done.1.refs_2_), channel_id=1, source_target_pairs={{0,14},{2,0},{4,2},{6,4},{8,6},{10,8},{12,10},{14,12},{1,15},{3,1}... | collective-permute-start | bytes 1867784 | tf_op jit(solution)/shard_map/ppermute | solution.py:127
  94.4 12.6 %copy-start.1 = (bf16[8,128,576]{2,1,0:T(8,128)(2,1)S(1)}, bf16[8,128,576]{2,1,0:T(8,128)(2,1)}, u32[]{:S(2)}) copy-start(bf16[8,128,576]{2,1,0:T(8,128)(2,1)} %copy.14) | copy-start | bytes 3538948
  94.4 8.4 %collective-permute-start.5 = (bf16[2,256,192]{2,1,0:T(8,128)(2,1)S(1)}, bf16[2,256,192]{2,1,0:T(8,128)(2,1)S(1)}, u32[]{:S(2)}, u32[]{:S(2)}) collective-permute-start(bf16[2,256,192]{2,1,0:T(8,128)(2,1)S(1)} %fusion.12), channel_id=1, source_target_pairs={{0,1},{1,0},{2,3},{3,2},{4,5},{5,4},{6,7},{7,6},{8,9},{9,8},{10,11... | collective-permute-start | bytes 589832 | tf_op jit(solution)/shard_map/ppermute | solution.py:158
  102.8 11.0 %copy-start.4 = (bf16[128,2432]{1,0:T(8,128)(2,1)}, bf16[128,2432]{1,0:T(8,128)(2,1)S(1)}, u32[]{:S(2)}) copy-start(bf16[128,2432]{1,0:T(8,128)(2,1)S(1)} %collective-permute-done.2.refs_3_) | copy-start | bytes 1867780
  102.8 11.0 %copy-start.6 = (bf16[128,2432]{1,0:T(8,128)(2,1)}, bf16[128,2432]{1,0:T(8,128)(2,1)S(1)}, u32[]{:S(2)}) copy-start(bf16[128,2432]{1,0:T(8,128)(2,1)S(1)} %collective-permute-done.3.refs_4_) | copy-start | bytes 1867780
  102.8 13.7 %collective-permute-start.6 = (bf16[128,2432]{1,0:T(8,128)(2,1)S(1)}, bf16[128,2432]{1,0:T(8,128)(2,1)S(1)}, u32[]{:S(2)}, u32[]{:S(2)}) collective-permute-start(bf16[128,2432]{1,0:T(8,128)(2,1)S(1)} %collective-permute-done.2.refs_3_), channel_id=1, source_target_pairs={{0,2},{2,4},{4,6},{6,8},{8,10},{10,12},{12,14},{14,0},{1,3},{3,5},... | collective-permute-start | bytes 1867784 | tf_op jit(solution)/shard_map/ppermute | solution.py:127
  102.9 13.6 %collective-permute-start.7 = (bf16[128,2432]{1,0:T(8,128)(2,1)S(1)}, bf16[128,2432]{1,0:T(8,128)(2,1)}, u32[]{:S(2)}, u32[]{:S(2)}) collective-permute-start(bf16[128,2432]{1,0:T(8,128)(2,1)S(1)} %collective-permute-done.3.refs_4_), channel_id=1, source_target_pairs={{0,14},{2,0},{4,2},{6,4},{8,6},{10,8},{12,10},{14,12},{1,15},{3,1}... | collective-permute-start | bytes 1867784 | tf_op jit(solution)/shard_map/ppermute | solution.py:127
  117.5 22.0 %all-to-all-start.2 = ((bf16[8,128,192]{1,2,0:T(8,128)(2,1)}), bf16[8,128,192]{1,2,0:T(8,128)(2,1)}, u32[]{:S(2)}, u32[]{:S(2)}) async-start(bf16[8,128,192]{1,2,0:T(8,128)(2,1)} %copy.17), calls=%async_computation.2 | async-start | bytes 786432 | tf_op jit(solution)/shard_map/all_to_all | solution.py:171
  122.7 13.7 %collective-permute-start.8 = (bf16[64,2432]{1,0:T(8,128)(2,1)}, bf16[64,2432]{1,0:T(8,128)(2,1)}, u32[]{:S(2)}, u32[]{:S(2)}) collective-permute-start(bf16[64,2432]{1,0:T(8,128)(2,1)} %slice.16), channel_id=1, source_target_pairs={{0,2},{2,4},{4,6},{6,8},{8,10},{10,12},{12,14},{14,0},{1,3},{3,5},... | collective-permute-start | bytes 933896 | tf_op jit(solution)/shard_map/ppermute | solution.py:127
  126.5 10.0 %collective-permute-start.9 = (bf16[64,2432]{1,0:T(8,128)(2,1)}, bf16[64,2432]{1,0:T(8,128)(2,1)}, u32[]{:S(2)}, u32[]{:S(2)}) collective-permute-start(bf16[64,2432]{1,0:T(8,128)(2,1)} %slice.17), channel_id=1, source_target_pairs={{0,14},{2,0},{4,2},{6,4},{8,6},{10,8},{12,10},{14,12},{1,15},{3,1}... | collective-permute-start | bytes 933896 | tf_op jit(solution)/shard_map/ppermute | solution.py:127
  127.7 1.1 copy-start.3
  128.7 1.1 copy-start.5
  129.8 1.1 copy-start.7
  139.5 9.3 %copy-start.8 = (bf16[1,128,2432]{2,1,0:T(8,128)(2,1)S(1)}, bf16[1,128,2432]{2,1,0:T(8,128)(2,1)}, u32[]{:S(2)}) copy-start(bf16[1,128,2432]{2,1,0:T(8,128)(2,1)} %param.11) | copy-start | bytes 1867780
  139.5 26.7 %all-to-all-start.3 = ((bf16[32,6,2432]{2,1,0:T(8,128)(2,1)}), bf16[32,6,2432]{2,1,0:T(8,128)(2,1)S(1)}, u32[]{:S(2)}, u32[]{:S(2)}) async-start(bf16[32,6,2432]{2,1,0:T(8,128)(2,1)} %reshape.44), calls=%async_computation.3 | async-start | bytes 2490368 | tf_op jit(solution)/shard_map/all_to_all | solution.py:178
  154.3 3.8 %collective-permute-start.10 = (f32[1,2432]{1,0:T(1,128)S(1)}, f32[1,2432]{1,0:T(1,128)S(1)}, u32[]{:S(2)}, u32[]{:S(2)}) collective-permute-start(f32[1,2432]{1,0:T(1,128)S(1)} %broadcast_in_dim.14), channel_id=1, source_target_pairs={{0,2},{2,0},{4,6},{6,4},{8,10},{10,8},{12,14},{14,12},{1,3},{3,1},... | collective-permute-start | bytes 29192 | tf_op jit(solution)/shard_map/ppermute | solution.py:186
  158.1 5.0 %collective-permute-start.11 = (f32[1,2432]{1,0:T(1,128)S(1)}, f32[1,2432]{1,0:T(1,128)S(1)}, u32[]{:S(2)}, u32[]{:S(2)}) collective-permute-start(f32[1,2432]{1,0:T(1,128)S(1)} %reshape_add_fusion), channel_id=1, source_target_pairs={{0,4},{2,6},{4,0},{6,2},{8,12},{10,14},{12,8},{14,10},{1,5},{3,7},... | collective-permute-start | bytes 29192 | tf_op jit(solution)/shard_map/ppermute | solution.py:186
  166.4 17.6 %collective-permute-start.13 = (bf16[6,2432]{1,0:T(8,128)(2,1)S(1)}, bf16[6,2432]{1,0:T(8,128)(2,1)S(1)}, u32[]{:S(2)}, u32[]{:S(2)}) collective-permute-start(bf16[6,2432]{1,0:T(8,128)(2,1)S(1)} %reduce_sum.22), channel_id=1, source_target_pairs={{0,0},{1,1},{2,32},{3,33},{4,64},{5,65},{6,96},{7,97},{8,128},{9,1... | collective-permute-start | bytes 87560 | tf_op jit(solution)/shard_map/ppermute | solution.py:195
  175.7 7.7 %collective-permute-start.12 = (f32[1,2432]{1,0:T(1,128)S(1)}, f32[1,2432]{1,0:T(1,128)S(1)}, u32[]{:S(2)}, u32[]{:S(2)}) collective-permute-start(f32[1,2432]{1,0:T(1,128)S(1)} %add.14), channel_id=1, source_target_pairs={{0,8},{2,10},{4,12},{6,14},{8,0},{10,2},{12,4},{14,6},{1,9},{3,11}... | collective-permute-start | bytes 29192 | tf_op jit(solution)/shard_map/ppermute | solution.py:186
Sparse Core Ops, SparseCore 0:
  9.8 64.3 all-gather.2
  88.3 49.9 all-gather.4

commit v5 on v4

--- a/solution.py
+++ b/solution.py
@@ -92,7 +92,7 @@
         in_specs=[pl.BlockSpec(memory_space=pltpu.SMEM)]
         + [pl.BlockSpec(memory_space=pltpu.VMEM)] * (1 + len(arrays) + len(before)),
         out_specs=pl.BlockSpec(memory_space=pltpu.VMEM),
-        compiler_params=pltpu.CompilerParams(vmem_limit_bytes=40 * 2**20),
+        compiler_params=pltpu.CompilerParams(vmem_limit_bytes=(40 if before else 58) * 2**20),
         cost_estimate=pl.CostEstimate(
             flops=2 * rows * attn.shape[1] * width,
             bytes_accessed=2 * rows * width,

time: 192 us -> 191 us (level)
  waiting for transfers between devices: 71.6 us -> 77.8 us
  local copies, waits for them, and re-layouts: 15.6 us -> 11.5 us
  starting transfers between devices: 63.7 us -> 60.5 us
    all_to_all x1, waiting for transfers between devices: 21.7 us -> 24.7 us  [per_device(): lax.all_to_all(jnp.swapaxes(image_qkv.reshape(tok, n_seq, group), 0, 1),...]
  transfers between devices with their start and end apart: 20 -> 20, of which waited for: 12 -> 12; matrix products, arithmetic and copies ran while one was open for 13% -> 11% of each run, Pallas kernels for 6% -> 7%
where the time goes in v5:
time: 191 us; the launch traced here: 190 us
  waiting for transfers between devices  77.8 us (41%)
  starting transfers between devices  60.5 us (32%)
  between operations  14.9 us (8%)
  Pallas kernels  13.1 us (7%)
  local copies, waits for them, and re-layouts  11.5 us (6%)
  matrix products  8.33 us (4%)
  other arithmetic  3.78 us (2%)
    ppermute x8, waiting for transfers between devices, send(): lax.ppermute(block, 'seq', [(i, (i + towards) % n_seq) for i in range(n_s...  29 us
    all_to_all x1, waiting for transfers between devices, per_device(): lax.all_to_all(jnp.swapaxes(image_qkv.reshape(tok, n_seq, group), 0, 1),...  24.7 us
    ppermute x8, starting transfers between devices, send(): lax.ppermute(block, 'seq', [(i, (i + towards) % n_seq) for i in range(n_s...  16.1 us
    ppermute x3, waiting for transfers between devices, per_device(): lax.ppermute(d_gate, 'seq', [(i, i ^ bit) for i in range(n_seq)])  12.3 us
    all_to_all x1, starting transfers between devices, per_device(): lax.all_to_all(grad.reshape(n_dp * n_enc, own_rows, width), PLANE, 0, 0)  8.99 us
    ppermute x1, starting transfers between devices, per_device(): d_out_weight = lax.ppermute(block, WHOLE, perm).astype(jnp.float32)  7.96 us
    pallas_call x1, Pallas kernels, attend(): pl.pallas_call(attend_kernel, out_shape=jax.ShapeDtypeStruct((full, group...  6.79 us
    all_to_all x1, starting transfers between devices, per_device(): lax.all_to_all(jnp.swapaxes(image_qkv.reshape(tok, n_seq, group), 0, 1),...  6.67 us
  transfers between devices with their start and end apart: 20, of which 12 were waited for; matrix products, arithmetic and copies ran while one was open for 11% of the time, Pallas kernels for 7%

profile of v5, /device:TPU:4, one launch (start us, length us, event | category | flops | bytes accessed | tf_op | source)
XLA Modules:
  0.0 190.0 jit_solution(5899968927495065233)
XLA Ops:
  7.2 0.0 copy-start
  7.2 0.0 all-gather.3.cloned.1.call-start
  7.2 0.7 all-gather.3.cloned.1.call-update
  7.9 0.7 reduce.1
  8.7 1.2 fusion.8.refs_0_
  9.8 0.0 copy-start.5
  9.9 2.0 %collective-permute-start = (bf16[128,2432]{1,0:T(8,128)(2,1)S(1)}, bf16[128,2432]{1,0:T(8,128)(2,1)S(1)}, u32[]{:S(2)}, u32[]{:S(2)}) collective-permute-start(bf16[128,2432]{1,0:T(8,128)(2,1)S(1)} %fusion.8.refs_0_), channel_id=1, source_target_pairs={{0,2},{2,4},{4,6},{6,8},{8,10},{10,12},{12,14},{14,0},{1,3},{3,5},... | collective-permute-start | bytes 1867784 | tf_op jit(solution)/shard_map/ppermute | solution.py:127
  11.9 4.0 %collective-permute-start.1 = (bf16[128,2432]{1,0:T(8,128)(2,1)S(1)}, bf16[128,2432]{1,0:T(8,128)(2,1)}, u32[]{:S(2)}, u32[]{:S(2)}) collective-permute-start(bf16[128,2432]{1,0:T(8,128)(2,1)S(1)} %fusion.8.refs_0_), channel_id=1, source_target_pairs={{0,14},{2,0},{4,2},{6,4},{8,6},{10,8},{12,10},{14,12},{1,15},{3,1}... | collective-permute-start | bytes 1867784 | tf_op jit(solution)/shard_map/ppermute | solution.py:127
  15.9 0.7 broadcast_in_dim.12
  16.6 5.8 %all-to-all-start.1 = ((bf16[8,6,2432]{2,1,0:T(8,128)(2,1)}), bf16[8,6,2432]{2,1,0:T(8,128)(2,1)S(1)}, u32[]{:S(2)}, u32[]{:S(2)}) async-start(bf16[8,6,2432]{2,1,0:T(8,128)(2,1)} %broadcast_in_dim.12), calls=%async_computation.1 | async-start | bytes 622592 | tf_op jit(solution)/shard_map/all_to_all | solution.py:114
  22.4 12.1 %collective-permute-done.refs_1_ = bf16[128,2432]{1,0:T(8,128)(2,1)S(1)} collective-permute-done((bf16[128,2432]{1,0:T(8,128)(2,1)S(1)}, bf16[128,2432]{1,0:T(8,128)(2,1)S(1)}, u32[]{:S(2)}, u32[]{:S(2)}) %collective-permute-start) | collective-permute-done | bytes 622624 | tf_op jit(solution)/shard_map/ppermute | solution.py:127
  34.5 5.3 %collective-permute-done.1.refs_2_ = bf16[128,2432]{1,0:T(8,128)(2,1)} collective-permute-done((bf16[128,2432]{1,0:T(8,128)(2,1)S(1)}, bf16[128,2432]{1,0:T(8,128)(2,1)}, u32[]{:S(2)}, u32[]{:S(2)}) %collective-permute-start.1) | collective-permute-done | bytes 622624 | tf_op jit(solution)/shard_map/ppermute | solution.py:127
  39.8 2.4 %copy.13 = bf16[1,128,4608]{1,2,0:T(8,128)(2,1)} copy(bf16[1,128,4608]{2,1,0:T(8,128)(2,1)} %param.8) | data formatting | bytes 2359296 | tf_op jit(solution)/shard_map/optimization_barrier | solution.py:134
  42.2 2.5 %all-to-all-done.1 = bf16[8,6,2432]{2,1,0:T(8,128)(2,1)S(1)} async-done(((bf16[8,6,2432]{2,1,0:T(8,128)(2,1)}), bf16[8,6,2432]{2,1,0:T(8,128)(2,1)S(1)}, u32[]{:S(2)}, u32[]{:S(2)}) %all-to-all-start.1) | async-done | bytes 233504 | tf_op jit(solution)/shard_map/all_to_all | solution.py:114
  44.7 6.7 %all-to-all-start = ((bf16[8,128,576]{1,2,0:T(8,128)(2,1)}), bf16[8,128,576]{1,2,0:T(8,128)(2,1)}, u32[]{:S(2)}, u32[]{:S(2)}) async-start(bf16[8,128,576]{1,2,0:T(8,128)(2,1)} %bitcast.3), calls=%async_computation | async-start | bytes 2359296 | tf_op jit(solution)/shard_map/all_to_all | solution.py:143
  51.4 0.0 all-gather.5.cloned.1.call-start
  51.4 3.4 %collective-permute-start.4 = (bf16[8,6,2432]{2,1,0:T(8,128)(2,1)S(1)}, bf16[8,6,2432]{2,1,0:T(8,128)(2,1)S(1)}, u32[]{:S(2)}, u32[]{:S(2)}) collective-permute-start(bf16[8,6,2432]{2,1,0:T(8,128)(2,1)S(1)} %all-to-all-done.1), channel_id=1, source_target_pairs={{0,1},{1,0},{2,3},{3,2},{4,5},{5,4},{6,7},{7,6},{8,9},{9,8},{10,11... | collective-permute-start | bytes 700424 | tf_op jit(solution)/shard_map/ppermute | solution.py:117
  54.8 5.1 %collective-permute-done.4 = bf16[8,6,2432]{2,1,0:T(8,128)(2,1)S(1)} collective-permute-done((bf16[8,6,2432]{2,1,0:T(8,128)(2,1)S(1)}, bf16[8,6,2432]{2,1,0:T(8,128)(2,1)S(1)}, u32[]{:S(2)}, u32[]{:S(2)}) %collective-permute-start.4) | collective-permute-done | bytes 233504 | tf_op jit(solution)/shard_map/ppermute | solution.py:117
  59.9 0.1 select_bitcast_fusion.2
  60.0 0.2 pad_maximum_fusion
  60.1 0.9 reshape.40
  61.1 24.7 %all-to-all-done = bf16[8,128,576]{1,2,0:T(8,128)(2,1)} async-done(((bf16[8,128,576]{1,2,0:T(8,128)(2,1)}), bf16[8,128,576]{1,2,0:T(8,128)(2,1)}, u32[]{:S(2)}, u32[]{:S(2)}) %all-to-all-start) | async-done | bytes 1179680 | tf_op jit(solution)/shard_map/all_to_all | solution.py:143
  85.8 1.7 copy.14
  87.5 0.0 all-gather.3.cloned.1.call-done
  87.5 0.0 all-gather.5.cloned.1.call-update
  87.5 0.1 collective-permute-start.2
  87.6 3.2 %collective-permute-start.3 = (bf16[128,2432]{1,0:T(8,128)(2,1)}, bf16[128,2432]{1,0:T(8,128)(2,1)S(1)}, u32[]{:S(2)}, u32[]{:S(2)}) collective-permute-start(bf16[128,2432]{1,0:T(8,128)(2,1)} %collective-permute-done.1.refs_2_), channel_id=1, source_target_pairs={{0,14},{2,0},{4,2},{6,4},{8,6},{10,8},{12,10},{14,12},{1,15},{3,1}... | collective-permute-start | bytes 1867784 | tf_op jit(solution)/shard_map/ppermute | solution.py:127
  90.9 2.9 %fusion.3 = f32[2,2,256,192]{3,2,1,0:T(8,128)S(1)} fusion(bf16[2,2048,192]{1,2,0:T(8,128)(2,1)S(1)} %copy-done, bf16[2,256,2048]{2,1,0:T(8,128)(2,1)} %all-gather.3.cloned.1.call-done), kind=kOutput, calls=%fused_computation.5 | convolution fusion | flops 805306368 | bytes 4456448 | tf_op jit(solution)/shard_map/ntf,cfa->ncta/dot_general | solution.py:153
  93.7 0.1 fusion.12
  93.8 3.4 %collective-permute-start.5 = (bf16[2,256,192]{2,1,0:T(8,128)(2,1)S(1)}, bf16[2,256,192]{2,1,0:T(8,128)(2,1)S(1)}, u32[]{:S(2)}, u32[]{:S(2)}) collective-permute-start(bf16[2,256,192]{2,1,0:T(8,128)(2,1)S(1)} %fusion.12), channel_id=1, source_target_pairs={{0,1},{1,0},{2,3},{3,2},{4,5},{5,4},{6,7},{7,6},{8,9},{9,8},{10,11... | collective-permute-start | bytes 589832 | tf_op jit(solution)/shard_map/ppermute | solution.py:158
  97.2 5.1 %collective-permute-done.2.refs_3_ = bf16[128,2432]{1,0:T(8,128)(2,1)S(1)} collective-permute-done((bf16[128,2432]{1,0:T(8,128)(2,1)S(1)}, bf16[128,2432]{1,0:T(8,128)(2,1)S(1)}, u32[]{:S(2)}, u32[]{:S(2)}) %collective-permute-start.2) | collective-permute-done | bytes 622624 | tf_op jit(solution)/shard_map/ppermute | solution.py:127
  102.3 0.1 collective-permute-start.6
  102.4 3.3 %collective-permute-start.7 = (bf16[128,2432]{1,0:T(8,128)(2,1)S(1)}, bf16[128,2432]{1,0:T(8,128)(2,1)}, u32[]{:S(2)}, u32[]{:S(2)}) collective-permute-start(bf16[128,2432]{1,0:T(8,128)(2,1)S(1)} %collective-permute-done.3.refs_4_), channel_id=1, source_target_pairs={{0,14},{2,0},{4,2},{6,4},{8,6},{10,8},{12,10},{14,12},{1,15},{3,1}... | collective-permute-start | bytes 1867784 | tf_op jit(solution)/shard_map/ppermute | solution.py:127
  106.4 0.1 select_bitcast_fusion.mine_ref
  106.5 6.8 %shard_map.103.attn_ref = bf16[1024,192]{1,0:T(8,128)(2,1)S(1)} custom-call(s32[1]{0:T(128)S(6)} %copy.20.length_ref, bf16[1024,576]{1,0:T(8,128)(2,1)S(1)} %bitcast.45, f32[2,256,192]{2,1,0:T(8,128)S(1)} %select_bitcast_fusion.mine_ref, bf16[2,256,192]{2,1,0:T(8,128)(2,1)S(1)} %collective-permute-done.5.got_ref), custom_call_target="tpu_custom_call" | custom-call | flops 1006632960 | bytes 2359296 | tf_op jit(solution)/shard_map/pallas_call | solution.py:51
  113.3 3.0 %collective-permute-done.6.refs_5_ = bf16[128,2432]{1,0:T(8,128)(2,1)} collective-permute-done((bf16[128,2432]{1,0:T(8,128)(2,1)S(1)}, bf16[128,2432]{1,0:T(8,128)(2,1)}, u32[]{:S(2)}, u32[]{:S(2)}) %collective-permute-start.6) | collective-permute-done | bytes 622624 | tf_op jit(solution)/shard_map/ppermute | solution.py:127
  116.3 0.0 collective-permute-done.7.refs_6_
  116.3 1.0 copy.17
  117.3 4.3 %all-to-all-start.2 = ((bf16[8,128,192]{1,2,0:T(8,128)(2,1)}), bf16[8,128,192]{1,2,0:T(8,128)(2,1)}, u32[]{:S(2)}, u32[]{:S(2)}) async-start(bf16[8,128,192]{1,2,0:T(8,128)(2,1)} %copy.17), calls=%async_computation.2 | async-start | bytes 786432 | tf_op jit(solution)/shard_map/all_to_all | solution.py:171
  121.6 1.0 slice.16
  122.6 2.1 %collective-permute-start.8 = (bf16[64,2432]{1,0:T(8,128)(2,1)S(1)}, bf16[64,2432]{1,0:T(8,128)(2,1)S(1)}, u32[]{:S(2)}, u32[]{:S(2)}) collective-permute-start(bf16[64,2432]{1,0:T(8,128)(2,1)S(1)} %slice.16), channel_id=1, source_target_pairs={{0,2},{2,4},{4,6},{6,8},{8,10},{10,12},{12,14},{14,0},{1,3},{3,5},... | collective-permute-start | bytes 933896 | tf_op jit(solution)/shard_map/ppermute | solution.py:127
  124.7 1.0 slice.17
  125.7 1.3 collective-permute-start.9
  127.0 5.6 %shard_map.104.refs_2_ = f32[192,2432]{1,0:T(8,128)} custom-call(s32[1]{0:T(128)} %bitcast.18.start_ref, bf16[1024,192]{1,0:T(8,128)(2,1)} %copy-done.2, bf16[128,2432]{1,0:T(8,128)(2,1)} %copy-done.5, bf16[128,2432]{1,0:T(8,128)(2,1)} %copy-done.6, bf16[128,2432]{1,0:T(8,128)(2,1)} %collective-permute-done.1.refs_2_, bf16[128,2432]{1,0:T(8,128)(2,1)} %copy-done.7, ...), custom_call_target="tpu_custom_call" | custom-call | flops 836763648 | bytes 4358144 | tf_op jit(solution)/shard_map/pallas_call | solution.py:89
  132.6 3.5 %collective-permute-done.8.refs_0_ = bf16[64,2432]{1,0:T(8,128)(2,1)S(1)} collective-permute-done((bf16[64,2432]{1,0:T(8,128)(2,1)S(1)}, bf16[64,2432]{1,0:T(8,128)(2,1)S(1)}, u32[]{:S(2)}, u32[]{:S(2)}) %collective-permute-start.8) | collective-permute-done | bytes 311328 | tf_op jit(solution)/shard_map/ppermute | solution.py:127
  136.1 0.0 collective-permute-done.9.refs_1_
  136.1 1.5 copy-done.1
  137.7 0.7 shard_map.105
  138.3 1.3 reshape.44
  139.6 0.0 all-to-all-done.2
  139.6 9.0 %all-to-all-start.3 = ((bf16[32,6,2432]{2,1,0:T(8,128)(2,1)}), bf16[32,6,2432]{2,1,0:T(8,128)(2,1)S(1)}, u32[]{:S(2)}, u32[]{:S(2)}) async-start(bf16[32,6,2432]{2,1,0:T(8,128)(2,1)} %reshape.44), calls=%async_computation.3 | async-start | bytes 2490368 | tf_op jit(solution)/shard_map/all_to_all | solution.py:178
  148.6 0.0 all-gather.5.cloned.1.call-done
  148.7 5.5 %fusion.9 = (f32[2432]{0:T(1024)S(1)}, bf16[1,128,2432]{2,1,0:T(8,128)(2,1)}) fusion(bf16[1,128,2432]{2,1,0:T(8,128)(2,1)S(1)} %copy-done.4, f32[2432]{0:T(1024)S(1)} %reduce.1, bf16[1,128,2432]{2,1,0:T(8,128)(2,1)} %param.9, bf16[128,1536]{0,1:T(8,128)(2,1)} %bitcast.16, bf16[1536,2432]{1,0:T(8,128)(2,1)} %all-gather.5.cloned.1.call-done), kind=kOutput, calls=%fused_computation.7 | convolution fusion | flops 958477952 | bytes 9751552 | tf_op jit(solution)/shard_map/dot_general | solution.py:179
  154.2 0.8 collective-permute-start.10
  155.0 2.9 %collective-permute-done.10 = f32[1,2432]{1,0:T(1,128)S(1)} collective-permute-done((f32[1,2432]{1,0:T(1,128)S(1)}, f32[1,2432]{1,0:T(1,128)S(1)}, u32[]{:S(2)}, u32[]{:S(2)}) %collective-permute-start.10) | collective-permute-done | bytes 9760 | tf_op jit(solution)/shard_map/ppermute | solution.py:186
  157.9 2.5 %collective-permute-start.11 = (f32[1,2432]{1,0:T(1,128)S(1)}, f32[1,2432]{1,0:T(1,128)S(1)}, u32[]{:S(2)}, u32[]{:S(2)}) collective-permute-start(f32[1,2432]{1,0:T(1,128)S(1)} %reshape_add_fusion), channel_id=1, source_target_pairs={{0,4},{2,6},{4,0},{6,2},{8,12},{10,14},{12,8},{14,10},{1,5},{3,7},... | collective-permute-start | bytes 29192 | tf_op jit(solution)/shard_map/ppermute | solution.py:186
  160.4 2.1 %collective-permute-done.11 = f32[1,2432]{1,0:T(1,128)S(1)} collective-permute-done((f32[1,2432]{1,0:T(1,128)S(1)}, f32[1,2432]{1,0:T(1,128)S(1)}, u32[]{:S(2)}, u32[]{:S(2)}) %collective-permute-start.11) | collective-permute-done | bytes 9760 | tf_op jit(solution)/shard_map/ppermute | solution.py:186
  162.6 3.4 %all-to-all-done.3 = bf16[32,6,2432]{2,1,0:T(8,128)(2,1)S(1)} async-done(((bf16[32,6,2432]{2,1,0:T(8,128)(2,1)}), bf16[32,6,2432]{2,1,0:T(8,128)(2,1)S(1)}, u32[]{:S(2)}, u32[]{:S(2)}) %all-to-all-start.3) | async-done | bytes 933920 | tf_op jit(solution)/shard_map/all_to_all | solution.py:178
  166.0 0.3 reduce_sum.22
  166.3 8.0 %collective-permute-start.13 = (bf16[6,2432]{1,0:T(8,128)(2,1)S(1)}, bf16[6,2432]{1,0:T(8,128)(2,1)S(1)}, u32[]{:S(2)}, u32[]{:S(2)}) collective-permute-start(bf16[6,2432]{1,0:T(8,128)(2,1)S(1)} %reduce_sum.22), channel_id=1, source_target_pairs={{0,0},{1,1},{2,32},{3,33},{4,64},{5,65},{6,96},{7,97},{8,128},{9,1... | collective-permute-start | bytes 87560 | tf_op jit(solution)/shard_map/ppermute | solution.py:195
  174.3 0.4 collective-permute-start.12
  174.6 7.3 %collective-permute-done.12 = f32[1,2432]{1,0:T(1,128)S(1)} collective-permute-done((f32[1,2432]{1,0:T(1,128)S(1)}, f32[1,2432]{1,0:T(1,128)S(1)}, u32[]{:S(2)}, u32[]{:S(2)}) %collective-permute-start.12) | collective-permute-done | bytes 9760 | tf_op jit(solution)/shard_map/ppermute | solution.py:186
  181.9 0.6 add.15
  182.5 0.6 convert_element_type.37
  (23 shorter events, 0.1 us)
Async XLA Ops:
  7.2 83.7 %copy-start = (bf16[2,2048,192]{1,2,0:T(8,128)(2,1)S(1)}, bf16[2,2048,192]{1,2,0:T(8,128)(2,1)}, u32[]{:S(2)}) copy-start(bf16[2,2048,192]{1,2,0:T(8,128)(2,1)} %param.13) | copy-start | bytes 4718596
  7.2 8.7 %copy-start.9 = (bf16[6,2432]{1,0:T(8,128)(2,1)S(1)}, bf16[6,2432]{1,0:T(8,128)(2,1)}, u32[]{:S(2)}) copy-start(bf16[6,2432]{1,0:T(8,128)(2,1)} %param.14) | copy-start | bytes 87556
  7.2 80.3 %all-gather.3.cloned.1.call-start = ((), (), s32[]{:S(2)}) async-start(), calls=%async_computation.4 | async-start | bytes 2359296 | tf_op jit(solution)/shard_map/all_gather | solution.py:141
  9.8 32.3 %copy-start.5 = (bf16[128,2432]{1,0:T(8,128)(2,1)}, bf16[128,2432]{1,0:T(8,128)(2,1)S(1)}, u32[]{:S(2)}) copy-start(bf16[128,2432]{1,0:T(8,128)(2,1)S(1)} %fusion.8.refs_0_) | copy-start | bytes 1867780
  9.9 24.7 %collective-permute-start = (bf16[128,2432]{1,0:T(8,128)(2,1)S(1)}, bf16[128,2432]{1,0:T(8,128)(2,1)S(1)}, u32[]{:S(2)}, u32[]{:S(2)}) collective-permute-start(bf16[128,2432]{1,0:T(8,128)(2,1)S(1)} %fusion.8.refs_0_), channel_id=1, source_target_pairs={{0,2},{2,4},{4,6},{6,8},{8,10},{10,12},{12,14},{14,0},{1,3},{3,5},... | collective-permute-start | bytes 1867784 | tf_op jit(solution)/shard_map/ppermute | solution.py:127
  11.9 28.0 %collective-permute-start.1 = (bf16[128,2432]{1,0:T(8,128)(2,1)S(1)}, bf16[128,2432]{1,0:T(8,128)(2,1)}, u32[]{:S(2)}, u32[]{:S(2)}) collective-permute-start(bf16[128,2432]{1,0:T(8,128)(2,1)S(1)} %fusion.8.refs_0_), channel_id=1, source_target_pairs={{0,14},{2,0},{4,2},{6,4},{8,6},{10,8},{12,10},{14,12},{1,15},{3,1}... | collective-permute-start | bytes 1867784 | tf_op jit(solution)/shard_map/ppermute | solution.py:127
  16.6 28.1 %all-to-all-start.1 = ((bf16[8,6,2432]{2,1,0:T(8,128)(2,1)}), bf16[8,6,2432]{2,1,0:T(8,128)(2,1)S(1)}, u32[]{:S(2)}, u32[]{:S(2)}) async-start(bf16[8,6,2432]{2,1,0:T(8,128)(2,1)} %broadcast_in_dim.12), calls=%async_computation.1 | async-start | bytes 622592 | tf_op jit(solution)/shard_map/all_to_all | solution.py:114
  34.5 53.0 %copy-start.6 = (bf16[128,2432]{1,0:T(8,128)(2,1)}, bf16[128,2432]{1,0:T(8,128)(2,1)S(1)}, u32[]{:S(2)}) copy-start(bf16[128,2432]{1,0:T(8,128)(2,1)S(1)} %collective-permute-done.refs_1_) | copy-start | bytes 1867780
  44.7 41.1 %all-to-all-start = ((bf16[8,128,576]{1,2,0:T(8,128)(2,1)}), bf16[8,128,576]{1,2,0:T(8,128)(2,1)}, u32[]{:S(2)}, u32[]{:S(2)}) async-start(bf16[8,128,576]{1,2,0:T(8,128)(2,1)} %bitcast.3), calls=%async_computation | async-start | bytes 2359296 | tf_op jit(solution)/shard_map/all_to_all | solution.py:143
  51.4 97.3 %all-gather.5.cloned.1.call-start = ((), (), s32[]{:S(2)}) async-start(), calls=%async_computation.5 | async-start | bytes 7938048 | tf_op jit(solution)/shard_map/all_gather | solution.py:151
  51.4 8.5 %collective-permute-start.4 = (bf16[8,6,2432]{2,1,0:T(8,128)(2,1)S(1)}, bf16[8,6,2432]{2,1,0:T(8,128)(2,1)S(1)}, u32[]{:S(2)}, u32[]{:S(2)}) collective-permute-start(bf16[8,6,2432]{2,1,0:T(8,128)(2,1)S(1)} %all-to-all-done.1), channel_id=1, source_target_pairs={{0,1},{1,0},{2,3},{3,2},{4,5},{5,4},{6,7},{7,6},{8,9},{9,8},{10,11... | collective-permute-start | bytes 700424 | tf_op jit(solution)/shard_map/ppermute | solution.py:117
  87.5 14.8 %collective-permute-start.2 = (bf16[128,2432]{1,0:T(8,128)(2,1)S(1)}, bf16[128,2432]{1,0:T(8,128)(2,1)S(1)}, u32[]{:S(2)}, u32[]{:S(2)}) collective-permute-start(bf16[128,2432]{1,0:T(8,128)(2,1)S(1)} %collective-permute-done.refs_1_), channel_id=1, source_target_pairs={{0,2},{2,4},{4,6},{6,8},{8,10},{10,12},{12,14},{14,0},{1,3},{3,5},... | collective-permute-start | bytes 1867784 | tf_op jit(solution)/shard_map/ppermute | solution.py:127
  87.6 14.7 %collective-permute-start.3 = (bf16[128,2432]{1,0:T(8,128)(2,1)}, bf16[128,2432]{1,0:T(8,128)(2,1)S(1)}, u32[]{:S(2)}, u32[]{:S(2)}) collective-permute-start(bf16[128,2432]{1,0:T(8,128)(2,1)} %collective-permute-done.1.refs_2_), channel_id=1, source_target_pairs={{0,14},{2,0},{4,2},{6,4},{8,6},{10,8},{12,10},{14,12},{1,15},{3,1}... | collective-permute-start | bytes 1867784 | tf_op jit(solution)/shard_map/ppermute | solution.py:127
  93.8 8.6 %collective-permute-start.5 = (bf16[2,256,192]{2,1,0:T(8,128)(2,1)S(1)}, bf16[2,256,192]{2,1,0:T(8,128)(2,1)S(1)}, u32[]{:S(2)}, u32[]{:S(2)}) collective-permute-start(bf16[2,256,192]{2,1,0:T(8,128)(2,1)S(1)} %fusion.12), channel_id=1, source_target_pairs={{0,1},{1,0},{2,3},{3,2},{4,5},{5,4},{6,7},{7,6},{8,9},{9,8},{10,11... | collective-permute-start | bytes 589832 | tf_op jit(solution)/shard_map/ppermute | solution.py:158
  102.3 11.0 %copy-start.7 = (bf16[128,2432]{1,0:T(8,128)(2,1)}, bf16[128,2432]{1,0:T(8,128)(2,1)S(1)}, u32[]{:S(2)}) copy-start(bf16[128,2432]{1,0:T(8,128)(2,1)S(1)} %collective-permute-done.2.refs_3_) | copy-start | bytes 1867780
  102.3 11.0 %copy-start.8 = (bf16[128,2432]{1,0:T(8,128)(2,1)}, bf16[128,2432]{1,0:T(8,128)(2,1)S(1)}, u32[]{:S(2)}) copy-start(bf16[128,2432]{1,0:T(8,128)(2,1)S(1)} %collective-permute-done.3.refs_4_) | copy-start | bytes 1867780
  102.3 14.0 %collective-permute-start.6 = (bf16[128,2432]{1,0:T(8,128)(2,1)S(1)}, bf16[128,2432]{1,0:T(8,128)(2,1)}, u32[]{:S(2)}, u32[]{:S(2)}) collective-permute-start(bf16[128,2432]{1,0:T(8,128)(2,1)S(1)} %collective-permute-done.2.refs_3_), channel_id=1, source_target_pairs={{0,2},{2,4},{4,6},{6,8},{8,10},{10,12},{12,14},{14,0},{1,3},{3,5},... | collective-permute-start | bytes 1867784 | tf_op jit(solution)/shard_map/ppermute | solution.py:127
  102.4 13.9 %collective-permute-start.7 = (bf16[128,2432]{1,0:T(8,128)(2,1)S(1)}, bf16[128,2432]{1,0:T(8,128)(2,1)}, u32[]{:S(2)}, u32[]{:S(2)}) collective-permute-start(bf16[128,2432]{1,0:T(8,128)(2,1)S(1)} %collective-permute-done.3.refs_4_), channel_id=1, source_target_pairs={{0,14},{2,0},{4,2},{6,4},{8,6},{10,8},{12,10},{14,12},{1,15},{3,1}... | collective-permute-start | bytes 1867784 | tf_op jit(solution)/shard_map/ppermute | solution.py:127
  113.3 12.4 %copy-start.2 = (bf16[1024,192]{1,0:T(8,128)(2,1)}, bf16[1024,192]{1,0:T(8,128)(2,1)S(1)}, u32[]{:S(2)}) copy-start(bf16[1024,192]{1,0:T(8,128)(2,1)S(1)} %shard_map.103.attn_ref) | copy-start | bytes 1179652
  117.3 22.4 %all-to-all-start.2 = ((bf16[8,128,192]{1,2,0:T(8,128)(2,1)}), bf16[8,128,192]{1,2,0:T(8,128)(2,1)}, u32[]{:S(2)}, u32[]{:S(2)}) async-start(bf16[8,128,192]{1,2,0:T(8,128)(2,1)} %copy.17), calls=%async_computation.2 | async-start | bytes 786432 | tf_op jit(solution)/shard_map/all_to_all | solution.py:171
  122.6 13.5 %collective-permute-start.8 = (bf16[64,2432]{1,0:T(8,128)(2,1)S(1)}, bf16[64,2432]{1,0:T(8,128)(2,1)S(1)}, u32[]{:S(2)}, u32[]{:S(2)}) collective-permute-start(bf16[64,2432]{1,0:T(8,128)(2,1)S(1)} %slice.16), channel_id=1, source_target_pairs={{0,2},{2,4},{4,6},{6,8},{8,10},{10,12},{12,14},{14,0},{1,3},{3,5},... | collective-permute-start | bytes 933896 | tf_op jit(solution)/shard_map/ppermute | solution.py:127
  125.7 10.4 %collective-permute-start.9 = (bf16[64,2432]{1,0:T(8,128)(2,1)S(1)}, bf16[64,2432]{1,0:T(8,128)(2,1)S(1)}, u32[]{:S(2)}, u32[]{:S(2)}) collective-permute-start(bf16[64,2432]{1,0:T(8,128)(2,1)S(1)} %slice.17), channel_id=1, source_target_pairs={{0,14},{2,0},{4,2},{6,4},{8,6},{10,8},{12,10},{14,12},{1,15},{3,1}... | collective-permute-start | bytes 933896 | tf_op jit(solution)/shard_map/ppermute | solution.py:127
  127.0 9.1 %copy-start.3 = (bf16[1024,192]{1,0:T(8,128)(2,1)S(1)}, bf16[1024,192]{1,0:T(8,128)(2,1)}, u32[]{:S(2)}) copy-start(bf16[1024,192]{1,0:T(8,128)(2,1)} %copy-done.2) | copy-start | bytes 1179652
  136.1 1.5 copy-start.1
  139.6 9.0 %copy-start.4 = (bf16[1,128,2432]{2,1,0:T(8,128)(2,1)S(1)}, bf16[1,128,2432]{2,1,0:T(8,128)(2,1)}, u32[]{:S(2)}) copy-start(bf16[1,128,2432]{2,1,0:T(8,128)(2,1)} %param.11) | copy-start | bytes 1867780
  139.6 26.4 %all-to-all-start.3 = ((bf16[32,6,2432]{2,1,0:T(8,128)(2,1)}), bf16[32,6,2432]{2,1,0:T(8,128)(2,1)S(1)}, u32[]{:S(2)}, u32[]{:S(2)}) async-start(bf16[32,6,2432]{2,1,0:T(8,128)(2,1)} %reshape.44), calls=%async_computation.3 | async-start | bytes 2490368 | tf_op jit(solution)/shard_map/all_to_all | solution.py:178
  154.2 3.8 %collective-permute-start.10 = (f32[1,2432]{1,0:T(1,128)S(1)}, f32[1,2432]{1,0:T(1,128)S(1)}, u32[]{:S(2)}, u32[]{:S(2)}) collective-permute-start(f32[1,2432]{1,0:T(1,128)S(1)} %broadcast_in_dim.14), channel_id=1, source_target_pairs={{0,2},{2,0},{4,6},{6,4},{8,10},{10,8},{12,14},{14,12},{1,3},{3,1},... | collective-permute-start | bytes 29192 | tf_op jit(solution)/shard_map/ppermute | solution.py:186
  157.9 4.7 %collective-permute-start.11 = (f32[1,2432]{1,0:T(1,128)S(1)}, f32[1,2432]{1,0:T(1,128)S(1)}, u32[]{:S(2)}, u32[]{:S(2)}) collective-permute-start(f32[1,2432]{1,0:T(1,128)S(1)} %reshape_add_fusion), channel_id=1, source_target_pairs={{0,4},{2,6},{4,0},{6,2},{8,12},{10,14},{12,8},{14,10},{1,5},{3,7},... | collective-permute-start | bytes 29192 | tf_op jit(solution)/shard_map/ppermute | solution.py:186
  166.3 16.2 %collective-permute-start.13 = (bf16[6,2432]{1,0:T(8,128)(2,1)S(1)}, bf16[6,2432]{1,0:T(8,128)(2,1)S(1)}, u32[]{:S(2)}, u32[]{:S(2)}) collective-permute-start(bf16[6,2432]{1,0:T(8,128)(2,1)S(1)} %reduce_sum.22), channel_id=1, source_target_pairs={{0,0},{1,1},{2,32},{3,33},{4,64},{5,65},{6,96},{7,97},{8,128},{9,1... | collective-permute-start | bytes 87560 | tf_op jit(solution)/shard_map/ppermute | solution.py:195
  174.3 7.7 %collective-permute-start.12 = (f32[1,2432]{1,0:T(1,128)S(1)}, f32[1,2432]{1,0:T(1,128)S(1)}, u32[]{:S(2)}, u32[]{:S(2)}) collective-permute-start(f32[1,2432]{1,0:T(1,128)S(1)} %add.14), channel_id=1, source_target_pairs={{0,8},{2,10},{4,12},{6,14},{8,0},{10,2},{12,4},{14,6},{1,9},{3,11}... | collective-permute-start | bytes 29192 | tf_op jit(solution)/shard_map/ppermute | solution.py:186
Sparse Core Ops, SparseCore 0:
  9.8 64.3 all-gather.2
  87.7 49.9 all-gather.4
